TPU v7x, 1024 devices: a whole 4x8x16 slice. The times are simulated.
1024 devices in a mesh: cells: 128 (over y, z_lo, core), inst: 8 (over x, z_hi).
Axes of the slice: x: 4, y: 8, z: 16 (z_hi: 2, z_lo: 8; z = z_hi * 8 + z_lo), core: 2. Of those that a mesh axis runs over, the one named last changes fastest.
Arguments:
- state: float32 [16, 5, 2048, 512], P('inst', None, 'cells'), may hold values from -1 to 6, as said below
- wall_distance: float32 [2048, 512], P('cells'), may hold values from 1 to 8
- blade_counts: int32 [2], replicated, may hold values from 30 to 90
Outputs:
- increment: float32 [16, 5, 2048, 512], P('inst', None, 'cells')
Inputs may be any that keep to these rules, and one draw needn't show every extreme that they name: `state`: each cell holds density, x and y momentum, total energy and density times the turbulence variable of a gas with heat ratio 1.4; density lies in 0.8 to 1.25, pressure in 0.6 to 1.4.
All inputs are finite; a program needn't handle non-finite values.
Results may differ from a plain program's by a relative error of at most 0.0003.
Values sent between devices are 32-bit elements; how exact they have to be, the bound alone decides.
No kernel may reach another device: no remote copies, remote signals or barrier semaphores. Data moves between devices by JAX's collectives and lax.ppermute only.
A program may use at most 32 MiB of HBM per device.

v0:
```python
import math

import jax
import jax.numpy as jnp
from jax import lax
from jax.sharding import PartitionSpec as P

NT = 16


GAMMA_GAS = 1.4
ROTATION = 0.001
DESTRUCTION = 0.4
SEGMENT_WEIGHTS = (0.25, 1.0 / 6.0, 0.375, 0.5, 1.0)


def with_halo(x, sides, width):
    for axis, dim in sides:
        count, length = (lax.axis_size(axis), x.shape[dim])
        up = [(i, (i + 1) % count) for i in range(count)]
        down = [(j, i) for i, j in up]
        last = lax.slice_in_dim(x, length - width, length, axis=dim)
        first = lax.slice_in_dim(x, 0, width, axis=dim)
        before = lax.ppermute(last, axis, up)
        after = lax.ppermute(first, axis, down)
        x = jnp.concatenate([before, x, after], axis=dim)
    return x


def derivative_matrix(count):
    half = count // 2
    angles = 2.0 * math.pi * jnp.arange(count, dtype=jnp.float32) / count
    spread = angles[:, None] - angles[None, :]
    orders = jnp.arange(1, half, dtype=jnp.float32)
    terms = orders[None, None, :] * jnp.sin(orders[None, None, :] * spread[:, :, None])
    return -(2.0 / count) * jnp.sum(terms, axis=2)


def lag_matrix(count, shift):
    half = count // 2
    angles = 2.0 * math.pi * jnp.arange(count, dtype=jnp.float32) / count
    spread = angles[:, None] - angles[None, :] + shift
    orders = jnp.arange(1, half, dtype=jnp.float32)
    terms = jnp.cos(orders[None, None, :] * spread[:, :, None])
    return (1.0 + 2.0 * jnp.sum(terms, axis=2) + jnp.cos(half * spread)) / count


def speeds(field):
    density = field[:, 0]
    velocity_x = field[:, 1] / density
    velocity_y = field[:, 2] / density
    pressure = (GAMMA_GAS - 1.0) * (
        field[:, 3] - 0.5 * (field[:, 1] * velocity_x + field[:, 2] * velocity_y)
    )
    sound = jnp.sqrt(GAMMA_GAS * pressure / density)
    return (jnp.abs(velocity_x) + sound, jnp.abs(velocity_y) + sound)


def fluxes(field):
    density = field[:, 0]
    flow_x = field[:, 1]
    flow_y = field[:, 2]
    energy = field[:, 3]
    turbulent = field[:, 4]
    velocity_x = flow_x / density
    velocity_y = flow_y / density
    pressure = (GAMMA_GAS - 1.0) * (energy - 0.5 * (flow_x * velocity_x + flow_y * velocity_y))
    enthalpy = energy + pressure
    along_x = jnp.stack(
        [
            flow_x,
            flow_x * velocity_x + pressure,
            flow_y * velocity_x,
            enthalpy * velocity_x,
            turbulent * velocity_x,
        ],
        1,
    )
    along_y = jnp.stack(
        [
            flow_y,
            flow_x * velocity_y,
            flow_y * velocity_y + pressure,
            enthalpy * velocity_y,
            turbulent * velocity_y,
        ],
        1,
    )
    return (along_x, along_y)


def residual(padded, wave_max, distance):
    widened = jnp.concatenate([padded[..., :1], padded, padded[..., -1:]], axis=-1)
    along_x, along_y = fluxes(widened)
    inner = widened[:, :, 1:-1]
    flux_x = along_x[:, :, 1:-1]
    face_x = 0.5 * (flux_x[..., :-1] + flux_x[..., 1:]) - 0.5 * wave_max * (
        inner[..., 1:] - inner[..., :-1]
    )
    middle = widened[..., 1:-1]
    flux_y = along_y[..., 1:-1]
    face_y = 0.5 * (flux_y[:, :, :-1] + flux_y[:, :, 1:]) - 0.5 * wave_max * (
        middle[:, :, 1:] - middle[:, :, :-1]
    )
    balance = face_x[..., 1:] - face_x[..., :-1] + (face_y[:, :, 1:] - face_y[:, :, :-1])
    cells_now = padded[:, :, 1:-1]
    decay = (
        DESTRUCTION * cells_now[:, 4] * cells_now[:, 4] / (cells_now[:, 0] * distance * distance)
    )
    return jnp.concatenate([balance[:, :4], balance[:, 4:] + decay[:, None]], 1)


def lag_rows(lower_rim, upper_rim, lag_lower, lag_upper):
    rims = jnp.stack([lower_rim, upper_rim], 2)
    everyone = lax.all_gather(rims, "inst", axis=0, tiled=True)
    below = jnp.einsum("nm,mvi->nvi", lag_lower, everyone[:, :, 0], precision=lax.Precision.HIGHEST)
    above = jnp.einsum("nm,mvi->nvi", lag_upper, everyone[:, :, 1], precision=lax.Precision.HIGHEST)
    return (below, above)


def local(state, wall_distance, blade_counts):
    counts = blade_counts.astype(jnp.float32)
    omega = 2.0 * math.pi * ROTATION * counts[1]
    sigma = 2.0 * math.pi * counts[1] / counts[0]
    own_count = state.shape[0]
    first_row = lax.axis_index("inst") * own_count
    speed_x, speed_y = speeds(state)
    wave_max = lax.pmax(jnp.max(jnp.maximum(speed_x, speed_y)), ("cells", "inst"))
    derivative = derivative_matrix(NT) * omega
    own_derivative = lax.dynamic_slice_in_dim(derivative, first_row, own_count, 0)
    source = jnp.einsum(
        "nm,mvji->nvji",
        own_derivative,
        lax.all_gather(state, "inst", axis=0, tiled=True),
        precision=lax.Precision.HIGHEST,
    )
    place = lax.axis_index("cells")
    is_first = place == 0
    is_last = place == lax.axis_size("cells") - 1
    lag_lower = lax.dynamic_slice_in_dim(lag_matrix(NT, sigma), first_row, own_count, 0)
    lag_upper = lax.dynamic_slice_in_dim(lag_matrix(NT, -sigma), first_row, own_count, 0)
    pseudo_step = 1.0 / (speed_x + speed_y + omega * (NT // 2))
    current = state
    below = state[:, :, 0]
    above = state[:, :, 0]
    for segment_index, weight in enumerate(SEGMENT_WEIGHTS):
        padded = with_halo(current, (("cells", 2),), 1)
        if segment_index == 0:
            below, above = lag_rows(padded[:, :, 0], padded[:, :, -1], lag_lower, lag_upper)
        lower_row = jnp.where(is_first, below, padded[:, :, 0])
        upper_row = jnp.where(is_last, above, padded[:, :, -1])
        padded = jnp.concatenate(
            [lower_row[:, :, None], padded[:, :, 1:-1], upper_row[:, :, None]], 2
        )
        current = state - weight * pseudo_step[:, None] * (
            residual(padded, wave_max, wall_distance) + source
        )
    return current - state


def solution(mesh):
    placed = (P("inst", None, "cells", None), P("cells", None), P())
    return jax.shard_map(
        local, mesh=mesh, in_specs=placed, out_specs=P("inst", None, "cells", None), check_vma=False
    )
```

profile of v0, /device:TPU:32, one launch (start us, length us, event | category | flops | bytes accessed | tf_op | source)
XLA Modules:
  0.0 357.1 jit_solution(7178235208846112363)
XLA Ops:
  6.5 0.7 all-gather.2.cloned.1.call-update
  7.3 1.0 fusion.124
  8.3 15.7 %collective-permute-start.1 = (f32[2,5,1,512]{3,0,1,2:T(2,128)S(1)}, f32[2,5,1,512]{3,0,1,2:T(2,128)S(1)}, u32[]{:S(2)}, u32[]{:S(2)}) collective-permute-start(f32[2,5,1,512]{3,0,1,2:T(2,128)S(1)} %copy.1291), channel_id=1, source_target_pairs={{8,0},{16,8},{24,16},{32,24},{40,32},{48,40},{56,48},{64,56},{72,6... | collective-permute-start | bytes 61448 | tf_op jit(solution)/shard_map/ppermute | solution.py:25
  24.0 1.9 collective-permute-start
  25.9 1.6 maximum_reduce_fusion
  27.6 0.7 convert_element_type.3
  28.2 0.6 fusion.125
  30.3 0.7 multiply_reduce_fusion
  31.0 172.2 %pmax.7 = f32[]{:T(128)} all-reduce(f32[]{:T(128)} %maximum_reduce_fusion), channel_id=1, replica_groups=mesh['cells'=128,'inst'=8] {'cells','inst'}, use_global_device_ids=true, to_apply=%region_3.0 | all-reduce | flops 1 | bytes 8 | tf_op jit(solution)/shard_map/pmax | solution.py:128
  205.2 66.4 %all_gather.6 = f32[16,5,2,512]{3,2,1,0:T(2,128)S(1)} all-gather(f32[2,5,2,512]{3,2,1,0:T(2,128)S(1)} %copy.1249), channel_id=1, replica_groups=mesh['cells'=128,'inst'=8] {'inst'}, dimensions={0}, use_global_device_ids=true | all-gather | bytes 368640 | tf_op jit(solution)/shard_map/all_gather | solution.py:115
  272.6 0.4 pad_maximum_fusion
  273.3 0.4 fusion.35
  274.3 4.4 %fusion = f32[2,5,16,512]{3,0,2,1:T(2,128)S(1)} fusion(f32[16,5,16,512]{3,2,1,0:T(8,128)} %all-gather.2.cloned.1.call-done, f32[16,16]{1,0:T(8,128)S(1)} %get-tuple-element.5, s32[]{:T(128)S(6)} %select_n.52, f32[]{:T(128)} %bitcast.24), kind=kOutput, calls=%fused_computation | convolution fusion | flops 15728672 | bytes 2950152 | tf_op jit(solution)/shard_map/nm,mvji->nvji/dot_general | solution.py:131
  278.9 1.9 collective-permute-start.2
  280.9 12.4 %collective-permute-start.3 = (f32[2,5,1,512]{3,2,1,0:T(1,128)S(1)}, f32[2,5,1,512]{3,2,1,0:T(1,128)S(1)}, u32[]{:S(2)}, u32[]{:S(2)}) collective-permute-start(f32[2,5,1,512]{3,2,1,0:T(1,128)S(1)} %get-tuple-element.77), channel_id=1, source_target_pairs={{8,0},{16,8},{24,16},{32,24},{40,32},{48,40},{56,48},{64,56},{72,6... | collective-permute-start | bytes 61448 | tf_op jit(solution)/shard_map/ppermute | solution.py:25
  293.3 1.4 collective-permute-done.3
  294.9 0.4 pad_maximum_fusion.1
  295.5 0.4 fusion.31
  296.6 1.9 collective-permute-start.4
  298.5 12.4 %collective-permute-start.5 = (f32[2,5,1,512]{3,2,1,0:T(1,128)S(1)}, f32[2,5,1,512]{3,2,1,0:T(1,128)S(1)}, u32[]{:S(2)}, u32[]{:S(2)}) collective-permute-start(f32[2,5,1,512]{3,2,1,0:T(1,128)S(1)} %get-tuple-element.75), channel_id=1, source_target_pairs={{8,0},{16,8},{24,16},{32,24},{40,32},{48,40},{56,48},{64,56},{72,6... | collective-permute-start | bytes 61448 | tf_op jit(solution)/shard_map/ppermute | solution.py:25
  311.0 1.4 collective-permute-done.5
  312.5 0.4 pad_maximum_fusion.2
  313.2 0.4 fusion.27
  314.3 1.9 collective-permute-start.6
  316.2 12.5 %collective-permute-start.7 = (f32[2,5,1,512]{3,2,1,0:T(1,128)S(1)}, f32[2,5,1,512]{3,2,1,0:T(1,128)S(1)}, u32[]{:S(2)}, u32[]{:S(2)}) collective-permute-start(f32[2,5,1,512]{3,2,1,0:T(1,128)S(1)} %get-tuple-element.73), channel_id=1, source_target_pairs={{8,0},{16,8},{24,16},{32,24},{40,32},{48,40},{56,48},{64,56},{72,6... | collective-permute-start | bytes 61448 | tf_op jit(solution)/shard_map/ppermute | solution.py:25
  328.8 1.2 collective-permute-done.7
  330.2 0.4 pad_maximum_fusion.3
  331.9 1.9 collective-permute-start.8
  333.9 12.4 %collective-permute-start.9 = (f32[2,5,1,512]{3,2,1,0:T(1,128)S(1)}, f32[2,5,1,512]{3,2,1,0:T(1,128)S(1)}, u32[]{:S(2)}, u32[]{:S(2)}) collective-permute-start(f32[2,5,1,512]{3,2,1,0:T(1,128)S(1)} %get-tuple-element.71), channel_id=1, source_target_pairs={{8,0},{16,8},{24,16},{32,24},{40,32},{48,40},{56,48},{64,56},{72,6... | collective-permute-start | bytes 61448 | tf_op jit(solution)/shard_map/ppermute | solution.py:25
  346.3 1.4 collective-permute-done.9
  347.9 0.4 pad_maximum_fusion.4
  349.4 0.8 subtract_subtract_fusion
  (113 shorter events, 7.2 us)
Async XLA Ops:
  6.5 266.0 %copy-start = (f32[2,5,16,512]{3,2,1,0:T(8,128)S(1)}, f32[2,5,16,512]{3,2,1,0:T(8,128)}, u32[]{:S(2)}) copy-start(f32[2,5,16,512]{3,2,1,0:T(8,128)} %param.3) | copy-start | bytes 983044
  6.5 267.8 %all-gather.2.cloned.1.call-start = ((), (), s32[]{:S(2)}) async-start(), calls=%async_computation | async-start | bytes 2949120 | tf_op jit(solution)/shard_map/all_gather | solution.py:134
  8.3 196.8 %collective-permute-start.1 = (f32[2,5,1,512]{3,0,1,2:T(2,128)S(1)}, f32[2,5,1,512]{3,0,1,2:T(2,128)S(1)}, u32[]{:S(2)}, u32[]{:S(2)}) collective-permute-start(f32[2,5,1,512]{3,0,1,2:T(2,128)S(1)} %copy.1291), channel_id=1, source_target_pairs={{8,0},{16,8},{24,16},{32,24},{40,32},{48,40},{56,48},{64,56},{72,6... | collective-permute-start | bytes 61448 | tf_op jit(solution)/shard_map/ppermute | solution.py:25
  24.0 181.1 %collective-permute-start = (f32[2,5,1,512]{3,0,1,2:T(2,128)S(1)}, f32[2,5,1,512]{3,0,1,2:T(2,128)S(1)}, u32[]{:S(2)}, u32[]{:S(2)}) collective-permute-start(f32[2,5,1,512]{3,0,1,2:T(2,128)S(1)} %copy.1290), channel_id=1, source_target_pairs={{0,8},{8,16},{16,24},{24,32},{32,40},{40,48},{48,56},{56,64},{64,7... | collective-permute-start | bytes 61448 | tf_op jit(solution)/shard_map/ppermute | solution.py:24
  273.2 0.9 copy-start.1
  278.9 14.3 %collective-permute-start.2 = (f32[2,5,1,512]{3,2,1,0:T(1,128)S(1)}, f32[2,5,1,512]{3,2,1,0:T(1,128)S(1)}, u32[]{:S(2)}, u32[]{:S(2)}) collective-permute-start(f32[2,5,1,512]{3,2,1,0:T(1,128)S(1)} %get-tuple-element.76), channel_id=1, source_target_pairs={{0,8},{8,16},{16,24},{24,32},{32,40},{40,48},{48,56},{56,64},{64,7... | collective-permute-start | bytes 61448 | tf_op jit(solution)/shard_map/ppermute | solution.py:24
  280.9 13.8 %collective-permute-start.3 = (f32[2,5,1,512]{3,2,1,0:T(1,128)S(1)}, f32[2,5,1,512]{3,2,1,0:T(1,128)S(1)}, u32[]{:S(2)}, u32[]{:S(2)}) collective-permute-start(f32[2,5,1,512]{3,2,1,0:T(1,128)S(1)} %get-tuple-element.77), channel_id=1, source_target_pairs={{8,0},{16,8},{24,16},{32,24},{40,32},{48,40},{56,48},{64,56},{72,6... | collective-permute-start | bytes 61448 | tf_op jit(solution)/shard_map/ppermute | solution.py:25
  296.6 14.3 %collective-permute-start.4 = (f32[2,5,1,512]{3,2,1,0:T(1,128)S(1)}, f32[2,5,1,512]{3,2,1,0:T(1,128)S(1)}, u32[]{:S(2)}, u32[]{:S(2)}) collective-permute-start(f32[2,5,1,512]{3,2,1,0:T(1,128)S(1)} %get-tuple-element.74), channel_id=1, source_target_pairs={{0,8},{8,16},{16,24},{24,32},{32,40},{40,48},{48,56},{56,64},{64,7... | collective-permute-start | bytes 61448 | tf_op jit(solution)/shard_map/ppermute | solution.py:24
  298.5 13.8 %collective-permute-start.5 = (f32[2,5,1,512]{3,2,1,0:T(1,128)S(1)}, f32[2,5,1,512]{3,2,1,0:T(1,128)S(1)}, u32[]{:S(2)}, u32[]{:S(2)}) collective-permute-start(f32[2,5,1,512]{3,2,1,0:T(1,128)S(1)} %get-tuple-element.75), channel_id=1, source_target_pairs={{8,0},{16,8},{24,16},{32,24},{40,32},{48,40},{56,48},{64,56},{72,6... | collective-permute-start | bytes 61448 | tf_op jit(solution)/shard_map/ppermute | solution.py:25
  314.3 14.5 %collective-permute-start.6 = (f32[2,5,1,512]{3,2,1,0:T(1,128)S(1)}, f32[2,5,1,512]{3,2,1,0:T(1,128)S(1)}, u32[]{:S(2)}, u32[]{:S(2)}) collective-permute-start(f32[2,5,1,512]{3,2,1,0:T(1,128)S(1)} %get-tuple-element.72), channel_id=1, source_target_pairs={{0,8},{8,16},{16,24},{24,32},{32,40},{40,48},{48,56},{56,64},{64,7... | collective-permute-start | bytes 61448 | tf_op jit(solution)/shard_map/ppermute | solution.py:24
  316.2 13.8 %collective-permute-start.7 = (f32[2,5,1,512]{3,2,1,0:T(1,128)S(1)}, f32[2,5,1,512]{3,2,1,0:T(1,128)S(1)}, u32[]{:S(2)}, u32[]{:S(2)}) collective-permute-start(f32[2,5,1,512]{3,2,1,0:T(1,128)S(1)} %get-tuple-element.73), channel_id=1, source_target_pairs={{8,0},{16,8},{24,16},{32,24},{40,32},{48,40},{56,48},{64,56},{72,6... | collective-permute-start | bytes 61448 | tf_op jit(solution)/shard_map/ppermute | solution.py:25
  331.9 14.3 %collective-permute-start.8 = (f32[2,5,1,512]{3,2,1,0:T(1,128)S(1)}, f32[2,5,1,512]{3,2,1,0:T(1,128)S(1)}, u32[]{:S(2)}, u32[]{:S(2)}) collective-permute-start(f32[2,5,1,512]{3,2,1,0:T(1,128)S(1)} %get-tuple-element.70), channel_id=1, source_target_pairs={{0,8},{8,16},{16,24},{24,32},{32,40},{40,48},{48,56},{56,64},{64,7... | collective-permute-start | bytes 61448 | tf_op jit(solution)/shard_map/ppermute | solution.py:24
  333.9 13.8 %collective-permute-start.9 = (f32[2,5,1,512]{3,2,1,0:T(1,128)S(1)}, f32[2,5,1,512]{3,2,1,0:T(1,128)S(1)}, u32[]{:S(2)}, u32[]{:S(2)}) collective-permute-start(f32[2,5,1,512]{3,2,1,0:T(1,128)S(1)} %get-tuple-element.71), channel_id=1, source_target_pairs={{8,0},{16,8},{24,16},{32,24},{40,32},{48,40},{56,48},{64,56},{72,6... | collective-permute-start | bytes 61448 | tf_op jit(solution)/shard_map/ppermute | solution.py:25
Sparse Core Ops, SparseCore 0:
  11.7 148.7 all-gather.1
where the time goes:
time: 358 us; the launch traced here: 357 us
  blocking collectives  239 us (67%)
  starting transfers between devices  74.9 us (21%)
  between operations  17.5 us (5%)
  other arithmetic  12.6 us (4%)
  waiting for transfers between devices  6.15 us (2%)
  matrix products  4.96 us (1%)
    pmax x1, blocking collectives, local(): lax.pmax(jnp.max(jnp.maximum(speed_x, speed_y)), ('cells', 'inst'))  172 us
    all_gather x1, blocking collectives, lag_rows(): everyone = lax.all_gather(rims, 'inst', axis=0, tiled=True)  66.4 us
    ppermute x5, starting transfers between devices, with_halo(): after = lax.ppermute(first, axis, down)  65.3 us
    ppermute x5, starting transfers between devices, with_halo(): before = lax.ppermute(last, axis, up)  9.6 us
  transfers between devices with their start and end apart: 11, of which 4 were waited for; matrix products, arithmetic and copies ran while one was open for 2% of the time, Pallas kernels for 0%

commit v1 on v0

v1 whole, which is shorter than its diff:
```python
import functools
import math

import jax
import jax.numpy as jnp
from jax import lax
from jax.experimental import pallas as pl
from jax.experimental.pallas import tpu as pltpu
from jax.sharding import Mesh
from jax.sharding import PartitionSpec as P

NT = 16
HALF = NT // 2
ROTATION = 0.001
SEGMENT_WEIGHTS = (0.25, 1.0 / 6.0, 0.375, 0.5, 1.0)
CELLS = ("y", "zl", "core")
VMEM = pl.BlockSpec(memory_space=pltpu.VMEM)
SMEM = pl.BlockSpec(memory_space=pltpu.SMEM)
PARAMS = pltpu.CompilerParams(vmem_limit_bytes=48 * 1024 * 1024)

SLOPE = [
    -(2.0 / NT) * sum(k * math.sin(2.0 * math.pi * k * j / NT) for k in range(1, HALF))
    for j in range(NT)
]


def omega_of(counts_ref):
    return (2.0 * math.pi * ROTATION) * counts_ref[1].astype(jnp.float32)


def speed_sum_and_max(r, mx, my, e):
    inv = 1.0 / r
    vx = mx * inv
    vy = my * inv
    p = 0.4 * (e - 0.5 * (mx * vx + my * vy))
    c = jnp.sqrt(1.4 * p * inv)
    ax = jnp.abs(vx)
    ay = jnp.abs(vy)
    return ax + ay + 2.0 * c, jnp.maximum(ax, ay) + c


def peak_kernel(state_ref, out_ref):
    best = None
    for n in range(2):
        for t in range(2):
            rows = pl.ds(8 * t, 8)
            _, top = speed_sum_and_max(*(state_ref[n, v, rows, :] for v in range(4)))
            best = top if best is None else jnp.maximum(best, top)
    peak = jnp.max(best, axis=(0, 1), keepdims=True)
    out_ref[...] = jnp.broadcast_to(peak[None], out_ref.shape)


def partial_kernel(counts_ref, state_ref, other_ref, peaks_ref, out_ref, lag_ref):
    me_x = lax.axis_index("x")
    upper_half = lax.axis_index("zh")
    place = lax.axis_index(CELLS)
    is_last = place == lax.axis_size(CELLS) - 1
    omega = omega_of(counts_ref)
    ratio = jnp.full((NT, 128), counts_ref[1].astype(jnp.float32)) / jnp.full(
        (NT, 128), counts_ref[0].astype(jnp.float32)
    )
    sigma = 2.0 * math.pi * ratio
    shift = jnp.where(is_last, sigma, -sigma)
    offset = lax.broadcasted_iota(jnp.int32, (NT, 128), 0).astype(jnp.float32)
    order = lax.broadcasted_iota(jnp.int32, (NT, 128), 1)
    angle = (2.0 * math.pi / NT) * offset + shift
    share = jnp.where(order > HALF, 0.0, jnp.where((order == 0) | (order == HALF), 1.0, 2.0))
    terms = share * jnp.cos(order.astype(jnp.float32) * angle)
    lag_ref[...] = jnp.broadcast_to(
        jnp.sum(terms, axis=1, keepdims=True) * (1.0 / NT), lag_ref.shape
    )
    peak = jnp.max(peaks_ref[...], axis=0)
    for step in range(4):
        target = lax.rem(me_x + step, 4)
        own = [[(4 * step + n - m) % NT for m in range(2)] for n in range(2)]
        high = [[(4 * step + 2 + n - m) % NT for m in range(2)] for n in range(2)]
        low = [[(4 * step - 2 + n - m) % NT for m in range(2)] for n in range(2)]
        scale = [
            [omega * SLOPE[own[n][m]] for m in range(2)]
            + [
                omega * jnp.where(upper_half == 1, SLOPE[high[n][m]], SLOPE[low[n][m]])
                for m in range(2)
            ]
            for n in range(2)
        ]
        for v in range(5):
            for t in range(2):
                rows = pl.ds(8 * t, 8)
                fields = [state_ref[m, v, rows, :] for m in range(2)] + [
                    other_ref[m, v, rows, :] for m in range(2)
                ]
                for n in range(2):
                    total = scale[n][0] * fields[0]
                    for m in range(1, 4):
                        total = total + scale[n][m] * fields[m]
                    out_ref[target, pl.ds((n * 5 + v) * 16 + 8 * t, 8), :] = total

        def lag(j):
            return jnp.concatenate([lag_ref[j : j + 1, :]] * 4, axis=1)

        factor = [
            [lag(own[n][m]) for m in range(2)]
            + [jnp.where(upper_half == 1, lag(high[n][m]), lag(low[n][m])) for m in range(2)]
            for n in range(2)
        ]
        for v in range(5):
            edges = [
                jnp.where(is_last, ref[m, v, 15:16, :], ref[m, v, 0:1, :])
                for ref in (state_ref, other_ref)
                for m in range(2)
            ]
            for n in range(2):
                total = factor[n][0] * edges[0]
                for m in range(1, 4):
                    total = total + factor[n][m] * edges[m]
                out_ref[target, pl.ds(160 + n * 5 + v, 1), :] = total
        out_ref[target, pl.ds(170, 6), :] = jnp.broadcast_to(
            jnp.concatenate([peak] * 4, axis=1), (6, 512)
        )


def edge_kernel(state_ref, wall_ref, parts_ref, up_ref, down_ref):
    place = lax.axis_index(CELLS)
    is_first = place == 0
    is_last = place == lax.axis_size(CELLS) - 1
    row = lax.broadcasted_iota(jnp.int32, (8, 512), 0)

    def added(start, count):
        total = parts_ref[0, pl.ds(start, count), :]
        for k in range(1, 4):
            total = total + parts_ref[k, pl.ds(start, count), :]
        return total

    for n in range(2):
        for v in range(5):
            at = n * 5 + v
            lagged = jnp.broadcast_to(added(160 + at, 1), (8, 512))
            source = pltpu.roll(added(at * 16 + 8, 8), 4, axis=0)
            packed = jnp.where(row >= 4, state_ref[n, v, 8:16, :], source)
            packed = jnp.where(is_last & (row == 7), lagged, packed)
            up_ref[pl.ds(at * 8, 8), :] = packed
            source = pltpu.roll(added(at * 16, 8), 4, axis=0)
            packed = jnp.where(row < 4, state_ref[n, v, 0:8, :], source)
            packed = jnp.where(is_first & (row == 0), lagged, packed)
            down_ref[pl.ds(at * 8, 8), :] = packed
            up_ref[pl.ds(80 + at, 1), :] = state_ref[n, v, 11:12, :]
            down_ref[pl.ds(80 + at, 1), :] = state_ref[n, v, 4:5, :]
    up_ref[pl.ds(90, 4), :] = wall_ref[12:16, :]
    down_ref[pl.ds(90, 4), :] = wall_ref[0:4, :]
    peak = parts_ref[0, 170:172, :]
    for k in range(1, 4):
        peak = jnp.maximum(peak, parts_ref[k, 170:172, :])
    up_ref[pl.ds(94, 2), :] = peak
    down_ref[pl.ds(94, 2), :] = peak


def march_kernel(
    counts_ref,
    state_ref,
    wall_ref,
    parts_ref,
    lower_ref,
    upper_ref,
    out_ref,
    start_ref,
    now_ref,
    source_ref,
    step_ref,
    decay_ref,
    across_ref,
    ahead_ref,
    behind_ref,
):
    place = lax.axis_index(CELLS)
    is_first = place == 0
    is_last = place == lax.axis_size(CELLS) - 1
    omega = omega_of(counts_ref)
    row = lax.broadcasted_iota(jnp.int32, (8, 512), 0)
    column = lax.broadcasted_iota(jnp.int32, (8, 512), 1)
    at_left = column == 0
    at_right = column == 511
    peak = jnp.maximum(lower_ref[94:95, :], upper_ref[94:95, :])
    for k in range(4):
        peak = jnp.maximum(peak, parts_ref[k, 170:171, :])
    wave = jnp.broadcast_to(peak, (8, 512))

    walls = [
        jnp.concatenate([lower_ref[90:94, :]] * 2, axis=0),
        wall_ref[0:8, :],
        wall_ref[8:16, :],
        jnp.concatenate([upper_ref[90:94, :]] * 2, axis=0),
    ]
    for t in range(4):
        decay_ref[pl.ds(8 * t, 8), :] = 0.8 / (walls[t] * walls[t])
    for n in range(2):
        for v in range(5):
            at = n * 5 + v
            packed = lower_ref[pl.ds(at * 8, 8), :]
            fifth = jnp.broadcast_to(lower_ref[pl.ds(80 + at, 1), :], (8, 512))
            start_ref[n, v, 0:8, :] = jnp.where(row >= 4, packed, fifth)
            source_ref[n, v, 0:8, :] = 2.0 * pltpu.roll(packed, 4, axis=0)
            packed = upper_ref[pl.ds(at * 8, 8), :]
            fifth = jnp.broadcast_to(upper_ref[pl.ds(80 + at, 1), :], (8, 512))
            start_ref[n, v, 24:32, :] = jnp.where(row < 4, packed, fifth)
            source_ref[n, v, 24:32, :] = 2.0 * pltpu.roll(packed, 4, axis=0)
            start_ref[n, v, 8:24, :] = state_ref[n, v, :, :]
            total = parts_ref[0, pl.ds(at * 16, 16), :]
            for k in range(1, 4):
                total = total + parts_ref[k, pl.ds(at * 16, 16), :]
            source_ref[n, v, 8:24, :] = 2.0 * total
        for t in range(4):
            rows = pl.ds(8 * t, 8)
            both, _ = speed_sum_and_max(*(start_ref[n, v, rows, :] for v in range(4)))
            step_ref[n, rows, :] = 0.5 / (both + omega * HALF)

    for segment, weight in enumerate(SEGMENT_WEIGHTS):
        from_ref = start_ref if segment == 0 else now_ref
        for n in range(2):
            for t in range(4):
                rows = pl.ds(8 * t, 8)
                r, mx, my, e, q = (from_ref[n, v, rows, :] for v in range(5))
                inv = 1.0 / r
                vx = mx * inv
                vy = my * inv
                p = 0.4 * (e - 0.5 * (mx * vx + my * vy))
                h = e + p
                fx = (mx, mx * vx + p, my * vx, h * vx, q * vx)
                fy = (my, mx * vy, my * vy + p, h * vy, q * vy)
                for v, u in enumerate((r, mx, my, e, q)):
                    wu = wave * u
                    after = fx[v] - wu
                    before = fx[v] + wu
                    after = jnp.where(at_right, after, pltpu.roll(after, 511, axis=1))
                    before = jnp.where(at_left, before, pltpu.roll(before, 1, axis=1))
                    balance = after - before + 4.0 * wu
                    if v == 4:
                        balance = balance + decay_ref[rows, :] * (q * q * inv)
                    across_ref[v, rows, :] = balance
                    ahead_ref[v, pl.ds(8 * t + 8, 8), :] = fy[v] - wu
                    behind_ref[v, pl.ds(8 * t + 8, 8), :] = fy[v] + wu
            last = segment == len(SEGMENT_WEIGHTS) - 1
            for t in (1, 2) if last else range(4):
                rows = pl.ds(8 * t, 8)
                step = weight * step_ref[n, rows, :]
                for v in range(5):
                    total = (
                        across_ref[v, rows, :]
                        + ahead_ref[v, pl.ds(8 * t + 9, 8), :]
                        - behind_ref[v, pl.ds(8 * t + 7, 8), :]
                        + source_ref[n, v, rows, :]
                    )
                    change = step * total
                    begin = start_ref[n, v, rows, :]
                    if last:
                        out_ref[n, v, pl.ds(8 * t - 8, 8), :] = -change
                        continue
                    after = begin - change
                    if t == 0:
                        after = jnp.where(is_first, begin, after)
                    if t == 3:
                        after = jnp.where(is_last, begin, after)
                    now_ref[n, v, rows, :] = after


def local(state, wall_distance, blade_counts):
    f32 = jnp.float32
    field = functools.partial(jax.ShapeDtypeStruct, dtype=f32)
    other = lax.ppermute(state, "zh", [(0, 1), (1, 0)])
    peak = pl.pallas_call(
        peak_kernel, out_shape=field((128, 1, 128)), in_specs=[VMEM], out_specs=VMEM,
        compiler_params=PARAMS, name="peak",
    )(state)
    peaks = lax.all_to_all(peak, ("y", "zl", "zh"), 0, 0)
    parts = pl.pallas_call(
        partial_kernel, out_shape=field((4, 176, 512)),
        in_specs=[SMEM, VMEM, VMEM, VMEM], out_specs=VMEM,
        scratch_shapes=[pltpu.VMEM((NT, 128), f32)],
        compiler_params=PARAMS, name="partial_sources",
    )(blade_counts, state, other, peaks)
    parts = lax.all_to_all(parts, "x", 0, 0)
    up, down = pl.pallas_call(
        edge_kernel, out_shape=(field((96, 512)), field((96, 512))),
        in_specs=[VMEM] * 3, out_specs=(VMEM, VMEM),
        compiler_params=PARAMS, name="edges",
    )(state, wall_distance, parts)
    count = lax.axis_size(CELLS)
    ring = [(i, (i + 1) % count) for i in range(count)]
    lower = lax.ppermute(up, CELLS, ring)
    upper = lax.ppermute(down, CELLS, [(j, i) for i, j in ring])
    return pl.pallas_call(
        march_kernel, out_shape=field(state.shape),
        in_specs=[SMEM] + [VMEM] * 5, out_specs=VMEM,
        scratch_shapes=[
            pltpu.VMEM((2, 5, 32, 512), f32),
            pltpu.VMEM((2, 5, 32, 512), f32),
            pltpu.VMEM((2, 5, 32, 512), f32),
            pltpu.VMEM((2, 32, 512), f32),
            pltpu.VMEM((32, 512), f32),
            pltpu.VMEM((5, 32, 512), f32),
            pltpu.VMEM((5, 48, 512), f32),
            pltpu.VMEM((5, 48, 512), f32),
        ],
        compiler_params=PARAMS, name="march",
    )(blade_counts, state, wall_distance, parts, lower, upper)


def solution(mesh):
    fine = Mesh(mesh.devices.reshape(8, 8, 2, 4, 2), ("y", "zl", "core", "x", "zh"))
    inst = ("x", "zh")
    placed = (P(inst, None, CELLS, None), P(CELLS, None), P())
    return jax.shard_map(
        local, mesh=fine, in_specs=placed, out_specs=P(inst, None, CELLS, None), check_vma=False
    )
```

time: 358 us -> 110 us (0.31)
  the two profiles are of different devices: /device:TPU:32 before, /device:TPU:8 now
where the time goes in v1:
time: 110 us; the launch traced here: 109 us
  blocking collectives  66.3 us (60%)
  starting transfers between devices  32.4 us (29%)
  Pallas kernels  5.87 us (5%)
  waiting for transfers between devices  3.17 us (3%)
  local copies, waits for them, and re-layouts  1.64 us (1%)
    all_to_all x1, blocking collectives, local(): peaks = lax.all_to_all(peak, ('y', 'zl', 'zh'), 0, 0)  43.4 us
    all_to_all x1, blocking collectives, local(): parts = lax.all_to_all(parts, 'x', 0, 0)  22.9 us
    ppermute x1, starting transfers between devices, local(): other = lax.ppermute(state, 'zh', [(0, 1), (1, 0)])  19.3 us
    ppermute x1, starting transfers between devices, local(): upper = lax.ppermute(down, CELLS, [(j, i) for i, j in ring])  11.1 us
    pallas_call x1, Pallas kernels, local(): pl.pallas_call(march_kernel, out_shape=field(state.shape), in_specs=[SMEM...  4.33 us
  transfers between devices with their start and end apart: 3, of which 2 were waited for; matrix products, arithmetic and copies ran while one was open for 0% of the time, Pallas kernels for 0%

profile of v1, /device:TPU:8, one launch (start us, length us, event | category | flops | bytes accessed | tf_op | source)
XLA Modules:
  0.0 109.5 jit_solution(6190001461318636736)
XLA Ops:
  0.0 19.3 %collective-permute-start = (f32[2,5,16,512]{3,2,1,0:T(8,128)}, f32[2,5,16,512]{3,2,1,0:T(8,128)S(1)}, u32[]{:S(2)}, u32[]{:S(2)}) collective-permute-start(f32[2,5,16,512]{3,2,1,0:T(8,128)} %state_ref.7), channel_id=1, source_target_pairs={{0,1},{1,0},{2,3},{3,2},{4,5},{5,4},{6,7},{7,6},{8,9},{9,8},{10,11... | collective-permute-start | bytes 983048 | tf_op jit(solution)/shard_map/ppermute | solution.py:268
  19.4 0.0 copy-start
  19.4 1.0 copy-done
  20.3 0.2 peak.1
  20.6 43.4 %all_to_all.10.peaks_ref = f32[128,1,128]{2,1,0:T(1,128)S(1)} all-to-all(f32[128,1,128]{2,1,0:T(1,128)S(1)} %peak.1), channel_id=1, replica_groups=mesh['y'=8,'zl'=8,'core'=2,'x'=4,'zh'=2] {'y','zl','zh'}, dimensions={0} | all-to-all | bytes 131072 | tf_op jit(solution)/shard_map/all_to_all | solution.py:273
  64.0 0.0 collective-permute-done.other_ref
  64.0 0.0 copy-start.2
  64.0 0.7 copy-done.2
  64.7 1.2 %partial_sources.1 = f32[4,176,512]{2,1,0:T(8,128)S(1)} custom-call(s32[2]{0:T(128)S(1)} %copy-done.2, f32[2,5,16,512]{3,2,1,0:T(8,128)S(1)} %copy-done, f32[2,5,16,512]{3,2,1,0:T(8,128)S(1)} %collective-permute-done.other_ref, f32[128,1,128]{2,1,0:T(1,128)S(1)} %all_to_all.10.peaks_ref), custom_call_target="tpu_custom_call" | custom-call | tf_op jit(solution)/shard_map/partial_sources/pallas_call | solution.py:274
  65.9 0.0 copy-start.1
  65.9 22.9 %all_to_all.11.parts_ref = f32[4,176,512]{2,1,0:T(8,128)S(1)} all-to-all(f32[4,176,512]{2,1,0:T(8,128)S(1)} %partial_sources.1), channel_id=1, replica_groups=mesh['y'=8,'zl'=8,'core'=2,'x'=4,'zh'=2] {'x'}, dimensions={0} | all-to-all | bytes 2883584 | tf_op jit(solution)/shard_map/all_to_all | solution.py:280
  88.8 0.0 copy-done.1
  88.8 0.1 edges.1
  88.9 1.9 %collective-permute-start.1 = (f32[96,512]{1,0:T(8,128)S(1)}, f32[96,512]{1,0:T(8,128)S(1)}, u32[]{:S(2)}, u32[]{:S(2)}) collective-permute-start(f32[96,512]{1,0:T(8,128)S(1)} %get-tuple-element.7), channel_id=1, source_target_pairs={{0,8},{8,16},{16,24},{24,32},{32,40},{40,48},{48,56},{56,64},{64,7... | collective-permute-start | bytes 589832 | tf_op jit(solution)/shard_map/ppermute | solution.py:288
  90.8 11.1 %collective-permute-start.2 = (f32[96,512]{1,0:T(8,128)S(1)}, f32[96,512]{1,0:T(8,128)S(1)}, u32[]{:S(2)}, u32[]{:S(2)}) collective-permute-start(f32[96,512]{1,0:T(8,128)S(1)} %get-tuple-element.8), channel_id=1, source_target_pairs={{8,0},{16,8},{24,16},{32,24},{40,32},{48,40},{56,48},{64,56},{72,6... | collective-permute-start | bytes 589832 | tf_op jit(solution)/shard_map/ppermute | solution.py:289
  102.0 1.4 %collective-permute-done.1.lower_ref = f32[96,512]{1,0:T(8,128)S(1)} collective-permute-done((f32[96,512]{1,0:T(8,128)S(1)}, f32[96,512]{1,0:T(8,128)S(1)}, u32[]{:S(2)}, u32[]{:S(2)}) %collective-permute-start.1) | collective-permute-done | bytes 196640 | tf_op jit(solution)/shard_map/ppermute | solution.py:288
  103.4 1.8 %collective-permute-done.2.upper_ref = f32[96,512]{1,0:T(8,128)S(1)} collective-permute-done((f32[96,512]{1,0:T(8,128)S(1)}, f32[96,512]{1,0:T(8,128)S(1)}, u32[]{:S(2)}, u32[]{:S(2)}) %collective-permute-start.2) | collective-permute-done | bytes 196640 | tf_op jit(solution)/shard_map/ppermute | solution.py:289
  105.2 4.3 %march.1 = f32[2,5,16,512]{3,2,1,0:T(8,128)} custom-call(s32[2]{0:T(128)S(1)} %copy-done.2, f32[2,5,16,512]{3,2,1,0:T(8,128)S(1)} %copy-done, f32[16,512]{1,0:T(8,128)S(1)} %copy-done.1, f32[4,176,512]{2,1,0:T(8,128)S(1)} %all_to_all.11.parts_ref, f32[96,512]{1,0:T(8,128)S(1)} %collective-permute-done.1.lower_ref, f32[96,512]{1,0:T(8,128)S(1)} %collective-permute-done.2.upper_ref), custom_call_target="tpu_custom_call" | custom-call | tf_op jit(solution)/shard_map/march/pallas_call | solution.py:290
Async XLA Ops:
  0.0 64.0 %collective-permute-start = (f32[2,5,16,512]{3,2,1,0:T(8,128)}, f32[2,5,16,512]{3,2,1,0:T(8,128)S(1)}, u32[]{:S(2)}, u32[]{:S(2)}) collective-permute-start(f32[2,5,16,512]{3,2,1,0:T(8,128)} %state_ref.7), channel_id=1, source_target_pairs={{0,1},{1,0},{2,3},{3,2},{4,5},{5,4},{6,7},{7,6},{8,9},{9,8},{10,11... | collective-permute-start | bytes 983048 | tf_op jit(solution)/shard_map/ppermute | solution.py:268
  19.4 1.0 copy-start
  64.0 0.7 copy-start.2
  65.9 22.9 %copy-start.1 = (f32[16,512]{1,0:T(8,128)S(1)}, f32[16,512]{1,0:T(8,128)}, u32[]{:S(2)}) copy-start(f32[16,512]{1,0:T(8,128)} %wall_ref.3) | copy-start | bytes 98308
  88.9 14.5 %collective-permute-start.1 = (f32[96,512]{1,0:T(8,128)S(1)}, f32[96,512]{1,0:T(8,128)S(1)}, u32[]{:S(2)}, u32[]{:S(2)}) collective-permute-start(f32[96,512]{1,0:T(8,128)S(1)} %get-tuple-element.7), channel_id=1, source_target_pairs={{0,8},{8,16},{16,24},{24,32},{32,40},{40,48},{48,56},{56,64},{64,7... | collective-permute-start | bytes 589832 | tf_op jit(solution)/shard_map/ppermute | solution.py:288
  90.8 14.3 %collective-permute-start.2 = (f32[96,512]{1,0:T(8,128)S(1)}, f32[96,512]{1,0:T(8,128)S(1)}, u32[]{:S(2)}, u32[]{:S(2)}) collective-permute-start(f32[96,512]{1,0:T(8,128)S(1)} %get-tuple-element.8), channel_id=1, source_target_pairs={{8,0},{16,8},{24,16},{32,24},{40,32},{48,40},{56,48},{64,56},{72,6... | collective-permute-start | bytes 589832 | tf_op jit(solution)/shard_map/ppermute | solution.py:289

commit v2 on v1

--- a/solution.py
+++ b/solution.py
@@ -50,8 +50,10 @@
     out_ref[...] = jnp.broadcast_to(peak[None], out_ref.shape)
 
 
-def partial_kernel(counts_ref, state_ref, other_ref, peaks_ref, out_ref, lag_ref):
-    me_x = lax.axis_index("x")
+def partial_kernel(counts_ref, state_ref, other_ref, peaks_ref, *rest):
+    *out_refs, peak_ref, lag_ref = rest
+    peak = jnp.max(peaks_ref[...], axis=0)
+    peak_ref[...] = jnp.broadcast_to(peak[None], peak_ref.shape)
     upper_half = lax.axis_index("zh")
     place = lax.axis_index(CELLS)
     is_last = place == lax.axis_size(CELLS) - 1
@@ -69,9 +71,7 @@
     lag_ref[...] = jnp.broadcast_to(
         jnp.sum(terms, axis=1, keepdims=True) * (1.0 / NT), lag_ref.shape
     )
-    peak = jnp.max(peaks_ref[...], axis=0)
-    for step in range(4):
-        target = lax.rem(me_x + step, 4)
+    for step, out_ref in enumerate(out_refs):
         own = [[(4 * step + n - m) % NT for m in range(2)] for n in range(2)]
         high = [[(4 * step + 2 + n - m) % NT for m in range(2)] for n in range(2)]
         low = [[(4 * step - 2 + n - m) % NT for m in range(2)] for n in range(2)]
@@ -93,7 +93,7 @@
                     total = scale[n][0] * fields[0]
                     for m in range(1, 4):
                         total = total + scale[n][m] * fields[m]
-                    out_ref[target, pl.ds((n * 5 + v) * 16 + 8 * t, 8), :] = total
+                    out_ref[pl.ds((n * 5 + v) * 16 + 8 * t, 8), :] = total
 
         def lag(j):
             return jnp.concatenate([lag_ref[j : j + 1, :]] * 4, axis=1)
@@ -113,54 +113,54 @@
                 total = factor[n][0] * edges[0]
                 for m in range(1, 4):
                     total = total + factor[n][m] * edges[m]
-                out_ref[target, pl.ds(160 + n * 5 + v, 1), :] = total
-        out_ref[target, pl.ds(170, 6), :] = jnp.broadcast_to(
-            jnp.concatenate([peak] * 4, axis=1), (6, 512)
-        )
-
-
-def edge_kernel(state_ref, wall_ref, parts_ref, up_ref, down_ref):
+                out_ref[pl.ds(160 + n * 5 + v, 1), :] = total
+
+
+def edge_kernel(state_ref, wall_ref, peaks_ref, part0, part1, part2, part3, far_ref, near_ref):
     place = lax.axis_index(CELLS)
     is_first = place == 0
     is_last = place == lax.axis_size(CELLS) - 1
+    is_even = lax.axis_index("core") == 0
     row = lax.broadcasted_iota(jnp.int32, (8, 512), 0)
 
+    def put(rows, up, down):
+        far_ref[rows, :] = jnp.where(is_even, down, up)
+        near_ref[rows, :] = jnp.where(is_even, up, down)
+
     def added(start, count):
-        total = parts_ref[0, pl.ds(start, count), :]
-        for k in range(1, 4):
-            total = total + parts_ref[k, pl.ds(start, count), :]
-        return total
+        rows = pl.ds(start, count)
+        return (part0[rows, :] + part1[rows, :]) + (part2[rows, :] + part3[rows, :])
 
     for n in range(2):
         for v in range(5):
             at = n * 5 + v
             lagged = jnp.broadcast_to(added(160 + at, 1), (8, 512))
             source = pltpu.roll(added(at * 16 + 8, 8), 4, axis=0)
-            packed = jnp.where(row >= 4, state_ref[n, v, 8:16, :], source)
-            packed = jnp.where(is_last & (row == 7), lagged, packed)
-            up_ref[pl.ds(at * 8, 8), :] = packed
+            up = jnp.where(row >= 4, state_ref[n, v, 8:16, :], source)
+            up = jnp.where(is_last & (row == 7), lagged, up)
             source = pltpu.roll(added(at * 16, 8), 4, axis=0)
-            packed = jnp.where(row < 4, state_ref[n, v, 0:8, :], source)
-            packed = jnp.where(is_first & (row == 0), lagged, packed)
-            down_ref[pl.ds(at * 8, 8), :] = packed
-            up_ref[pl.ds(80 + at, 1), :] = state_ref[n, v, 11:12, :]
-            down_ref[pl.ds(80 + at, 1), :] = state_ref[n, v, 4:5, :]
-    up_ref[pl.ds(90, 4), :] = wall_ref[12:16, :]
-    down_ref[pl.ds(90, 4), :] = wall_ref[0:4, :]
-    peak = parts_ref[0, 170:172, :]
-    for k in range(1, 4):
-        peak = jnp.maximum(peak, parts_ref[k, 170:172, :])
-    up_ref[pl.ds(94, 2), :] = peak
-    down_ref[pl.ds(94, 2), :] = peak
+            down = jnp.where(row < 4, state_ref[n, v, 0:8, :], source)
+            down = jnp.where(is_first & (row == 0), lagged, down)
+            put(pl.ds(at * 8, 8), up, down)
+            put(pl.ds(80 + at, 1), state_ref[n, v, 11:12, :], state_ref[n, v, 4:5, :])
+    put(pl.ds(90, 4), wall_ref[12:16, :], wall_ref[0:4, :])
+    peak = jnp.max(peaks_ref[...], axis=0)
+    peak = jnp.broadcast_to(jnp.concatenate([peak] * 4, axis=1), (2, 512))
+    far_ref[94:96, :] = peak
+    near_ref[94:96, :] = peak
 
 
 def march_kernel(
     counts_ref,
     state_ref,
     wall_ref,
-    parts_ref,
-    lower_ref,
-    upper_ref,
+    part0,
+    part1,
+    part2,
+    part3,
+    far_ref,
+    near_ref,
+    peaks_ref,
     out_ref,
     start_ref,
     now_ref,
@@ -179,34 +179,41 @@
     column = lax.broadcasted_iota(jnp.int32, (8, 512), 1)
     at_left = column == 0
     at_right = column == 511
-    peak = jnp.maximum(lower_ref[94:95, :], upper_ref[94:95, :])
-    for k in range(4):
-        peak = jnp.maximum(peak, parts_ref[k, 170:171, :])
+    is_even = lax.axis_index("core") == 0
+
+    def lower(rows):
+        return jnp.where(is_even, far_ref[rows, :], near_ref[rows, :])
+
+    def upper(rows):
+        return jnp.where(is_even, near_ref[rows, :], far_ref[rows, :])
+
+    peak = jnp.max(peaks_ref[...], axis=0)
+    peak = jnp.concatenate([peak] * 4, axis=1)
+    peak = jnp.maximum(peak, near_ref[94:95, :])
     wave = jnp.broadcast_to(peak, (8, 512))
 
     walls = [
-        jnp.concatenate([lower_ref[90:94, :]] * 2, axis=0),
+        jnp.concatenate([lower(pl.ds(90, 4))] * 2, axis=0),
         wall_ref[0:8, :],
         wall_ref[8:16, :],
-        jnp.concatenate([upper_ref[90:94, :]] * 2, axis=0),
+        jnp.concatenate([upper(pl.ds(90, 4))] * 2, axis=0),
     ]
     for t in range(4):
         decay_ref[pl.ds(8 * t, 8), :] = 0.8 / (walls[t] * walls[t])
     for n in range(2):
         for v in range(5):
             at = n * 5 + v
-            packed = lower_ref[pl.ds(at * 8, 8), :]
-            fifth = jnp.broadcast_to(lower_ref[pl.ds(80 + at, 1), :], (8, 512))
+            packed = lower(pl.ds(at * 8, 8))
+            fifth = jnp.broadcast_to(lower(pl.ds(80 + at, 1)), (8, 512))
             start_ref[n, v, 0:8, :] = jnp.where(row >= 4, packed, fifth)
             source_ref[n, v, 0:8, :] = 2.0 * pltpu.roll(packed, 4, axis=0)
-            packed = upper_ref[pl.ds(at * 8, 8), :]
-            fifth = jnp.broadcast_to(upper_ref[pl.ds(80 + at, 1), :], (8, 512))
+            packed = upper(pl.ds(at * 8, 8))
+            fifth = jnp.broadcast_to(upper(pl.ds(80 + at, 1)), (8, 512))
             start_ref[n, v, 24:32, :] = jnp.where(row < 4, packed, fifth)
             source_ref[n, v, 24:32, :] = 2.0 * pltpu.roll(packed, 4, axis=0)
             start_ref[n, v, 8:24, :] = state_ref[n, v, :, :]
-            total = parts_ref[0, pl.ds(at * 16, 16), :]
-            for k in range(1, 4):
-                total = total + parts_ref[k, pl.ds(at * 16, 16), :]
+            rows = pl.ds(at * 16, 16)
+            total = (part0[rows, :] + part1[rows, :]) + (part2[rows, :] + part3[rows, :])
             source_ref[n, v, 8:24, :] = 2.0 * total
         for t in range(4):
             rows = pl.ds(8 * t, 8)
@@ -267,29 +274,34 @@
     field = functools.partial(jax.ShapeDtypeStruct, dtype=f32)
     other = lax.ppermute(state, "zh", [(0, 1), (1, 0)])
     peak = pl.pallas_call(
-        peak_kernel, out_shape=field((128, 1, 128)), in_specs=[VMEM], out_specs=VMEM,
+        peak_kernel, out_shape=field((32, 1, 128)), in_specs=[VMEM], out_specs=VMEM,
         compiler_params=PARAMS, name="peak",
     )(state)
-    peaks = lax.all_to_all(peak, ("y", "zl", "zh"), 0, 0)
-    parts = pl.pallas_call(
-        partial_kernel, out_shape=field((4, 176, 512)),
-        in_specs=[SMEM, VMEM, VMEM, VMEM], out_specs=VMEM,
+    peaks = lax.all_to_all(peak, ("y", "x"), 0, 0)
+    *parts, peak = pl.pallas_call(
+        partial_kernel, out_shape=[field((176, 512))] * 4 + [field((16, 1, 128))],
+        in_specs=[SMEM, VMEM, VMEM, VMEM], out_specs=[VMEM] * 5,
         scratch_shapes=[pltpu.VMEM((NT, 128), f32)],
         compiler_params=PARAMS, name="partial_sources",
     )(blade_counts, state, other, peaks)
-    parts = lax.all_to_all(parts, "x", 0, 0)
-    up, down = pl.pallas_call(
+    sent = [
+        lax.ppermute(parts[step], "x", [(i, (i + step) % 4) for i in range(4)])
+        for step in (2, 1, 3)
+    ]
+    parts = [parts[0], *sent]
+    peaks = lax.all_to_all(peak, ("zl", "zh"), 0, 0)
+    far, near = pl.pallas_call(
         edge_kernel, out_shape=(field((96, 512)), field((96, 512))),
-        in_specs=[VMEM] * 3, out_specs=(VMEM, VMEM),
+        in_specs=[VMEM] * 7, out_specs=(VMEM, VMEM),
         compiler_params=PARAMS, name="edges",
-    )(state, wall_distance, parts)
+    )(state, wall_distance, peaks, *parts)
     count = lax.axis_size(CELLS)
-    ring = [(i, (i + 1) % count) for i in range(count)]
-    lower = lax.ppermute(up, CELLS, ring)
-    upper = lax.ppermute(down, CELLS, [(j, i) for i, j in ring])
+    across = [((i + 1) % count, (i + 2) % count) for i in range(0, count, 2)]
+    far = lax.ppermute(far, CELLS, across + [(j, i) for i, j in across])
+    near = lax.ppermute(near, "core", [(0, 1), (1, 0)])
     return pl.pallas_call(
         march_kernel, out_shape=field(state.shape),
-        in_specs=[SMEM] + [VMEM] * 5, out_specs=VMEM,
+        in_specs=[SMEM] + [VMEM] * 9, out_specs=VMEM,
         scratch_shapes=[
             pltpu.VMEM((2, 5, 32, 512), f32),
             pltpu.VMEM((2, 5, 32, 512), f32),
@@ -301,7 +313,7 @@
             pltpu.VMEM((5, 48, 512), f32),
         ],
         compiler_params=PARAMS, name="march",
-    )(blade_counts, state, wall_distance, parts, lower, upper)
+    )(blade_counts, state, wall_distance, *parts, far, near, peaks)
 
 
 def solution(mesh):

time: 110 us -> 106 us (0.964)
  the two profiles are of different devices: /device:TPU:8 before, /device:TPU:32 now
where the time goes in v2:
time: 106 us
  blocking collectives  53.7 us (51%)
  starting transfers between devices  34 us (32%)
  waiting for transfers between devices  11.2 us (11%)
  Pallas kernels  5.89 us (6%)
    all_to_all x1, blocking collectives, local(): peaks = lax.all_to_all(peak, ('zl', 'zh'), 0, 0)  39.3 us
    ppermute x1, starting transfers between devices, local(): other = lax.ppermute(state, 'zh', [(0, 1), (1, 0)])  19.3 us
    all_to_all x1, blocking collectives, local(): peaks = lax.all_to_all(peak, ('y', 'x'), 0, 0)  14.4 us
    ppermute x1, waiting for transfers between devices, local(): far = lax.ppermute(far, CELLS, across + [(j, i) for i, j in across])  11.2 us
    ppermute x3, starting transfers between devices, local(): lax.ppermute(parts[step], 'x', [(i, (i + step) % 4) for i in range(4)])  10.1 us
    pallas_call x1, Pallas kernels, local(): pl.pallas_call(march_kernel, out_shape=field(state.shape), in_specs=[SMEM...  4.35 us
    ppermute x1, starting transfers between devices, local(): near = lax.ppermute(near, 'core', [(0, 1), (1, 0)])  2.61 us
  transfers between devices with their start and end apart: 6, of which 1 were waited for; matrix products, arithmetic and copies ran while one was open for 0% of the time, Pallas kernels for 0%

profile of v2, /device:TPU:32, one launch (start us, length us, event | category | flops | bytes accessed | tf_op | source)
XLA Modules:
  0.0 105.9 jit_solution(10859513935543451578)
XLA Ops:
  0.0 19.3 %collective-permute-start = (f32[2,5,16,512]{3,2,1,0:T(8,128)}, f32[2,5,16,512]{3,2,1,0:T(8,128)S(1)}, u32[]{:S(2)}, u32[]{:S(2)}) collective-permute-start(f32[2,5,16,512]{3,2,1,0:T(8,128)} %state_ref.7), channel_id=1, source_target_pairs={{0,1},{1,0},{2,3},{3,2},{4,5},{5,4},{6,7},{7,6},{8,9},{9,8},{10,11... | collective-permute-start | bytes 983048 | tf_op jit(solution)/shard_map/ppermute | solution.py:275
  19.4 0.0 copy-start
  19.4 1.0 copy-done
  20.3 0.2 peak.1
  20.5 0.0 copy-start.2
  20.5 14.4 %all_to_all.10.peaks_ref = f32[32,1,128]{2,1,0:T(1,128)S(1)} all-to-all(f32[32,1,128]{2,1,0:T(1,128)S(1)} %peak.1), channel_id=1, replica_groups=mesh['y'=8,'zl'=8,'core'=2,'x'=4,'zh'=2] {'y','x'}, dimensions={0} | all-to-all | bytes 32768 | tf_op jit(solution)/shard_map/all_to_all | solution.py:280
  34.9 0.0 collective-permute-done.other_ref
  34.9 0.0 copy-done.2
  34.9 0.0 copy-start.1
  34.9 1.2 %partial_sources.1 = (f32[176,512]{1,0:T(8,128)S(1)}, f32[176,512]{1,0:T(8,128)S(1)}, f32[176,512]{1,0:T(8,128)S(1)}, f32[176,512]{1,0:T(8,128)S(1)}, f32[16,1,128]{2,1,0:T(1,128)S(1)}) custom-call(s32[2]{0:T(128)S(1)} %copy-done.2, f32[2,5,16,512]{3,2,1,0:T(8,128)S(1)} %copy-done, f32[2,5,16,512]{3,2,1,0:T(8,128)S(1)} %collective-permute-done.other_ref, ...), custom_call_target="tpu_custom_call" | custom-call | tf_op jit(solution)/shard_map/partial_sources/pallas_call | solution.py:281
  36.1 3.1 %collective-permute-start.1 = (f32[176,512]{1,0:T(8,128)S(1)}, f32[176,512]{1,0:T(8,128)S(1)}, u32[]{:S(2)}, u32[]{:S(2)}) collective-permute-start(f32[176,512]{1,0:T(8,128)S(1)} %get-tuple-element.13), channel_id=1, source_target_pairs={{0,4},{2,6},{4,0},{6,2},{1,5},{3,7},{5,1},{7,3},{8,12},{10,14},{12... | collective-permute-start | bytes 1081352 | tf_op jit(solution)/shard_map/ppermute | solution.py:288
  39.2 2.8 %collective-permute-start.2 = (f32[176,512]{1,0:T(8,128)S(1)}, f32[176,512]{1,0:T(8,128)S(1)}, u32[]{:S(2)}, u32[]{:S(2)}) collective-permute-start(f32[176,512]{1,0:T(8,128)S(1)} %get-tuple-element.14), channel_id=1, source_target_pairs={{0,2},{2,4},{4,6},{6,0},{1,3},{3,5},{5,7},{7,1},{8,10},{10,12},{12... | collective-permute-start | bytes 1081352 | tf_op jit(solution)/shard_map/ppermute | solution.py:288
  42.0 4.3 %collective-permute-start.3 = (f32[176,512]{1,0:T(8,128)S(1)}, f32[176,512]{1,0:T(8,128)S(1)}, u32[]{:S(2)}, u32[]{:S(2)}) collective-permute-start(f32[176,512]{1,0:T(8,128)S(1)} %get-tuple-element.15), channel_id=1, source_target_pairs={{0,6},{2,0},{4,2},{6,4},{1,7},{3,1},{5,3},{7,5},{8,14},{10,8},{12,... | collective-permute-start | bytes 1081352 | tf_op jit(solution)/shard_map/ppermute | solution.py:288
  46.3 39.3 %all_to_all.11.peaks_ref = f32[16,1,128]{2,1,0:T(1,128)S(1)} all-to-all(f32[16,1,128]{2,1,0:T(1,128)S(1)} %get-tuple-element.16), channel_id=1, replica_groups=mesh['y'=8,'zl'=8,'core'=2,'x'=4,'zh'=2] {'zl','zh'}, dimensions={0} | all-to-all | bytes 16384 | tf_op jit(solution)/shard_map/all_to_all | solution.py:292
  85.6 0.0 collective-permute-done.1.part1
  85.6 0.0 collective-permute-done.2.part2
  85.6 0.0 collective-permute-done.3.part3
  85.6 0.0 copy-done.1
  85.6 0.2 edges.1
  85.8 1.9 %collective-permute-start.4 = (f32[96,512]{1,0:T(8,128)S(1)}, f32[96,512]{1,0:T(8,128)S(1)}, u32[]{:S(2)}, u32[]{:S(2)}) collective-permute-start(f32[96,512]{1,0:T(8,128)S(1)} %get-tuple-element.17), channel_id=1, source_target_pairs={{8,16},{24,32},{40,48},{56,64},{72,80},{88,96},{104,112},{120,128}... | collective-permute-start | bytes 589832 | tf_op jit(solution)/shard_map/ppermute | solution.py:300
  87.7 2.6 %collective-permute-start.5 = (f32[96,512]{1,0:T(8,128)S(1)}, f32[96,512]{1,0:T(8,128)S(1)}, u32[]{:S(2)}, u32[]{:S(2)}) collective-permute-start(f32[96,512]{1,0:T(8,128)S(1)} %get-tuple-element.18), channel_id=1, source_target_pairs={{0,8},{8,0},{1,9},{9,1},{2,10},{10,2},{3,11},{11,3},{4,12},{12,4},... | collective-permute-start | bytes 589832 | tf_op jit(solution)/shard_map/ppermute | solution.py:301
  90.4 11.2 %collective-permute-done.4.far_ref = f32[96,512]{1,0:T(8,128)S(1)} collective-permute-done((f32[96,512]{1,0:T(8,128)S(1)}, f32[96,512]{1,0:T(8,128)S(1)}, u32[]{:S(2)}, u32[]{:S(2)}) %collective-permute-start.4) | collective-permute-done | bytes 196640 | tf_op jit(solution)/shard_map/ppermute | solution.py:300
  101.5 0.0 collective-permute-done.5.near_ref
  101.5 4.4 %march.1 = f32[2,5,16,512]{3,2,1,0:T(8,128)} custom-call(s32[2]{0:T(128)S(1)} %copy-done.2, f32[2,5,16,512]{3,2,1,0:T(8,128)S(1)} %copy-done, f32[16,512]{1,0:T(8,128)S(1)} %copy-done.1, f32[176,512]{1,0:T(8,128)S(1)} %get-tuple-element.12.part0, f32[176,512]{1,0:T(8,128)S(1)} %collective-permute-done.1.part1, f32[176,512]{1,0:T(8,128)S(1)} %collective-permute-done.2.part2, ...), custom_call_target="tpu_custom_call" | custom-call | tf_op jit(solution)/shard_map/march/pallas_call | solution.py:302
Async XLA Ops:
  0.0 34.9 %collective-permute-start = (f32[2,5,16,512]{3,2,1,0:T(8,128)}, f32[2,5,16,512]{3,2,1,0:T(8,128)S(1)}, u32[]{:S(2)}, u32[]{:S(2)}) collective-permute-start(f32[2,5,16,512]{3,2,1,0:T(8,128)} %state_ref.7), channel_id=1, source_target_pairs={{0,1},{1,0},{2,3},{3,2},{4,5},{5,4},{6,7},{7,6},{8,9},{9,8},{10,11... | collective-permute-start | bytes 983048 | tf_op jit(solution)/shard_map/ppermute | solution.py:275
  19.4 1.0 copy-start
  20.5 14.4 %copy-start.2 = (s32[2]{0:T(128)S(1)}, s32[2]{0:T(128)}, u32[]{:S(2)}) copy-start(s32[2]{0:T(128)} %counts_ref.3) | copy-start | bytes 28
  34.9 50.7 %copy-start.1 = (f32[16,512]{1,0:T(8,128)S(1)}, f32[16,512]{1,0:T(8,128)}, u32[]{:S(2)}) copy-start(f32[16,512]{1,0:T(8,128)} %wall_ref.3) | copy-start | bytes 98308
  36.1 49.5 %collective-permute-start.1 = (f32[176,512]{1,0:T(8,128)S(1)}, f32[176,512]{1,0:T(8,128)S(1)}, u32[]{:S(2)}, u32[]{:S(2)}) collective-permute-start(f32[176,512]{1,0:T(8,128)S(1)} %get-tuple-element.13), channel_id=1, source_target_pairs={{0,4},{2,6},{4,0},{6,2},{1,5},{3,7},{5,1},{7,3},{8,12},{10,14},{12... | collective-permute-start | bytes 1081352 | tf_op jit(solution)/shard_map/ppermute | solution.py:288
  39.2 46.4 %collective-permute-start.2 = (f32[176,512]{1,0:T(8,128)S(1)}, f32[176,512]{1,0:T(8,128)S(1)}, u32[]{:S(2)}, u32[]{:S(2)}) collective-permute-start(f32[176,512]{1,0:T(8,128)S(1)} %get-tuple-element.14), channel_id=1, source_target_pairs={{0,2},{2,4},{4,6},{6,0},{1,3},{3,5},{5,7},{7,1},{8,10},{10,12},{12... | collective-permute-start | bytes 1081352 | tf_op jit(solution)/shard_map/ppermute | solution.py:288
  42.0 43.7 %collective-permute-start.3 = (f32[176,512]{1,0:T(8,128)S(1)}, f32[176,512]{1,0:T(8,128)S(1)}, u32[]{:S(2)}, u32[]{:S(2)}) collective-permute-start(f32[176,512]{1,0:T(8,128)S(1)} %get-tuple-element.15), channel_id=1, source_target_pairs={{0,6},{2,0},{4,2},{6,4},{1,7},{3,1},{5,3},{7,5},{8,14},{10,8},{12,... | collective-permute-start | bytes 1081352 | tf_op jit(solution)/shard_map/ppermute | solution.py:288
  85.8 15.7 %collective-permute-start.4 = (f32[96,512]{1,0:T(8,128)S(1)}, f32[96,512]{1,0:T(8,128)S(1)}, u32[]{:S(2)}, u32[]{:S(2)}) collective-permute-start(f32[96,512]{1,0:T(8,128)S(1)} %get-tuple-element.17), channel_id=1, source_target_pairs={{8,16},{24,32},{40,48},{56,64},{72,80},{88,96},{104,112},{120,128}... | collective-permute-start | bytes 589832 | tf_op jit(solution)/shard_map/ppermute | solution.py:300
  87.7 13.8 %collective-permute-start.5 = (f32[96,512]{1,0:T(8,128)S(1)}, f32[96,512]{1,0:T(8,128)S(1)}, u32[]{:S(2)}, u32[]{:S(2)}) collective-permute-start(f32[96,512]{1,0:T(8,128)S(1)} %get-tuple-element.18), channel_id=1, source_target_pairs={{0,8},{8,0},{1,9},{9,1},{2,10},{10,2},{3,11},{11,3},{4,12},{12,4},... | collective-permute-start | bytes 589832 | tf_op jit(solution)/shard_map/ppermute | solution.py:301

commit v3 on v2

--- a/solution.py
+++ b/solution.py
@@ -16,7 +16,7 @@
 CELLS = ("y", "zl", "core")
 VMEM = pl.BlockSpec(memory_space=pltpu.VMEM)
 SMEM = pl.BlockSpec(memory_space=pltpu.SMEM)
-PARAMS = pltpu.CompilerParams(vmem_limit_bytes=48 * 1024 * 1024)
+PARAMS = pltpu.CompilerParams(vmem_limit_bytes=12 * 1024 * 1024)
 
 SLOPE = [
     -(2.0 / NT) * sum(k * math.sin(2.0 * math.pi * k * j / NT) for k in range(1, HALF))
@@ -25,7 +25,7 @@
 
 
 def omega_of(counts_ref):
-    return (2.0 * math.pi * ROTATION) * counts_ref[1].astype(jnp.float32)
+    return (2.0 * math.pi * ROTATION) * counts_ref[1]
 
 
 def speed_sum_and_max(r, mx, my, e):
@@ -39,7 +39,10 @@
     return ax + ay + 2.0 * c, jnp.maximum(ax, ay) + c
 
 
-def peak_kernel(state_ref, out_ref):
+def peak_kernel(whole_ref, state_ref, out_ref, counts_ref, held_ref):
+    held_ref[...] = state_ref[...]
+    for k in range(2):
+        counts_ref[k] = whole_ref[k].astype(jnp.float32)
     best = None
     for n in range(2):
         for t in range(2):
@@ -50,17 +53,19 @@
     out_ref[...] = jnp.broadcast_to(peak[None], out_ref.shape)
 
 
-def partial_kernel(counts_ref, state_ref, other_ref, peaks_ref, *rest):
-    *out_refs, peak_ref, lag_ref = rest
+def fold_kernel(peaks_ref, out_ref):
     peak = jnp.max(peaks_ref[...], axis=0)
-    peak_ref[...] = jnp.broadcast_to(peak[None], peak_ref.shape)
+    out_ref[...] = jnp.broadcast_to(peak[None], out_ref.shape)
+
+
+def partial_kernel(counts_ref, state_ref, other_ref, peaks_ref, out_ref, lag_ref):
+    me_x = lax.axis_index("x")
+    peak = jnp.max(peaks_ref[...], axis=0)
     upper_half = lax.axis_index("zh")
     place = lax.axis_index(CELLS)
     is_last = place == lax.axis_size(CELLS) - 1
     omega = omega_of(counts_ref)
-    ratio = jnp.full((NT, 128), counts_ref[1].astype(jnp.float32)) / jnp.full(
-        (NT, 128), counts_ref[0].astype(jnp.float32)
-    )
+    ratio = jnp.full((NT, 128), counts_ref[1]) / jnp.full((NT, 128), counts_ref[0])
     sigma = 2.0 * math.pi * ratio
     shift = jnp.where(is_last, sigma, -sigma)
     offset = lax.broadcasted_iota(jnp.int32, (NT, 128), 0).astype(jnp.float32)
@@ -71,7 +76,8 @@
     lag_ref[...] = jnp.broadcast_to(
         jnp.sum(terms, axis=1, keepdims=True) * (1.0 / NT), lag_ref.shape
     )
-    for step, out_ref in enumerate(out_refs):
+    for step in range(4):
+        target = lax.rem(me_x + step, 4)
         own = [[(4 * step + n - m) % NT for m in range(2)] for n in range(2)]
         high = [[(4 * step + 2 + n - m) % NT for m in range(2)] for n in range(2)]
         low = [[(4 * step - 2 + n - m) % NT for m in range(2)] for n in range(2)]
@@ -93,7 +99,7 @@
                     total = scale[n][0] * fields[0]
                     for m in range(1, 4):
                         total = total + scale[n][m] * fields[m]
-                    out_ref[pl.ds((n * 5 + v) * 16 + 8 * t, 8), :] = total
+                    out_ref[target, pl.ds((n * 5 + v) * 16 + 8 * t, 8), :] = total
 
         def lag(j):
             return jnp.concatenate([lag_ref[j : j + 1, :]] * 4, axis=1)
@@ -113,10 +119,13 @@
                 total = factor[n][0] * edges[0]
                 for m in range(1, 4):
                     total = total + factor[n][m] * edges[m]
-                out_ref[pl.ds(160 + n * 5 + v, 1), :] = total
-
-
-def edge_kernel(state_ref, wall_ref, peaks_ref, part0, part1, part2, part3, far_ref, near_ref):
+                out_ref[target, pl.ds(160 + n * 5 + v, 1), :] = total
+        out_ref[target, pl.ds(170, 6), :] = jnp.broadcast_to(
+            jnp.concatenate([peak] * 4, axis=1), (6, 512)
+        )
+
+
+def edge_kernel(state_ref, wall_ref, parts_ref, far_ref, near_ref):
     place = lax.axis_index(CELLS)
     is_first = place == 0
     is_last = place == lax.axis_size(CELLS) - 1
@@ -129,7 +138,9 @@
 
     def added(start, count):
         rows = pl.ds(start, count)
-        return (part0[rows, :] + part1[rows, :]) + (part2[rows, :] + part3[rows, :])
+        return (parts_ref[0, rows, :] + parts_ref[1, rows, :]) + (
+            parts_ref[2, rows, :] + parts_ref[3, rows, :]
+        )
 
     for n in range(2):
         for v in range(5):
@@ -144,23 +155,16 @@
             put(pl.ds(at * 8, 8), up, down)
             put(pl.ds(80 + at, 1), state_ref[n, v, 11:12, :], state_ref[n, v, 4:5, :])
     put(pl.ds(90, 4), wall_ref[12:16, :], wall_ref[0:4, :])
-    peak = jnp.max(peaks_ref[...], axis=0)
-    peak = jnp.broadcast_to(jnp.concatenate([peak] * 4, axis=1), (2, 512))
-    far_ref[94:96, :] = peak
-    near_ref[94:96, :] = peak
+    put(pl.ds(94, 2), wall_ref[14:16, :], wall_ref[0:2, :])
 
 
 def march_kernel(
     counts_ref,
     state_ref,
     wall_ref,
-    part0,
-    part1,
-    part2,
-    part3,
+    parts_ref,
     far_ref,
     near_ref,
-    peaks_ref,
     out_ref,
     start_ref,
     now_ref,
@@ -187,9 +191,9 @@
     def upper(rows):
         return jnp.where(is_even, near_ref[rows, :], far_ref[rows, :])
 
-    peak = jnp.max(peaks_ref[...], axis=0)
-    peak = jnp.concatenate([peak] * 4, axis=1)
-    peak = jnp.maximum(peak, near_ref[94:95, :])
+    peak = parts_ref[0, 170:171, :]
+    for k in range(1, 4):
+        peak = jnp.maximum(peak, parts_ref[k, 170:171, :])
     wave = jnp.broadcast_to(peak, (8, 512))
 
     walls = [
@@ -213,7 +217,9 @@
             source_ref[n, v, 24:32, :] = 2.0 * pltpu.roll(packed, 4, axis=0)
             start_ref[n, v, 8:24, :] = state_ref[n, v, :, :]
             rows = pl.ds(at * 16, 16)
-            total = (part0[rows, :] + part1[rows, :]) + (part2[rows, :] + part3[rows, :])
+            total = (parts_ref[0, rows, :] + parts_ref[1, rows, :]) + (
+                parts_ref[2, rows, :] + parts_ref[3, rows, :]
+            )
             source_ref[n, v, 8:24, :] = 2.0 * total
         for t in range(4):
             rows = pl.ds(8 * t, 8)
@@ -273,35 +279,36 @@
     f32 = jnp.float32
     field = functools.partial(jax.ShapeDtypeStruct, dtype=f32)
     other = lax.ppermute(state, "zh", [(0, 1), (1, 0)])
+    peak, counts, state = pl.pallas_call(
+        peak_kernel, out_shape=(field((8, 1, 128)), field((2,)), field(state.shape)),
+        in_specs=[SMEM, VMEM], out_specs=(VMEM, SMEM, VMEM),
+        compiler_params=PARAMS, name="peak",
+    )(blade_counts, state)
+    peaks = lax.all_to_all(peak, "y", 0, 0)
     peak = pl.pallas_call(
-        peak_kernel, out_shape=field((32, 1, 128)), in_specs=[VMEM], out_specs=VMEM,
-        compiler_params=PARAMS, name="peak",
-    )(state)
-    peaks = lax.all_to_all(peak, ("y", "x"), 0, 0)
-    *parts, peak = pl.pallas_call(
-        partial_kernel, out_shape=[field((176, 512))] * 4 + [field((16, 1, 128))],
-        in_specs=[SMEM, VMEM, VMEM, VMEM], out_specs=[VMEM] * 5,
+        fold_kernel, out_shape=field((32, 1, 128)), in_specs=[VMEM], out_specs=VMEM,
+        compiler_params=PARAMS, name="fold",
+    )(peaks)
+    peaks = lax.all_to_all(peak, ("zl", "zh", "core"), 0, 0)
+    parts = pl.pallas_call(
+        partial_kernel, out_shape=field((4, 176, 512)),
+        in_specs=[SMEM, VMEM, VMEM, VMEM], out_specs=VMEM,
         scratch_shapes=[pltpu.VMEM((NT, 128), f32)],
         compiler_params=PARAMS, name="partial_sources",
-    )(blade_counts, state, other, peaks)
-    sent = [
-        lax.ppermute(parts[step], "x", [(i, (i + step) % 4) for i in range(4)])
-        for step in (2, 1, 3)
-    ]
-    parts = [parts[0], *sent]
-    peaks = lax.all_to_all(peak, ("zl", "zh"), 0, 0)
+    )(counts, state, other, peaks)
+    parts = lax.all_to_all(parts, "x", 0, 0)
     far, near = pl.pallas_call(
         edge_kernel, out_shape=(field((96, 512)), field((96, 512))),
-        in_specs=[VMEM] * 7, out_specs=(VMEM, VMEM),
+        in_specs=[VMEM] * 3, out_specs=(VMEM, VMEM),
         compiler_params=PARAMS, name="edges",
-    )(state, wall_distance, peaks, *parts)
+    )(state, wall_distance, parts)
     count = lax.axis_size(CELLS)
     across = [((i + 1) % count, (i + 2) % count) for i in range(0, count, 2)]
     far = lax.ppermute(far, CELLS, across + [(j, i) for i, j in across])
     near = lax.ppermute(near, "core", [(0, 1), (1, 0)])
     return pl.pallas_call(
         march_kernel, out_shape=field(state.shape),
-        in_specs=[SMEM] + [VMEM] * 9, out_specs=VMEM,
+        in_specs=[SMEM] + [VMEM] * 5, out_specs=VMEM,
         scratch_shapes=[
             pltpu.VMEM((2, 5, 32, 512), f32),
             pltpu.VMEM((2, 5, 32, 512), f32),
@@ -313,7 +320,7 @@
             pltpu.VMEM((5, 48, 512), f32),
         ],
         compiler_params=PARAMS, name="march",
-    )(blade_counts, state, wall_distance, *parts, far, near, peaks)
+    )(counts, state, wall_distance, parts, far, near)
 
 
 def solution(mesh):

time: 106 us -> 103 us (0.972)
  starting transfers between devices: 34 us -> 24.7 us
  blocking collectives: 53.7 us -> 58.8 us
    ppermute x3 -> x0, starting transfers between devices: 10.1 us -> none  [local(): lax.ppermute(parts[step], 'x', [(i, (i + step) % 4) for i in range(4)])]
    all_to_all x2 -> x3, blocking collectives: 53.7 us -> 58.8 us  [the longest x1 26.1 us: local(): peaks = lax.all_to_all(peak, ('zl', 'zh', 'core'), 0, 0)]
    pallas_call x2 -> x3, Pallas kernels: 1.38 us -> 2.35 us  [the longest x1 1.18 us: local(): pl.pallas_call(partial_kernel, out_shape=field((4, 176, 512)), in_specs=[...]
  transfers between devices with their start and end apart: 6 -> 3, of which waited for: 1 -> 1; matrix products, arithmetic and copies ran while one was open for 0% -> 0% of each run, Pallas kernels for 0% -> 1%
where the time goes in v3:
time: 103 us; the launch traced here: 102 us
  blocking collectives  58.8 us (57%)
  starting transfers between devices  24.7 us (24%)
  waiting for transfers between devices  10.3 us (10%)
  Pallas kernels  6.88 us (7%)
  local copies, waits for them, and re-layouts  1.64 us (2%)
    all_to_all x1, blocking collectives, local(): peaks = lax.all_to_all(peak, ('zl', 'zh', 'core'), 0, 0)  26.1 us
    all_to_all x1, blocking collectives, local(): parts = lax.all_to_all(parts, 'x', 0, 0)  23.4 us
    ppermute x1, starting transfers between devices, local(): other = lax.ppermute(state, 'zh', [(0, 1), (1, 0)])  19.3 us
    ppermute x1, waiting for transfers between devices, local(): far = lax.ppermute(far, CELLS, across + [(j, i) for i, j in across])  10.3 us
    all_to_all x1, blocking collectives, local(): peaks = lax.all_to_all(peak, 'y', 0, 0)  9.31 us
    pallas_call x1, Pallas kernels, local(): pl.pallas_call(march_kernel, out_shape=field(state.shape), in_specs=[SMEM...  4.42 us
    ppermute x1, starting transfers between devices, local(): far = lax.ppermute(far, CELLS, across + [(j, i) for i, j in across])  2.83 us
    ppermute x1, starting transfers between devices, local(): near = lax.ppermute(near, 'core', [(0, 1), (1, 0)])  2.54 us
  transfers between devices with their start and end apart: 3, of which 1 were waited for; matrix products, arithmetic and copies ran while one was open for 0% of the time, Pallas kernels for 1%

profile of v3, /device:TPU:32, one launch (start us, length us, event | category | flops | bytes accessed | tf_op | source)
XLA Modules:
  0.0 102.4 jit_solution(6162788166831537722)
XLA Ops:
  0.0 19.3 %collective-permute-start = (f32[2,5,16,512]{3,2,1,0:T(8,128)}, f32[2,5,16,512]{3,2,1,0:T(8,128)S(1)}, u32[]{:S(2)}, u32[]{:S(2)}) collective-permute-start(f32[2,5,16,512]{3,2,1,0:T(8,128)} %state_ref.1), channel_id=1, source_target_pairs={{0,1},{1,0},{2,3},{3,2},{4,5},{5,4},{6,7},{7,6},{8,9},{9,8},{10,11... | collective-permute-start | bytes 983048 | tf_op jit(solution)/shard_map/ppermute | solution.py:281
  19.4 0.0 copy-start
  19.4 1.0 copy-done
  20.3 0.0 copy-start.2
  20.3 0.7 copy-done.2
  21.0 1.2 %peak.1 = (f32[8,1,128]{2,1,0:T(1,128)S(1)}, f32[2]{0:T(128)S(1)}, f32[2,5,16,512]{3,2,1,0:T(8,128)S(1)}) custom-call(s32[2]{0:T(128)S(1)} %copy-done.2, f32[2,5,16,512]{3,2,1,0:T(8,128)S(1)} %copy-done), custom_call_target="tpu_custom_call" | custom-call | tf_op jit(solution)/shard_map/peak/pallas_call | solution.py:282
  22.2 9.3 %all_to_all.15.peaks_ref = f32[8,1,128]{2,1,0:T(1,128)S(1)} all-to-all(f32[8,1,128]{2,1,0:T(1,128)S(1)} %get-tuple-element.12), channel_id=1, replica_groups=mesh['y'=8,'zl'=8,'core'=2,'x'=4,'zh'=2] {'y'}, dimensions={0} | all-to-all | bytes 8192 | tf_op jit(solution)/shard_map/all_to_all | solution.py:287
  31.5 26.1 %all_to_all.16.peaks_ref = f32[32,1,128]{2,1,0:T(1,128)S(1)} all-to-all(f32[32,1,128]{2,1,0:T(1,128)S(1)} %fold.1), channel_id=1, replica_groups=mesh['y'=8,'zl'=8,'core'=2,'x'=4,'zh'=2] {'zl','zh','core'}, dimensions={0} | all-to-all | bytes 32768 | tf_op jit(solution)/shard_map/all_to_all | solution.py:292
  57.6 0.0 collective-permute-done.other_ref
  57.6 1.2 %partial_sources.1 = f32[4,176,512]{2,1,0:T(8,128)S(1)} custom-call(f32[2]{0:T(128)S(1)} %get-tuple-element.10.counts_ref, f32[2,5,16,512]{3,2,1,0:T(8,128)S(1)} %get-tuple-element.11.state_ref, f32[2,5,16,512]{3,2,1,0:T(8,128)S(1)} %collective-permute-done.other_ref, f32[32,1,128]{2,1,0:T(1,128)S(1)} %all_to_all.16.peaks_ref), custom_call_target="tpu_custom_call" | custom-call | tf_op jit(solution)/shard_map/partial_sources/pallas_call | solution.py:293
  58.8 0.0 copy-start.1
  58.8 23.4 %all_to_all.17.parts_ref = f32[4,176,512]{2,1,0:T(8,128)S(1)} all-to-all(f32[4,176,512]{2,1,0:T(8,128)S(1)} %partial_sources.1), channel_id=1, replica_groups=mesh['y'=8,'zl'=8,'core'=2,'x'=4,'zh'=2] {'x'}, dimensions={0} | all-to-all | bytes 2883584 | tf_op jit(solution)/shard_map/all_to_all | solution.py:299
  82.2 0.0 copy-done.1
  82.2 0.1 edges.1
  82.3 2.8 %collective-permute-start.1 = (f32[96,512]{1,0:T(8,128)S(1)}, f32[96,512]{1,0:T(8,128)S(1)}, u32[]{:S(2)}, u32[]{:S(2)}) collective-permute-start(f32[96,512]{1,0:T(8,128)S(1)} %get-tuple-element.13), channel_id=1, source_target_pairs={{8,16},{24,32},{40,48},{56,64},{72,80},{88,96},{104,112},{120,128}... | collective-permute-start | bytes 589832 | tf_op jit(solution)/shard_map/ppermute | solution.py:307
  85.1 2.5 %collective-permute-start.2 = (f32[96,512]{1,0:T(8,128)S(1)}, f32[96,512]{1,0:T(8,128)S(1)}, u32[]{:S(2)}, u32[]{:S(2)}) collective-permute-start(f32[96,512]{1,0:T(8,128)S(1)} %get-tuple-element.14), channel_id=1, source_target_pairs={{0,8},{8,0},{1,9},{9,1},{2,10},{10,2},{3,11},{11,3},{4,12},{12,4},... | collective-permute-start | bytes 589832 | tf_op jit(solution)/shard_map/ppermute | solution.py:308
  87.7 10.3 %collective-permute-done.1.far_ref = f32[96,512]{1,0:T(8,128)S(1)} collective-permute-done((f32[96,512]{1,0:T(8,128)S(1)}, f32[96,512]{1,0:T(8,128)S(1)}, u32[]{:S(2)}, u32[]{:S(2)}) %collective-permute-start.1) | collective-permute-done | bytes 196640 | tf_op jit(solution)/shard_map/ppermute | solution.py:307
  98.0 0.0 collective-permute-done.2.near_ref
  98.0 4.4 %march.1 = f32[2,5,16,512]{3,2,1,0:T(8,128)} custom-call(f32[2]{0:T(128)S(1)} %get-tuple-element.10.counts_ref, f32[2,5,16,512]{3,2,1,0:T(8,128)S(1)} %get-tuple-element.11.state_ref, f32[16,512]{1,0:T(8,128)S(1)} %copy-done.1, f32[4,176,512]{2,1,0:T(8,128)S(1)} %all_to_all.17.parts_ref, f32[96,512]{1,0:T(8,128)S(1)} %collective-permute-done.1.far_ref, ...), custom_call_target="tpu_custom_call" | custom-call | tf_op jit(solution)/shard_map/march/pallas_call | solution.py:309
  (1 shorter events, 0.0 us)
Async XLA Ops:
  0.0 57.6 %collective-permute-start = (f32[2,5,16,512]{3,2,1,0:T(8,128)}, f32[2,5,16,512]{3,2,1,0:T(8,128)S(1)}, u32[]{:S(2)}, u32[]{:S(2)}) collective-permute-start(f32[2,5,16,512]{3,2,1,0:T(8,128)} %state_ref.1), channel_id=1, source_target_pairs={{0,1},{1,0},{2,3},{3,2},{4,5},{5,4},{6,7},{7,6},{8,9},{9,8},{10,11... | collective-permute-start | bytes 983048 | tf_op jit(solution)/shard_map/ppermute | solution.py:281
  19.4 1.0 copy-start
  20.3 0.7 copy-start.2
  58.8 23.4 %copy-start.1 = (f32[16,512]{1,0:T(8,128)S(1)}, f32[16,512]{1,0:T(8,128)}, u32[]{:S(2)}) copy-start(f32[16,512]{1,0:T(8,128)} %wall_ref.3) | copy-start | bytes 98308
  82.3 15.7 %collective-permute-start.1 = (f32[96,512]{1,0:T(8,128)S(1)}, f32[96,512]{1,0:T(8,128)S(1)}, u32[]{:S(2)}, u32[]{:S(2)}) collective-permute-start(f32[96,512]{1,0:T(8,128)S(1)} %get-tuple-element.13), channel_id=1, source_target_pairs={{8,16},{24,32},{40,48},{56,64},{72,80},{88,96},{104,112},{120,128}... | collective-permute-start | bytes 589832 | tf_op jit(solution)/shard_map/ppermute | solution.py:307
  85.1 12.9 %collective-permute-start.2 = (f32[96,512]{1,0:T(8,128)S(1)}, f32[96,512]{1,0:T(8,128)S(1)}, u32[]{:S(2)}, u32[]{:S(2)}) collective-permute-start(f32[96,512]{1,0:T(8,128)S(1)} %get-tuple-element.14), channel_id=1, source_target_pairs={{0,8},{8,0},{1,9},{9,1},{2,10},{10,2},{3,11},{11,3},{4,12},{12,4},... | collective-permute-start | bytes 589832 | tf_op jit(solution)/shard_map/ppermute | solution.py:308

commit v4 on v3

--- a/solution.py
+++ b/solution.py
@@ -58,13 +58,42 @@
     out_ref[...] = jnp.broadcast_to(peak[None], out_ref.shape)
 
 
+def add_partials(counts_ref, state_ref, other_ref, out_ref, edge):
+    me_x = lax.axis_index("x")
+    upper_half = lax.axis_index("zh")
+    omega = omega_of(counts_ref)
+    row = lax.broadcasted_iota(jnp.int32, (8, 512), 0)
+    for v in range(5):
+        fields = [
+            jnp.where((row < 4) == edge, ref[m, v, 0:8, :], ref[m, v, 8:16, :])
+            for ref in (state_ref, other_ref)
+            for m in range(2)
+        ]
+        for step in range(4):
+            target = lax.rem(me_x + step, 4)
+            for n in range(2):
+                total = None
+                for m, field in enumerate(fields):
+                    own, high, low = offsets(step, n, m)
+                    factor = SLOPE[own]
+                    if m >= 2:
+                        factor = jnp.where(upper_half == 1, SLOPE[high], SLOPE[low])
+                    term = (omega * factor) * field
+                    total = term if total is None else total + term
+                out_ref[target, pl.ds((n * 5 + v) * 8, 8), :] = total
+
+
+def offsets(step, n, m):
+    apart = 4 * step + n - m % 2
+    return apart % NT, (apart + 2) % NT, (apart - 2) % NT
+
+
 def partial_kernel(counts_ref, state_ref, other_ref, peaks_ref, out_ref, lag_ref):
     me_x = lax.axis_index("x")
-    peak = jnp.max(peaks_ref[...], axis=0)
     upper_half = lax.axis_index("zh")
     place = lax.axis_index(CELLS)
     is_last = place == lax.axis_size(CELLS) - 1
-    omega = omega_of(counts_ref)
+    add_partials(counts_ref, state_ref, other_ref, out_ref, True)
     ratio = jnp.full((NT, 128), counts_ref[1]) / jnp.full((NT, 128), counts_ref[0])
     sigma = 2.0 * math.pi * ratio
     shift = jnp.where(is_last, sigma, -sigma)
@@ -76,56 +105,39 @@
     lag_ref[...] = jnp.broadcast_to(
         jnp.sum(terms, axis=1, keepdims=True) * (1.0 / NT), lag_ref.shape
     )
+
+    def lag(j):
+        return jnp.concatenate([lag_ref[j : j + 1, :]] * 4, axis=1)
+
+    peak = jnp.max(peaks_ref[...], axis=0)
+    peak = jnp.broadcast_to(jnp.concatenate([peak] * 4, axis=1), (6, 512))
     for step in range(4):
         target = lax.rem(me_x + step, 4)
-        own = [[(4 * step + n - m) % NT for m in range(2)] for n in range(2)]
-        high = [[(4 * step + 2 + n - m) % NT for m in range(2)] for n in range(2)]
-        low = [[(4 * step - 2 + n - m) % NT for m in range(2)] for n in range(2)]
-        scale = [
-            [omega * SLOPE[own[n][m]] for m in range(2)]
-            + [
-                omega * jnp.where(upper_half == 1, SLOPE[high[n][m]], SLOPE[low[n][m]])
-                for m in range(2)
-            ]
-            for n in range(2)
-        ]
-        for v in range(5):
-            for t in range(2):
-                rows = pl.ds(8 * t, 8)
-                fields = [state_ref[m, v, rows, :] for m in range(2)] + [
-                    other_ref[m, v, rows, :] for m in range(2)
-                ]
-                for n in range(2):
-                    total = scale[n][0] * fields[0]
-                    for m in range(1, 4):
-                        total = total + scale[n][m] * fields[m]
-                    out_ref[target, pl.ds((n * 5 + v) * 16 + 8 * t, 8), :] = total
-
-        def lag(j):
-            return jnp.concatenate([lag_ref[j : j + 1, :]] * 4, axis=1)
-
-        factor = [
-            [lag(own[n][m]) for m in range(2)]
-            + [jnp.where(upper_half == 1, lag(high[n][m]), lag(low[n][m])) for m in range(2)]
-            for n in range(2)
-        ]
-        for v in range(5):
-            edges = [
-                jnp.where(is_last, ref[m, v, 15:16, :], ref[m, v, 0:1, :])
-                for ref in (state_ref, other_ref)
-                for m in range(2)
-            ]
-            for n in range(2):
-                total = factor[n][0] * edges[0]
-                for m in range(1, 4):
-                    total = total + factor[n][m] * edges[m]
-                out_ref[target, pl.ds(160 + n * 5 + v, 1), :] = total
-        out_ref[target, pl.ds(170, 6), :] = jnp.broadcast_to(
-            jnp.concatenate([peak] * 4, axis=1), (6, 512)
-        )
-
-
-def edge_kernel(state_ref, wall_ref, parts_ref, far_ref, near_ref):
+        for n in range(2):
+            factor = []
+            for m in range(4):
+                own, high, low = offsets(step, n, m)
+                factor.append(
+                    lag(own) if m < 2 else jnp.where(upper_half == 1, lag(high), lag(low))
+                )
+            for v in range(5):
+                total = None
+                for m, ref in enumerate((state_ref, state_ref, other_ref, other_ref)):
+                    edge = jnp.where(is_last, ref[m % 2, v, 15:16, :], ref[m % 2, v, 0:1, :])
+                    term = factor[m] * edge
+                    total = term if total is None else total + term
+                out_ref[target, pl.ds(80 + n * 5 + v, 1), :] = total
+        out_ref[target, pl.ds(90, 6), :] = peak
+
+
+def added(parts_ref, start, count):
+    rows = pl.ds(start, count)
+    return (parts_ref[0, rows, :] + parts_ref[1, rows, :]) + (
+        parts_ref[2, rows, :] + parts_ref[3, rows, :]
+    )
+
+
+def edge_kernel(counts_ref, state_ref, other_ref, wall_ref, outer_ref, far_ref, near_ref, inner_ref):
     place = lax.axis_index(CELLS)
     is_first = place == 0
     is_last = place == lax.axis_size(CELLS) - 1
@@ -136,33 +148,28 @@
         far_ref[rows, :] = jnp.where(is_even, down, up)
         near_ref[rows, :] = jnp.where(is_even, up, down)
 
-    def added(start, count):
-        rows = pl.ds(start, count)
-        return (parts_ref[0, rows, :] + parts_ref[1, rows, :]) + (
-            parts_ref[2, rows, :] + parts_ref[3, rows, :]
-        )
-
     for n in range(2):
         for v in range(5):
             at = n * 5 + v
-            lagged = jnp.broadcast_to(added(160 + at, 1), (8, 512))
-            source = pltpu.roll(added(at * 16 + 8, 8), 4, axis=0)
+            lagged = jnp.broadcast_to(added(outer_ref, 80 + at, 1), (8, 512))
+            source = pltpu.roll(added(outer_ref, at * 8, 8), 4, axis=0)
             up = jnp.where(row >= 4, state_ref[n, v, 8:16, :], source)
             up = jnp.where(is_last & (row == 7), lagged, up)
-            source = pltpu.roll(added(at * 16, 8), 4, axis=0)
             down = jnp.where(row < 4, state_ref[n, v, 0:8, :], source)
             down = jnp.where(is_first & (row == 0), lagged, down)
             put(pl.ds(at * 8, 8), up, down)
             put(pl.ds(80 + at, 1), state_ref[n, v, 11:12, :], state_ref[n, v, 4:5, :])
     put(pl.ds(90, 4), wall_ref[12:16, :], wall_ref[0:4, :])
     put(pl.ds(94, 2), wall_ref[14:16, :], wall_ref[0:2, :])
+    add_partials(counts_ref, state_ref, other_ref, inner_ref, False)
 
 
 def march_kernel(
     counts_ref,
     state_ref,
     wall_ref,
-    parts_ref,
+    outer_ref,
+    inner_ref,
     far_ref,
     near_ref,
     out_ref,
@@ -191,9 +198,9 @@
     def upper(rows):
         return jnp.where(is_even, near_ref[rows, :], far_ref[rows, :])
 
-    peak = parts_ref[0, 170:171, :]
+    peak = outer_ref[0, 90:91, :]
     for k in range(1, 4):
-        peak = jnp.maximum(peak, parts_ref[k, 170:171, :])
+        peak = jnp.maximum(peak, outer_ref[k, 90:91, :])
     wave = jnp.broadcast_to(peak, (8, 512))
 
     walls = [
@@ -216,11 +223,10 @@
             start_ref[n, v, 24:32, :] = jnp.where(row < 4, packed, fifth)
             source_ref[n, v, 24:32, :] = 2.0 * pltpu.roll(packed, 4, axis=0)
             start_ref[n, v, 8:24, :] = state_ref[n, v, :, :]
-            rows = pl.ds(at * 16, 16)
-            total = (parts_ref[0, rows, :] + parts_ref[1, rows, :]) + (
-                parts_ref[2, rows, :] + parts_ref[3, rows, :]
-            )
-            source_ref[n, v, 8:24, :] = 2.0 * total
+            outer = 2.0 * added(outer_ref, at * 8, 8)
+            inner = 2.0 * added(inner_ref, at * 8, 8)
+            source_ref[n, v, 8:16, :] = jnp.where(row < 4, outer, inner)
+            source_ref[n, v, 16:24, :] = jnp.where(row < 4, inner, outer)
         for t in range(4):
             rows = pl.ds(8 * t, 8)
             both, _ = speed_sum_and_max(*(start_ref[n, v, rows, :] for v in range(4)))
@@ -290,25 +296,26 @@
         compiler_params=PARAMS, name="fold",
     )(peaks)
     peaks = lax.all_to_all(peak, ("zl", "zh", "core"), 0, 0)
-    parts = pl.pallas_call(
-        partial_kernel, out_shape=field((4, 176, 512)),
+    outer = pl.pallas_call(
+        partial_kernel, out_shape=field((4, 96, 512)),
         in_specs=[SMEM, VMEM, VMEM, VMEM], out_specs=VMEM,
         scratch_shapes=[pltpu.VMEM((NT, 128), f32)],
         compiler_params=PARAMS, name="partial_sources",
     )(counts, state, other, peaks)
-    parts = lax.all_to_all(parts, "x", 0, 0)
-    far, near = pl.pallas_call(
-        edge_kernel, out_shape=(field((96, 512)), field((96, 512))),
-        in_specs=[VMEM] * 3, out_specs=(VMEM, VMEM),
+    outer = lax.all_to_all(outer, "x", 0, 0)
+    far, near, inner = pl.pallas_call(
+        edge_kernel, out_shape=(field((96, 512)), field((96, 512)), field((4, 80, 512))),
+        in_specs=[SMEM] + [VMEM] * 4, out_specs=(VMEM, VMEM, VMEM),
         compiler_params=PARAMS, name="edges",
-    )(state, wall_distance, parts)
+    )(counts, state, other, wall_distance, outer)
     count = lax.axis_size(CELLS)
     across = [((i + 1) % count, (i + 2) % count) for i in range(0, count, 2)]
     far = lax.ppermute(far, CELLS, across + [(j, i) for i, j in across])
     near = lax.ppermute(near, "core", [(0, 1), (1, 0)])
+    inner = lax.all_to_all(inner, "x", 0, 0)
     return pl.pallas_call(
         march_kernel, out_shape=field(state.shape),
-        in_specs=[SMEM] + [VMEM] * 5, out_specs=VMEM,
+        in_specs=[SMEM] + [VMEM] * 6, out_specs=VMEM,
         scratch_shapes=[
             pltpu.VMEM((2, 5, 32, 512), f32),
             pltpu.VMEM((2, 5, 32, 512), f32),
@@ -320,7 +327,7 @@
             pltpu.VMEM((5, 48, 512), f32),
         ],
         compiler_params=PARAMS, name="march",
-    )(counts, state, wall_distance, parts, far, near)
+    )(counts, state, wall_distance, outer, inner, far, near)
 
 
 def solution(mesh):

time: 103 us -> 101 us (0.981)
  the two profiles are of different devices: /device:TPU:32 before, /device:TPU:34 now
where the time goes in v4:
time: 101 us
  blocking collectives  50.9 us (50%)
  starting transfers between devices  29.6 us (29%)
  waiting for transfers between devices  10.3 us (10%)
  Pallas kernels  8.12 us (8%)
  local copies, waits for them, and re-layouts  1.64 us (2%)
    all_to_all x1, blocking collectives, local(): peaks = lax.all_to_all(peak, ('zl', 'zh', 'core'), 0, 0)  26.1 us
    ppermute x1, starting transfers between devices, local(): other = lax.ppermute(state, 'zh', [(0, 1), (1, 0)])  19.3 us
    all_to_all x1, blocking collectives, local(): outer = lax.all_to_all(outer, 'x', 0, 0)  15.4 us
    ppermute x1, waiting for transfers between devices, local(): far = lax.ppermute(far, CELLS, across + [(j, i) for i, j in across])  10.3 us
    all_to_all x1, blocking collectives, local(): peaks = lax.all_to_all(peak, 'y', 0, 0)  9.31 us
    all_to_all x1, starting transfers between devices, local(): inner = lax.all_to_all(inner, 'x', 0, 0)  4.91 us
    pallas_call x1, Pallas kernels, local(): pl.pallas_call(march_kernel, out_shape=field(state.shape), in_specs=[SMEM...  4.31 us
    ppermute x1, starting transfers between devices, local(): near = lax.ppermute(near, 'core', [(0, 1), (1, 0)])  2.82 us
  transfers between devices with their start and end apart: 4, of which 1 were waited for; matrix products, arithmetic and copies ran while one was open for 0% of the time, Pallas kernels for 1%

profile of v4, /device:TPU:34, one launch (start us, length us, event | category | flops | bytes accessed | tf_op | source)
XLA Modules:
  0.0 100.6 jit_solution(14649211961202373338)
XLA Ops:
  0.0 19.3 %collective-permute-start = (f32[2,5,16,512]{3,2,1,0:T(8,128)}, f32[2,5,16,512]{3,2,1,0:T(8,128)S(1)}, u32[]{:S(2)}, u32[]{:S(2)}) collective-permute-start(f32[2,5,16,512]{3,2,1,0:T(8,128)} %state_ref.1), channel_id=1, source_target_pairs={{0,1},{1,0},{2,3},{3,2},{4,5},{5,4},{6,7},{7,6},{8,9},{9,8},{10,11... | collective-permute-start | bytes 983048 | tf_op jit(solution)/shard_map/ppermute | solution.py:287
  19.4 0.0 copy-start
  19.4 1.0 copy-done
  20.3 0.0 copy-start.2
  20.3 0.7 copy-done.2
  21.0 1.2 %peak.1 = (f32[8,1,128]{2,1,0:T(1,128)S(1)}, f32[2]{0:T(128)S(1)}, f32[2,5,16,512]{3,2,1,0:T(8,128)S(1)}) custom-call(s32[2]{0:T(128)S(1)} %copy-done.2, f32[2,5,16,512]{3,2,1,0:T(8,128)S(1)} %copy-done), custom_call_target="tpu_custom_call" | custom-call | tf_op jit(solution)/shard_map/peak/pallas_call | solution.py:288
  22.2 9.3 %all_to_all.20.peaks_ref = f32[8,1,128]{2,1,0:T(1,128)S(1)} all-to-all(f32[8,1,128]{2,1,0:T(1,128)S(1)} %get-tuple-element.13), channel_id=1, replica_groups=mesh['y'=8,'zl'=8,'core'=2,'x'=4,'zh'=2] {'y'}, dimensions={0} | all-to-all | bytes 8192 | tf_op jit(solution)/shard_map/all_to_all | solution.py:293
  31.5 26.1 %all_to_all.21.peaks_ref = f32[32,1,128]{2,1,0:T(1,128)S(1)} all-to-all(f32[32,1,128]{2,1,0:T(1,128)S(1)} %fold.1), channel_id=1, replica_groups=mesh['y'=8,'zl'=8,'core'=2,'x'=4,'zh'=2] {'zl','zh','core'}, dimensions={0} | all-to-all | bytes 32768 | tf_op jit(solution)/shard_map/all_to_all | solution.py:298
  57.6 0.0 collective-permute-done.other_ref
  57.6 1.1 %partial_sources.1 = f32[4,96,512]{2,1,0:T(8,128)S(1)} custom-call(f32[2]{0:T(128)S(1)} %get-tuple-element.11.counts_ref, f32[2,5,16,512]{3,2,1,0:T(8,128)S(1)} %get-tuple-element.12.state_ref, f32[2,5,16,512]{3,2,1,0:T(8,128)S(1)} %collective-permute-done.other_ref, f32[32,1,128]{2,1,0:T(1,128)S(1)} %all_to_all.21.peaks_ref), custom_call_target="tpu_custom_call" | custom-call | tf_op jit(solution)/shard_map/partial_sources/pallas_call | solution.py:299
  58.7 0.0 copy-start.1
  58.7 15.4 %all_to_all.22.outer_ref = f32[4,96,512]{2,1,0:T(8,128)S(1)} all-to-all(f32[4,96,512]{2,1,0:T(8,128)S(1)} %partial_sources.1), channel_id=1, replica_groups=mesh['y'=8,'zl'=8,'core'=2,'x'=4,'zh'=2] {'x'}, dimensions={0} | all-to-all | bytes 1572864 | tf_op jit(solution)/shard_map/all_to_all | solution.py:305
  74.1 0.0 copy-done.1
  74.1 1.6 %edges.1 = (f32[96,512]{1,0:T(8,128)S(1)}, f32[96,512]{1,0:T(8,128)S(1)}, f32[4,80,512]{2,1,0:T(8,128)}) custom-call(f32[2]{0:T(128)S(1)} %get-tuple-element.11.counts_ref, f32[2,5,16,512]{3,2,1,0:T(8,128)S(1)} %get-tuple-element.12.state_ref, f32[2,5,16,512]{3,2,1,0:T(8,128)S(1)} %collective-permute-done.other_ref, f32[16,512]{1,0:T(8,128)S(1)} %copy-done.1, ...), custom_call_target="tpu_custom_call" | custom-call | tf_op jit(solution)/shard_map/edges/pallas_call | solution.py:306
  75.7 4.9 %all-to-all-start.3 = ((f32[4,80,512]{2,1,0:T(8,128)}), f32[4,80,512]{2,1,0:T(8,128)S(1)}, u32[]{:S(2)}, u32[]{:S(2)}) async-start(f32[4,80,512]{2,1,0:T(8,128)} %get-tuple-element.14), calls=%async_computation.3 | async-start | bytes 1310720 | tf_op jit(solution)/shard_map/all_to_all | solution.py:315
  80.6 2.5 %collective-permute-start.1 = (f32[96,512]{1,0:T(8,128)S(1)}, f32[96,512]{1,0:T(8,128)S(1)}, u32[]{:S(2)}, u32[]{:S(2)}) collective-permute-start(f32[96,512]{1,0:T(8,128)S(1)} %get-tuple-element.15), channel_id=1, source_target_pairs={{8,16},{24,32},{40,48},{56,64},{72,80},{88,96},{104,112},{120,128}... | collective-permute-start | bytes 589832 | tf_op jit(solution)/shard_map/ppermute | solution.py:313
  83.1 2.8 %collective-permute-start.2 = (f32[96,512]{1,0:T(8,128)S(1)}, f32[96,512]{1,0:T(8,128)S(1)}, u32[]{:S(2)}, u32[]{:S(2)}) collective-permute-start(f32[96,512]{1,0:T(8,128)S(1)} %get-tuple-element.16), channel_id=1, source_target_pairs={{0,8},{8,0},{1,9},{9,1},{2,10},{10,2},{3,11},{11,3},{4,12},{12,4},... | collective-permute-start | bytes 589832 | tf_op jit(solution)/shard_map/ppermute | solution.py:314
  86.0 10.3 %collective-permute-done.1.far_ref = f32[96,512]{1,0:T(8,128)S(1)} collective-permute-done((f32[96,512]{1,0:T(8,128)S(1)}, f32[96,512]{1,0:T(8,128)S(1)}, u32[]{:S(2)}, u32[]{:S(2)}) %collective-permute-start.1) | collective-permute-done | bytes 196640 | tf_op jit(solution)/shard_map/ppermute | solution.py:313
  96.3 0.0 collective-permute-done.2.near_ref
  96.3 0.0 all-to-all-done.3.inner_ref
  96.3 4.3 %march.1 = f32[2,5,16,512]{3,2,1,0:T(8,128)} custom-call(f32[2]{0:T(128)S(1)} %get-tuple-element.11.counts_ref, f32[2,5,16,512]{3,2,1,0:T(8,128)S(1)} %get-tuple-element.12.state_ref, f32[16,512]{1,0:T(8,128)S(1)} %copy-done.1, f32[4,96,512]{2,1,0:T(8,128)S(1)} %all_to_all.22.outer_ref, f32[4,80,512]{2,1,0:T(8,128)S(1)} %all-to-all-done.3.inner_ref, ...), custom_call_target="tpu_custom_call" | custom-call | tf_op jit(solution)/shard_map/march/pallas_call | solution.py:316
  (1 shorter events, 0.0 us)
Async XLA Ops:
  0.0 57.6 %collective-permute-start = (f32[2,5,16,512]{3,2,1,0:T(8,128)}, f32[2,5,16,512]{3,2,1,0:T(8,128)S(1)}, u32[]{:S(2)}, u32[]{:S(2)}) collective-permute-start(f32[2,5,16,512]{3,2,1,0:T(8,128)} %state_ref.1), channel_id=1, source_target_pairs={{0,1},{1,0},{2,3},{3,2},{4,5},{5,4},{6,7},{7,6},{8,9},{9,8},{10,11... | collective-permute-start | bytes 983048 | tf_op jit(solution)/shard_map/ppermute | solution.py:287
  19.4 1.0 copy-start
  20.3 0.7 copy-start.2
  58.7 15.4 %copy-start.1 = (f32[16,512]{1,0:T(8,128)S(1)}, f32[16,512]{1,0:T(8,128)}, u32[]{:S(2)}) copy-start(f32[16,512]{1,0:T(8,128)} %wall_ref.3) | copy-start | bytes 98308
  75.7 20.6 %all-to-all-start.3 = ((f32[4,80,512]{2,1,0:T(8,128)}), f32[4,80,512]{2,1,0:T(8,128)S(1)}, u32[]{:S(2)}, u32[]{:S(2)}) async-start(f32[4,80,512]{2,1,0:T(8,128)} %get-tuple-element.14), calls=%async_computation.3 | async-start | bytes 1310720 | tf_op jit(solution)/shard_map/all_to_all | solution.py:315
  80.6 15.7 %collective-permute-start.1 = (f32[96,512]{1,0:T(8,128)S(1)}, f32[96,512]{1,0:T(8,128)S(1)}, u32[]{:S(2)}, u32[]{:S(2)}) collective-permute-start(f32[96,512]{1,0:T(8,128)S(1)} %get-tuple-element.15), channel_id=1, source_target_pairs={{8,16},{24,32},{40,48},{56,64},{72,80},{88,96},{104,112},{120,128}... | collective-permute-start | bytes 589832 | tf_op jit(solution)/shard_map/ppermute | solution.py:313
  83.1 13.1 %collective-permute-start.2 = (f32[96,512]{1,0:T(8,128)S(1)}, f32[96,512]{1,0:T(8,128)S(1)}, u32[]{:S(2)}, u32[]{:S(2)}) collective-permute-start(f32[96,512]{1,0:T(8,128)S(1)} %get-tuple-element.16), channel_id=1, source_target_pairs={{0,8},{8,0},{1,9},{9,1},{2,10},{10,2},{3,11},{11,3},{4,12},{12,4},... | collective-permute-start | bytes 589832 | tf_op jit(solution)/shard_map/ppermute | solution.py:314

commit v5 on v3

--- a/solution.py
+++ b/solution.py
@@ -50,11 +50,6 @@
             _, top = speed_sum_and_max(*(state_ref[n, v, rows, :] for v in range(4)))
             best = top if best is None else jnp.maximum(best, top)
     peak = jnp.max(best, axis=(0, 1), keepdims=True)
-    out_ref[...] = jnp.broadcast_to(peak[None], out_ref.shape)
-
-
-def fold_kernel(peaks_ref, out_ref):
-    peak = jnp.max(peaks_ref[...], axis=0)
     out_ref[...] = jnp.broadcast_to(peak[None], out_ref.shape)
 
 
@@ -125,7 +120,7 @@
         )
 
 
-def edge_kernel(state_ref, wall_ref, parts_ref, far_ref, near_ref):
+def edge_kernel(state_ref, wall_ref, parts_ref, far_ref, near_ref, peak_ref):
     place = lax.axis_index(CELLS)
     is_first = place == 0
     is_last = place == lax.axis_size(CELLS) - 1
@@ -156,6 +151,10 @@
             put(pl.ds(80 + at, 1), state_ref[n, v, 11:12, :], state_ref[n, v, 4:5, :])
     put(pl.ds(90, 4), wall_ref[12:16, :], wall_ref[0:4, :])
     put(pl.ds(94, 2), wall_ref[14:16, :], wall_ref[0:2, :])
+    peak = parts_ref[0, 170:171, 0:128]
+    for k in range(1, 4):
+        peak = jnp.maximum(peak, parts_ref[k, 170:171, 0:128])
+    peak_ref[...] = jnp.broadcast_to(peak[None], peak_ref.shape)
 
 
 def march_kernel(
@@ -165,6 +164,7 @@
     parts_ref,
     far_ref,
     near_ref,
+    peaks_ref,
     out_ref,
     start_ref,
     now_ref,
@@ -191,9 +191,8 @@
     def upper(rows):
         return jnp.where(is_even, near_ref[rows, :], far_ref[rows, :])
 
-    peak = parts_ref[0, 170:171, :]
-    for k in range(1, 4):
-        peak = jnp.maximum(peak, parts_ref[k, 170:171, :])
+    peak = jnp.max(peaks_ref[...], axis=0)
+    peak = jnp.concatenate([peak] * 4, axis=1)
     wave = jnp.broadcast_to(peak, (8, 512))
 
     walls = [
@@ -285,11 +284,6 @@
         compiler_params=PARAMS, name="peak",
     )(blade_counts, state)
     peaks = lax.all_to_all(peak, "y", 0, 0)
-    peak = pl.pallas_call(
-        fold_kernel, out_shape=field((32, 1, 128)), in_specs=[VMEM], out_specs=VMEM,
-        compiler_params=PARAMS, name="fold",
-    )(peaks)
-    peaks = lax.all_to_all(peak, ("zl", "zh", "core"), 0, 0)
     parts = pl.pallas_call(
         partial_kernel, out_shape=field((4, 176, 512)),
         in_specs=[SMEM, VMEM, VMEM, VMEM], out_specs=VMEM,
@@ -297,18 +291,19 @@
         compiler_params=PARAMS, name="partial_sources",
     )(counts, state, other, peaks)
     parts = lax.all_to_all(parts, "x", 0, 0)
-    far, near = pl.pallas_call(
-        edge_kernel, out_shape=(field((96, 512)), field((96, 512))),
-        in_specs=[VMEM] * 3, out_specs=(VMEM, VMEM),
+    far, near, peak = pl.pallas_call(
+        edge_kernel, out_shape=(field((96, 512)), field((96, 512)), field((32, 1, 128))),
+        in_specs=[VMEM] * 3, out_specs=(VMEM, VMEM, VMEM),
         compiler_params=PARAMS, name="edges",
     )(state, wall_distance, parts)
     count = lax.axis_size(CELLS)
     across = [((i + 1) % count, (i + 2) % count) for i in range(0, count, 2)]
     far = lax.ppermute(far, CELLS, across + [(j, i) for i, j in across])
     near = lax.ppermute(near, "core", [(0, 1), (1, 0)])
+    peaks = lax.all_to_all(peak, ("zl", "zh", "core"), 0, 0)
     return pl.pallas_call(
         march_kernel, out_shape=field(state.shape),
-        in_specs=[SMEM] + [VMEM] * 5, out_specs=VMEM,
+        in_specs=[SMEM] + [VMEM] * 6, out_specs=VMEM,
         scratch_shapes=[
             pltpu.VMEM((2, 5, 32, 512), f32),
             pltpu.VMEM((2, 5, 32, 512), f32),
@@ -320,7 +315,7 @@
             pltpu.VMEM((5, 48, 512), f32),
         ],
         compiler_params=PARAMS, name="march",
-    )(counts, state, wall_distance, parts, far, near)
+    )(counts, state, wall_distance, parts, far, near, peaks)
 
 
 def solution(mesh):

time: 103 us -> 107 us (1.039)
  the two profiles are of different devices: /device:TPU:32 before, /device:TPU:1 now
where the time goes in v5:
time: 107 us
  blocking collectives  56.8 us (53%)
  starting transfers between devices  41.4 us (39%)
  Pallas kernels  6.86 us (6%)
  local copies, waits for them, and re-layouts  1.64 us (2%)
    all_to_all x1, blocking collectives, local(): peaks = lax.all_to_all(peak, ('zl', 'zh', 'core'), 0, 0)  23.5 us
    all_to_all x1, blocking collectives, local(): parts = lax.all_to_all(parts, 'x', 0, 0)  20.2 us
    ppermute x1, starting transfers between devices, local(): other = lax.ppermute(state, 'zh', [(0, 1), (1, 0)])  19.9 us
    ppermute x1, starting transfers between devices, local(): far = lax.ppermute(far, CELLS, across + [(j, i) for i, j in across])  19.6 us
    all_to_all x1, blocking collectives, local(): peaks = lax.all_to_all(peak, 'y', 0, 0)  13.1 us
    pallas_call x1, Pallas kernels, local(): pl.pallas_call(march_kernel, out_shape=field(state.shape), in_specs=[SMEM...  4.4 us
  transfers between devices with their start and end apart: 3, of which 0 were waited for; matrix products, arithmetic and copies ran while one was open for 0% of the time, Pallas kernels for 1%

profile of v5, /device:TPU:1, one launch (start us, length us, event | category | flops | bytes accessed | tf_op | source)
XLA Modules:
  0.0 106.8 jit_solution(7306154244392429491)
XLA Ops:
  0.0 19.9 %collective-permute-start = (f32[2,5,16,512]{3,2,1,0:T(8,128)}, f32[2,5,16,512]{3,2,1,0:T(8,128)S(1)}, u32[]{:S(2)}, u32[]{:S(2)}) collective-permute-start(f32[2,5,16,512]{3,2,1,0:T(8,128)} %state_ref.1), channel_id=1, source_target_pairs={{0,1},{1,0},{2,3},{3,2},{4,5},{5,4},{6,7},{7,6},{8,9},{9,8},{10,11... | collective-permute-start | bytes 983048 | tf_op jit(solution)/shard_map/ppermute | solution.py:280
  19.9 0.0 copy-start
  19.9 1.0 copy-done
  20.9 0.0 copy-start.2
  20.9 0.7 copy-done.2
  21.5 1.2 %peak.1 = (f32[8,1,128]{2,1,0:T(1,128)S(1)}, f32[2]{0:T(128)S(1)}, f32[2,5,16,512]{3,2,1,0:T(8,128)S(1)}) custom-call(s32[2]{0:T(128)S(1)} %copy-done.2, f32[2,5,16,512]{3,2,1,0:T(8,128)S(1)} %copy-done), custom_call_target="tpu_custom_call" | custom-call | tf_op jit(solution)/shard_map/peak/pallas_call | solution.py:281
  22.7 13.1 %all_to_all.15.peaks_ref = f32[8,1,128]{2,1,0:T(1,128)S(1)} all-to-all(f32[8,1,128]{2,1,0:T(1,128)S(1)} %get-tuple-element.13), channel_id=1, replica_groups=mesh['y'=8,'zl'=8,'core'=2,'x'=4,'zh'=2] {'y'}, dimensions={0} | all-to-all | bytes 8192 | tf_op jit(solution)/shard_map/all_to_all | solution.py:286
  35.9 0.0 collective-permute-done.other_ref
  35.9 1.2 %partial_sources.1 = f32[4,176,512]{2,1,0:T(8,128)S(1)} custom-call(f32[2]{0:T(128)S(1)} %get-tuple-element.11.counts_ref, f32[2,5,16,512]{3,2,1,0:T(8,128)S(1)} %get-tuple-element.12.state_ref, f32[2,5,16,512]{3,2,1,0:T(8,128)S(1)} %collective-permute-done.other_ref, f32[8,1,128]{2,1,0:T(1,128)S(1)} %all_to_all.15.peaks_ref), custom_call_target="tpu_custom_call" | custom-call | tf_op jit(solution)/shard_map/partial_sources/pallas_call | solution.py:287
  37.0 0.0 copy-start.1
  37.1 20.2 %all_to_all.16.parts_ref = f32[4,176,512]{2,1,0:T(8,128)S(1)} all-to-all(f32[4,176,512]{2,1,0:T(8,128)S(1)} %partial_sources.1), channel_id=1, replica_groups=mesh['y'=8,'zl'=8,'core'=2,'x'=4,'zh'=2] {'x'}, dimensions={0} | all-to-all | bytes 2883584 | tf_op jit(solution)/shard_map/all_to_all | solution.py:293
  57.3 0.0 copy-done.1
  57.3 0.1 edges.1
  57.4 19.6 %collective-permute-start.1 = (f32[96,512]{1,0:T(8,128)S(1)}, f32[96,512]{1,0:T(8,128)S(1)}, u32[]{:S(2)}, u32[]{:S(2)}) collective-permute-start(f32[96,512]{1,0:T(8,128)S(1)} %get-tuple-element.14), channel_id=1, source_target_pairs={{8,16},{24,32},{40,48},{56,64},{72,80},{88,96},{104,112},{120,128}... | collective-permute-start | bytes 589832 | tf_op jit(solution)/shard_map/ppermute | solution.py:301
  77.0 1.9 %collective-permute-start.2 = (f32[96,512]{1,0:T(8,128)S(1)}, f32[96,512]{1,0:T(8,128)S(1)}, u32[]{:S(2)}, u32[]{:S(2)}) collective-permute-start(f32[96,512]{1,0:T(8,128)S(1)} %get-tuple-element.15), channel_id=1, source_target_pairs={{0,8},{8,0},{1,9},{9,1},{2,10},{10,2},{3,11},{11,3},{4,12},{12,4},... | collective-permute-start | bytes 589832 | tf_op jit(solution)/shard_map/ppermute | solution.py:302
  78.9 23.5 %all_to_all.17.peaks_ref = f32[32,1,128]{2,1,0:T(1,128)S(1)} all-to-all(f32[32,1,128]{2,1,0:T(1,128)S(1)} %get-tuple-element.16), channel_id=1, replica_groups=mesh['y'=8,'zl'=8,'core'=2,'x'=4,'zh'=2] {'zl','zh','core'}, dimensions={0} | all-to-all | bytes 32768 | tf_op jit(solution)/shard_map/all_to_all | solution.py:303
  102.4 0.0 collective-permute-done.1.far_ref
  102.4 0.0 collective-permute-done.2.near_ref
  102.4 4.4 %march.1 = f32[2,5,16,512]{3,2,1,0:T(8,128)} custom-call(f32[2]{0:T(128)S(1)} %get-tuple-element.11.counts_ref, f32[2,5,16,512]{3,2,1,0:T(8,128)S(1)} %get-tuple-element.12.state_ref, f32[16,512]{1,0:T(8,128)S(1)} %copy-done.1, f32[4,176,512]{2,1,0:T(8,128)S(1)} %all_to_all.16.parts_ref, f32[96,512]{1,0:T(8,128)S(1)} %collective-permute-done.1.far_ref, ...), custom_call_target="tpu_custom_call" | custom-call | tf_op jit(solution)/shard_map/march/pallas_call | solution.py:304
Async XLA Ops:
  0.0 35.9 %collective-permute-start = (f32[2,5,16,512]{3,2,1,0:T(8,128)}, f32[2,5,16,512]{3,2,1,0:T(8,128)S(1)}, u32[]{:S(2)}, u32[]{:S(2)}) collective-permute-start(f32[2,5,16,512]{3,2,1,0:T(8,128)} %state_ref.1), channel_id=1, source_target_pairs={{0,1},{1,0},{2,3},{3,2},{4,5},{5,4},{6,7},{7,6},{8,9},{9,8},{10,11... | collective-permute-start | bytes 983048 | tf_op jit(solution)/shard_map/ppermute | solution.py:280
  19.9 1.0 copy-start
  20.9 0.7 copy-start.2
  37.0 20.2 %copy-start.1 = (f32[16,512]{1,0:T(8,128)S(1)}, f32[16,512]{1,0:T(8,128)}, u32[]{:S(2)}) copy-start(f32[16,512]{1,0:T(8,128)} %wall_ref.3) | copy-start | bytes 98308
  57.4 45.1 %collective-permute-start.1 = (f32[96,512]{1,0:T(8,128)S(1)}, f32[96,512]{1,0:T(8,128)S(1)}, u32[]{:S(2)}, u32[]{:S(2)}) collective-permute-start(f32[96,512]{1,0:T(8,128)S(1)} %get-tuple-element.14), channel_id=1, source_target_pairs={{8,16},{24,32},{40,48},{56,64},{72,80},{88,96},{104,112},{120,128}... | collective-permute-start | bytes 589832 | tf_op jit(solution)/shard_map/ppermute | solution.py:301
  77.0 25.4 %collective-permute-start.2 = (f32[96,512]{1,0:T(8,128)S(1)}, f32[96,512]{1,0:T(8,128)S(1)}, u32[]{:S(2)}, u32[]{:S(2)}) collective-permute-start(f32[96,512]{1,0:T(8,128)S(1)} %get-tuple-element.15), channel_id=1, source_target_pairs={{0,8},{8,0},{1,9},{9,1},{2,10},{10,2},{3,11},{11,3},{4,12},{12,4},... | collective-permute-start | bytes 589832 | tf_op jit(solution)/shard_map/ppermute | solution.py:302

commit v6 on v4

--- a/solution.py
+++ b/solution.py
@@ -1,4 +1,3 @@
-import functools
 import math
 
 import jax
@@ -39,18 +38,30 @@
     return ax + ay + 2.0 * c, jnp.maximum(ax, ay) + c
 
 
-def peak_kernel(whole_ref, state_ref, out_ref, counts_ref, held_ref):
-    held_ref[...] = state_ref[...]
+def prepare_kernel(whole_ref, state_ref, outer_ref, inner_ref, blocks_ref, counts_ref):
     for k in range(2):
         counts_ref[k] = whole_ref[k].astype(jnp.float32)
+    row = lax.broadcasted_iota(jnp.int32, (8, 512), 0)
+    for n in range(2):
+        for v in range(5):
+            first = state_ref[n, v, 0:8, :]
+            second = state_ref[n, v, 8:16, :]
+            rows = pl.ds((n * 5 + v) * 8, 8)
+            outer = jnp.where(row < 4, first, second)
+            outer_ref[rows, :] = outer
+            inner_ref[rows, :] = jnp.where(row < 4, second, first)
+            for k in range(4):
+                blocks_ref[k, rows, :] = outer[:, 128 * k : 128 * k + 128]
+
+
+def peak_kernel(mine_ref, inside_ref, _, peak_ref):
     best = None
-    for n in range(2):
-        for t in range(2):
-            rows = pl.ds(8 * t, 8)
-            _, top = speed_sum_and_max(*(state_ref[n, v, rows, :] for v in range(4)))
+    for ref in (mine_ref, inside_ref):
+        for n in range(2):
+            _, top = speed_sum_and_max(*(ref[pl.ds((n * 5 + v) * 8, 8), :] for v in range(4)))
             best = top if best is None else jnp.maximum(best, top)
     peak = jnp.max(best, axis=(0, 1), keepdims=True)
-    out_ref[...] = jnp.broadcast_to(peak[None], out_ref.shape)
+    peak_ref[...] = jnp.broadcast_to(peak[None], peak_ref.shape)
 
 
 def fold_kernel(peaks_ref, out_ref):
@@ -58,16 +69,13 @@
     out_ref[...] = jnp.broadcast_to(peak[None], out_ref.shape)
 
 
-def add_partials(counts_ref, state_ref, other_ref, out_ref, edge):
+def add_partials(counts_ref, mine_ref, other_ref, out_ref):
     me_x = lax.axis_index("x")
     upper_half = lax.axis_index("zh")
     omega = omega_of(counts_ref)
-    row = lax.broadcasted_iota(jnp.int32, (8, 512), 0)
     for v in range(5):
         fields = [
-            jnp.where((row < 4) == edge, ref[m, v, 0:8, :], ref[m, v, 8:16, :])
-            for ref in (state_ref, other_ref)
-            for m in range(2)
+            ref[pl.ds((m * 5 + v) * 8, 8), :] for ref in (mine_ref, other_ref) for m in range(2)
         ]
         for step in range(4):
             target = lax.rem(me_x + step, 4)
@@ -88,12 +96,11 @@
     return apart % NT, (apart + 2) % NT, (apart - 2) % NT
 
 
-def partial_kernel(counts_ref, state_ref, other_ref, peaks_ref, out_ref, lag_ref):
-    me_x = lax.axis_index("x")
+def outer_kernel(counts_ref, ours_ref, theirs_ref, peaks_ref, _, out_ref, lag_ref):
     upper_half = lax.axis_index("zh")
     place = lax.axis_index(CELLS)
     is_last = place == lax.axis_size(CELLS) - 1
-    add_partials(counts_ref, state_ref, other_ref, out_ref, True)
+    omega = omega_of(counts_ref)
     ratio = jnp.full((NT, 128), counts_ref[1]) / jnp.full((NT, 128), counts_ref[0])
     sigma = 2.0 * math.pi * ratio
     shift = jnp.where(is_last, sigma, -sigma)
@@ -105,29 +112,38 @@
     lag_ref[...] = jnp.broadcast_to(
         jnp.sum(terms, axis=1, keepdims=True) * (1.0 / NT), lag_ref.shape
     )
-
-    def lag(j):
-        return jnp.concatenate([lag_ref[j : j + 1, :]] * 4, axis=1)
-
-    peak = jnp.max(peaks_ref[...], axis=0)
-    peak = jnp.broadcast_to(jnp.concatenate([peak] * 4, axis=1), (6, 512))
-    for step in range(4):
-        target = lax.rem(me_x + step, 4)
-        for n in range(2):
-            factor = []
-            for m in range(4):
-                own, high, low = offsets(step, n, m)
-                factor.append(
-                    lag(own) if m < 2 else jnp.where(upper_half == 1, lag(high), lag(low))
-                )
-            for v in range(5):
-                total = None
-                for m, ref in enumerate((state_ref, state_ref, other_ref, other_ref)):
-                    edge = jnp.where(is_last, ref[m % 2, v, 15:16, :], ref[m % 2, v, 0:1, :])
-                    term = factor[m] * edge
-                    total = term if total is None else total + term
-                out_ref[target, pl.ds(80 + n * 5 + v, 1), :] = total
-        out_ref[target, pl.ds(90, 6), :] = peak
+    slopes, lags = [], []
+    for j in range(NT):
+        high, low = (j + 2) % NT, (j - 2) % NT
+        across = jnp.where(upper_half == 1, SLOPE[high], SLOPE[low])
+        slopes.append((omega * SLOPE[j], omega * across))
+        high, low = lag_ref[high : high + 1, :], lag_ref[low : low + 1, :]
+        lags.append((lag_ref[j : j + 1, :], jnp.where(upper_half == 1, high, low)))
+    peak = jnp.broadcast_to(jnp.max(peaks_ref[...], axis=0), (6, 128))
+    for v in range(5):
+        sums = [None] * 8
+        rims = [None] * 8
+        for half, ref in enumerate((ours_ref, theirs_ref)):
+            for m in range(8):
+                at = ((m % 2) * 5 + v) * 8
+                field = ref[m // 2, pl.ds(at, 8), :]
+                rim = jnp.where(is_last, field[7:8, :], field[0:1, :])
+                for n in range(8):
+                    apart = (4 * (n // 2 - m // 2) + n % 2 - m % 2) % NT
+                    term = slopes[apart][half] * field
+                    sums[n] = term if sums[n] is None else sums[n] + term
+                    term = lags[apart][half] * rim
+                    rims[n] = term if rims[n] is None else rims[n] + term
+        for n in range(8):
+            at = (n % 2) * 5 + v
+            out_ref[n // 2, pl.ds(at * 8, 8), :] = sums[n]
+            out_ref[n // 2, pl.ds(80 + at, 1), :] = rims[n]
+    for k in range(4):
+        out_ref[k, pl.ds(90, 6), :] = peak
+
+
+def joined(blocks_ref, start, count):
+    return jnp.concatenate([blocks_ref[k, pl.ds(start, count), :] for k in range(4)], axis=1)
 
 
 def added(parts_ref, start, count):
@@ -137,7 +153,11 @@
     )
 
 
-def edge_kernel(counts_ref, state_ref, other_ref, wall_ref, outer_ref, far_ref, near_ref, inner_ref):
+def edge_kernel(
+    counts_ref, mine_ref, inside_ref, other_ref, wall_ref, outer_ref,
+    far_ref, near_ref, inner_ref,
+):
+    add_partials(counts_ref, inside_ref, other_ref, inner_ref)
     place = lax.axis_index(CELLS)
     is_first = place == 0
     is_last = place == lax.axis_size(CELLS) - 1
@@ -151,22 +171,27 @@
     for n in range(2):
         for v in range(5):
             at = n * 5 + v
-            lagged = jnp.broadcast_to(added(outer_ref, 80 + at, 1), (8, 512))
-            source = pltpu.roll(added(outer_ref, at * 8, 8), 4, axis=0)
-            up = jnp.where(row >= 4, state_ref[n, v, 8:16, :], source)
+            lagged = jnp.broadcast_to(joined(outer_ref, 80 + at, 1), (8, 512))
+            source = pltpu.roll(joined(outer_ref, at * 8, 8), 4, axis=0)
+            mine = mine_ref[pl.ds(at * 8, 8), :]
+            up = jnp.where(row >= 4, mine, source)
             up = jnp.where(is_last & (row == 7), lagged, up)
-            down = jnp.where(row < 4, state_ref[n, v, 0:8, :], source)
+            down = jnp.where(row < 4, mine, source)
             down = jnp.where(is_first & (row == 0), lagged, down)
             put(pl.ds(at * 8, 8), up, down)
-            put(pl.ds(80 + at, 1), state_ref[n, v, 11:12, :], state_ref[n, v, 4:5, :])
+            put(
+                pl.ds(80 + at, 1),
+                inside_ref[pl.ds(at * 8 + 3, 1), :],
+                inside_ref[pl.ds(at * 8 + 4, 1), :],
+            )
     put(pl.ds(90, 4), wall_ref[12:16, :], wall_ref[0:4, :])
     put(pl.ds(94, 2), wall_ref[14:16, :], wall_ref[0:2, :])
-    add_partials(counts_ref, state_ref, other_ref, inner_ref, False)
 
 
 def march_kernel(
     counts_ref,
-    state_ref,
+    mine_ref,
+    inside_ref,
     wall_ref,
     outer_ref,
     inner_ref,
@@ -201,6 +226,7 @@
     peak = outer_ref[0, 90:91, :]
     for k in range(1, 4):
         peak = jnp.maximum(peak, outer_ref[k, 90:91, :])
+    peak = jnp.concatenate([peak] * 4, axis=1)
     wave = jnp.broadcast_to(peak, (8, 512))
 
     walls = [
@@ -222,8 +248,11 @@
             fifth = jnp.broadcast_to(upper(pl.ds(80 + at, 1)), (8, 512))
             start_ref[n, v, 24:32, :] = jnp.where(row < 4, packed, fifth)
             source_ref[n, v, 24:32, :] = 2.0 * pltpu.roll(packed, 4, axis=0)
-            start_ref[n, v, 8:24, :] = state_ref[n, v, :, :]
-            outer = 2.0 * added(outer_ref, at * 8, 8)
+            mine = mine_ref[pl.ds(at * 8, 8), :]
+            inside = inside_ref[pl.ds(at * 8, 8), :]
+            start_ref[n, v, 8:16, :] = jnp.where(row < 4, mine, inside)
+            start_ref[n, v, 16:24, :] = jnp.where(row < 4, inside, mine)
+            outer = 2.0 * joined(outer_ref, at * 8, 8)
             inner = 2.0 * added(inner_ref, at * 8, 8)
             source_ref[n, v, 8:16, :] = jnp.where(row < 4, outer, inner)
             source_ref[n, v, 16:24, :] = jnp.where(row < 4, inner, outer)
@@ -281,53 +310,53 @@
                     now_ref[n, v, rows, :] = after
 
 
+def call(kernel, name, shapes, spaces, *operands, scratch=()):
+    f32 = jnp.float32
+    out_shape = [jax.ShapeDtypeStruct(shape, f32) for shape in shapes]
+    return pl.pallas_call(
+        kernel, out_shape=out_shape, name=name, compiler_params=PARAMS,
+        in_specs=[SMEM if x.shape == (2,) else VMEM for x in operands], out_specs=spaces,
+        scratch_shapes=[pltpu.VMEM(shape, f32) for shape in scratch],
+    )(*operands)
+
+
 def local(state, wall_distance, blade_counts):
-    f32 = jnp.float32
-    field = functools.partial(jax.ShapeDtypeStruct, dtype=f32)
-    other = lax.ppermute(state, "zh", [(0, 1), (1, 0)])
-    peak, counts, state = pl.pallas_call(
-        peak_kernel, out_shape=(field((8, 1, 128)), field((2,)), field(state.shape)),
-        in_specs=[SMEM, VMEM], out_specs=(VMEM, SMEM, VMEM),
-        compiler_params=PARAMS, name="peak",
-    )(blade_counts, state)
+    swap = [(0, 1), (1, 0)]
+    half = (80, 512)
+    mine, inside, blocks, counts = call(
+        prepare_kernel, "prepare", [half, half, (4, 80, 128), (2,)], [VMEM] * 3 + [SMEM],
+        blade_counts, state,
+    )
+    other_inside = lax.ppermute(inside, "zh", swap)
+    ours = lax.all_to_all(blocks, "x", 0, 0)
+    theirs = lax.ppermute(ours, "zh", swap)
+    (peak,) = call(peak_kernel, "peak", [(8, 1, 128)], [VMEM], mine, inside, ours)
     peaks = lax.all_to_all(peak, "y", 0, 0)
-    peak = pl.pallas_call(
-        fold_kernel, out_shape=field((32, 1, 128)), in_specs=[VMEM], out_specs=VMEM,
-        compiler_params=PARAMS, name="fold",
-    )(peaks)
+    (peak,) = call(fold_kernel, "fold", [(32, 1, 128)], [VMEM], peaks)
     peaks = lax.all_to_all(peak, ("zl", "zh", "core"), 0, 0)
-    outer = pl.pallas_call(
-        partial_kernel, out_shape=field((4, 96, 512)),
-        in_specs=[SMEM, VMEM, VMEM, VMEM], out_specs=VMEM,
-        scratch_shapes=[pltpu.VMEM((NT, 128), f32)],
-        compiler_params=PARAMS, name="partial_sources",
-    )(counts, state, other, peaks)
+    (outer,) = call(
+        outer_kernel, "outer_sources", [(4, 96, 128)], [VMEM],
+        counts, ours, theirs, peaks, other_inside, scratch=[(NT, 128)],
+    )
     outer = lax.all_to_all(outer, "x", 0, 0)
-    far, near, inner = pl.pallas_call(
-        edge_kernel, out_shape=(field((96, 512)), field((96, 512)), field((4, 80, 512))),
-        in_specs=[SMEM] + [VMEM] * 4, out_specs=(VMEM, VMEM, VMEM),
-        compiler_params=PARAMS, name="edges",
-    )(counts, state, other, wall_distance, outer)
+    far, near, inner = call(
+        edge_kernel, "edges", [(96, 512), (96, 512), (4, 80, 512)], [VMEM] * 3,
+        counts, mine, inside, other_inside, wall_distance, outer,
+    )
     count = lax.axis_size(CELLS)
     across = [((i + 1) % count, (i + 2) % count) for i in range(0, count, 2)]
     far = lax.ppermute(far, CELLS, across + [(j, i) for i, j in across])
-    near = lax.ppermute(near, "core", [(0, 1), (1, 0)])
+    near = lax.ppermute(near, "core", swap)
     inner = lax.all_to_all(inner, "x", 0, 0)
-    return pl.pallas_call(
-        march_kernel, out_shape=field(state.shape),
-        in_specs=[SMEM] + [VMEM] * 6, out_specs=VMEM,
-        scratch_shapes=[
-            pltpu.VMEM((2, 5, 32, 512), f32),
-            pltpu.VMEM((2, 5, 32, 512), f32),
-            pltpu.VMEM((2, 5, 32, 512), f32),
-            pltpu.VMEM((2, 32, 512), f32),
-            pltpu.VMEM((32, 512), f32),
-            pltpu.VMEM((5, 32, 512), f32),
-            pltpu.VMEM((5, 48, 512), f32),
-            pltpu.VMEM((5, 48, 512), f32),
+    (change,) = call(
+        march_kernel, "march", [state.shape], [VMEM],
+        counts, mine, inside, wall_distance, outer, inner, far, near,
+        scratch=[
+            (2, 5, 32, 512), (2, 5, 32, 512), (2, 5, 32, 512), (2, 32, 512), (32, 512),
+            (5, 32, 512), (5, 48, 512), (5, 48, 512),
         ],
-        compiler_params=PARAMS, name="march",
-    )(counts, state, wall_distance, outer, inner, far, near)
+    )
+    return change
 
 
 def solution(mesh):

time: 101 us -> 106 us (1.050)
  the two profiles are of different devices: /device:TPU:34 before, /device:TPU:2 now
where the time goes in v6:
time: 106 us
  starting transfers between devices  50.2 us (47%)
  waiting for transfers between devices  23.1 us (22%)
  blocking collectives  21.9 us (21%)
  Pallas kernels  8.9 us (8%)
  local copies, waits for them, and re-layouts  1.63 us (2%)
    all_to_all x1, starting transfers between devices, local(): ours = lax.all_to_all(blocks, 'x', 0, 0)  16.5 us
    all_to_all x1, blocking collectives, local(): peaks = lax.all_to_all(peak, 'y', 0, 0)  12.4 us
    all_to_all x1, waiting for transfers between devices, local(): peaks = lax.all_to_all(peak, ('zl', 'zh', 'core'), 0, 0)  12.1 us
    ppermute x1, waiting for transfers between devices, local(): far = lax.ppermute(far, CELLS, across + [(j, i) for i, j in across])  11.1 us
    all_to_all x1, starting transfers between devices, local(): peaks = lax.all_to_all(peak, ('zl', 'zh', 'core'), 0, 0)  9.67 us
    all_to_all x1, blocking collectives, local(): outer = lax.all_to_all(outer, 'x', 0, 0)  9.47 us
    pallas_call x6, Pallas kernels, call(): pl.pallas_call(kernel, out_shape=out_shape, name=name, compiler_params=PA...  8.9 us
    ppermute x1, starting transfers between devices, local(): other_inside = lax.ppermute(inside, 'zh', swap)  7.68 us
  transfers between devices with their start and end apart: 7, of which 2 were waited for; matrix products, arithmetic and copies ran while one was open for 0% of the time, Pallas kernels for 1%

profile of v6, /device:TPU:2, one launch (start us, length us, event | category | flops | bytes accessed | tf_op | source)
XLA Modules:
  0.0 105.9 jit_solution(12511588169522030722)
XLA Ops:
  0.0 0.0 copy-start
  0.0 1.0 copy-done
  1.0 0.0 copy-start.2
  1.0 0.7 copy-done.2
  1.6 1.2 %prepare.1 = (f32[80,512]{1,0:T(8,128)S(1)}, f32[80,512]{1,0:T(8,128)S(1)}, f32[4,80,128]{2,1,0:T(8,128)}, f32[2]{0:T(128)S(1)}) custom-call(s32[2]{0:T(128)S(1)} %copy-done.2, f32[2,5,16,512]{3,2,1,0:T(8,128)S(1)} %copy-done), custom_call_target="tpu_custom_call" | custom-call | tf_op jit(solution)/shard_map/prepare/pallas_call | solution.py:316
  2.9 16.5 %all-to-all-start = ((f32[4,80,128]{2,1,0:T(8,128)}), f32[4,80,128]{2,1,0:T(8,128)S(1)}, u32[]{:S(2)}, u32[]{:S(2)}) async-start(f32[4,80,128]{2,1,0:T(8,128)} %get-tuple-element.15), calls=%async_computation | async-start | bytes 327680 | tf_op jit(solution)/shard_map/all_to_all | solution.py:331
  19.4 7.7 %collective-permute-start.1 = (f32[80,512]{1,0:T(8,128)S(1)}, f32[80,512]{1,0:T(8,128)S(1)}, u32[]{:S(2)}, u32[]{:S(2)}) collective-permute-start(f32[80,512]{1,0:T(8,128)S(1)} %get-tuple-element.14.inside_ref), channel_id=1, source_target_pairs={{0,1},{1,0},{2,3},{3,2},{4,5},{5,4},{6,7},{7,6},{8,9},{9,8},{10,11... | collective-permute-start | bytes 491528 | tf_op jit(solution)/shard_map/ppermute | solution.py:330
  27.1 0.0 all-to-all-done._.ours_ref
  27.1 6.9 %collective-permute-start = (f32[4,80,128]{2,1,0:T(8,128)S(1)}, f32[4,80,128]{2,1,0:T(8,128)S(1)}, u32[]{:S(2)}, u32[]{:S(2)}) collective-permute-start(f32[4,80,128]{2,1,0:T(8,128)S(1)} %all-to-all-done._.ours_ref), channel_id=1, source_target_pairs={{0,1},{1,0},{2,3},{3,2},{4,5},{5,4},{6,7},{7,6},{8,9},{9,8},{10,11... | collective-permute-start | bytes 491528 | tf_op jit(solution)/shard_map/ppermute | solution.py:332
  34.0 0.2 peak.1
  34.2 12.4 %all_to_all.25.peaks_ref = f32[8,1,128]{2,1,0:T(1,128)S(1)} all-to-all(f32[8,1,128]{2,1,0:T(1,128)S(1)} %peak.1), channel_id=1, replica_groups=mesh['y'=8,'zl'=8,'core'=2,'x'=4,'zh'=2] {'y'}, dimensions={0} | all-to-all | bytes 8192 | tf_op jit(solution)/shard_map/all_to_all | solution.py:334
  46.5 0.6 fold.1
  47.2 9.7 %all-to-all-start.2 = ((f32[32,1,128]{2,1,0:T(1,128)}), f32[32,1,128]{2,1,0:T(1,128)S(1)}, u32[]{:S(2)}, u32[]{:S(2)}) async-start(f32[32,1,128]{2,1,0:T(1,128)} %fold.1), calls=%async_computation.2 | async-start | bytes 32768 | tf_op jit(solution)/shard_map/all_to_all | solution.py:336
  56.8 0.0 collective-permute-done.1._.other_ref
  56.8 12.1 %all-to-all-done.2.peaks_ref = f32[32,1,128]{2,1,0:T(1,128)S(1)} async-done(((f32[32,1,128]{2,1,0:T(1,128)}), f32[32,1,128]{2,1,0:T(1,128)S(1)}, u32[]{:S(2)}, u32[]{:S(2)}) %all-to-all-start.2) | async-done | bytes 16416 | tf_op jit(solution)/shard_map/all_to_all | solution.py:336
  68.9 0.0 collective-permute-done.theirs_ref
  68.9 1.0 outer_sources.1
  69.9 0.0 copy-start.1
  69.9 9.5 %all_to_all.26.outer_ref = f32[4,96,128]{2,1,0:T(8,128)S(1)} all-to-all(f32[4,96,128]{2,1,0:T(8,128)S(1)} %outer_sources.1), channel_id=1, replica_groups=mesh['y'=8,'zl'=8,'core'=2,'x'=4,'zh'=2] {'x'}, dimensions={0} | all-to-all | bytes 393216 | tf_op jit(solution)/shard_map/all_to_all | solution.py:341
  79.4 0.0 copy-done.1
  79.4 1.6 %edges.1 = (f32[96,512]{1,0:T(8,128)S(1)}, f32[96,512]{1,0:T(8,128)S(1)}, f32[4,80,512]{2,1,0:T(8,128)}) custom-call(f32[2]{0:T(128)S(1)} %get-tuple-element.12.counts_ref, f32[80,512]{1,0:T(8,128)S(1)} %get-tuple-element.13.mine_ref, f32[80,512]{1,0:T(8,128)S(1)} %get-tuple-element.14.inside_ref, f32[80,512]{1,0:T(8,128)S(1)} %collective-permute-done.1._.other_ref, ...), custom_call_target="tpu_custom_call" | custom-call | tf_op jit(solution)/shard_map/edges/pallas_call | solution.py:316
  81.0 4.9 %all-to-all-start.4 = ((f32[4,80,512]{2,1,0:T(8,128)}), f32[4,80,512]{2,1,0:T(8,128)S(1)}, u32[]{:S(2)}, u32[]{:S(2)}) async-start(f32[4,80,512]{2,1,0:T(8,128)} %get-tuple-element.16), calls=%async_computation.4 | async-start | bytes 1310720 | tf_op jit(solution)/shard_map/all_to_all | solution.py:350
  85.9 1.9 %collective-permute-start.2 = (f32[96,512]{1,0:T(8,128)S(1)}, f32[96,512]{1,0:T(8,128)S(1)}, u32[]{:S(2)}, u32[]{:S(2)}) collective-permute-start(f32[96,512]{1,0:T(8,128)S(1)} %get-tuple-element.17), channel_id=1, source_target_pairs={{8,16},{24,32},{40,48},{56,64},{72,80},{88,96},{104,112},{120,128}... | collective-permute-start | bytes 589832 | tf_op jit(solution)/shard_map/ppermute | solution.py:348
  87.8 2.7 %collective-permute-start.3 = (f32[96,512]{1,0:T(8,128)S(1)}, f32[96,512]{1,0:T(8,128)S(1)}, u32[]{:S(2)}, u32[]{:S(2)}) collective-permute-start(f32[96,512]{1,0:T(8,128)S(1)} %get-tuple-element.18), channel_id=1, source_target_pairs={{0,8},{8,0},{1,9},{9,1},{2,10},{10,2},{3,11},{11,3},{4,12},{12,4},... | collective-permute-start | bytes 589832 | tf_op jit(solution)/shard_map/ppermute | solution.py:349
  90.5 11.1 %collective-permute-done.2.far_ref = f32[96,512]{1,0:T(8,128)S(1)} collective-permute-done((f32[96,512]{1,0:T(8,128)S(1)}, f32[96,512]{1,0:T(8,128)S(1)}, u32[]{:S(2)}, u32[]{:S(2)}) %collective-permute-start.2) | collective-permute-done | bytes 196640 | tf_op jit(solution)/shard_map/ppermute | solution.py:348
  101.6 0.0 collective-permute-done.3.near_ref
  101.6 0.0 all-to-all-done.4.inner_ref
  101.6 4.3 %march.1 = f32[2,5,16,512]{3,2,1,0:T(8,128)} custom-call(f32[2]{0:T(128)S(1)} %get-tuple-element.12.counts_ref, f32[80,512]{1,0:T(8,128)S(1)} %get-tuple-element.13.mine_ref, f32[80,512]{1,0:T(8,128)S(1)} %get-tuple-element.14.inside_ref, f32[16,512]{1,0:T(8,128)S(1)} %copy-done.1, f32[4,96,128]{2,1,0:T(8,128)S(1)} %all_to_all.26.outer_ref, ...), custom_call_target="tpu_custom_call" | custom-call | tf_op jit(solution)/shard_map/march/pallas_call | solution.py:316
Async XLA Ops:
  0.0 1.0 copy-start
  1.0 0.7 copy-start.2
  2.9 24.2 %all-to-all-start = ((f32[4,80,128]{2,1,0:T(8,128)}), f32[4,80,128]{2,1,0:T(8,128)S(1)}, u32[]{:S(2)}, u32[]{:S(2)}) async-start(f32[4,80,128]{2,1,0:T(8,128)} %get-tuple-element.15), calls=%async_computation | async-start | bytes 327680 | tf_op jit(solution)/shard_map/all_to_all | solution.py:331
  19.4 37.4 %collective-permute-start.1 = (f32[80,512]{1,0:T(8,128)S(1)}, f32[80,512]{1,0:T(8,128)S(1)}, u32[]{:S(2)}, u32[]{:S(2)}) collective-permute-start(f32[80,512]{1,0:T(8,128)S(1)} %get-tuple-element.14.inside_ref), channel_id=1, source_target_pairs={{0,1},{1,0},{2,3},{3,2},{4,5},{5,4},{6,7},{7,6},{8,9},{9,8},{10,11... | collective-permute-start | bytes 491528 | tf_op jit(solution)/shard_map/ppermute | solution.py:330
  27.1 41.8 %collective-permute-start = (f32[4,80,128]{2,1,0:T(8,128)S(1)}, f32[4,80,128]{2,1,0:T(8,128)S(1)}, u32[]{:S(2)}, u32[]{:S(2)}) collective-permute-start(f32[4,80,128]{2,1,0:T(8,128)S(1)} %all-to-all-done._.ours_ref), channel_id=1, source_target_pairs={{0,1},{1,0},{2,3},{3,2},{4,5},{5,4},{6,7},{7,6},{8,9},{9,8},{10,11... | collective-permute-start | bytes 491528 | tf_op jit(solution)/shard_map/ppermute | solution.py:332
  47.2 21.8 %all-to-all-start.2 = ((f32[32,1,128]{2,1,0:T(1,128)}), f32[32,1,128]{2,1,0:T(1,128)S(1)}, u32[]{:S(2)}, u32[]{:S(2)}) async-start(f32[32,1,128]{2,1,0:T(1,128)} %fold.1), calls=%async_computation.2 | async-start | bytes 32768 | tf_op jit(solution)/shard_map/all_to_all | solution.py:336
  69.9 9.5 %copy-start.1 = (f32[16,512]{1,0:T(8,128)S(1)}, f32[16,512]{1,0:T(8,128)}, u32[]{:S(2)}) copy-start(f32[16,512]{1,0:T(8,128)} %wall_ref.3) | copy-start | bytes 98308
  81.0 20.6 %all-to-all-start.4 = ((f32[4,80,512]{2,1,0:T(8,128)}), f32[4,80,512]{2,1,0:T(8,128)S(1)}, u32[]{:S(2)}, u32[]{:S(2)}) async-start(f32[4,80,512]{2,1,0:T(8,128)} %get-tuple-element.16), calls=%async_computation.4 | async-start | bytes 1310720 | tf_op jit(solution)/shard_map/all_to_all | solution.py:350
  85.9 15.7 %collective-permute-start.2 = (f32[96,512]{1,0:T(8,128)S(1)}, f32[96,512]{1,0:T(8,128)S(1)}, u32[]{:S(2)}, u32[]{:S(2)}) collective-permute-start(f32[96,512]{1,0:T(8,128)S(1)} %get-tuple-element.17), channel_id=1, source_target_pairs={{8,16},{24,32},{40,48},{56,64},{72,80},{88,96},{104,112},{120,128}... | collective-permute-start | bytes 589832 | tf_op jit(solution)/shard_map/ppermute | solution.py:348
  87.8 13.8 %collective-permute-start.3 = (f32[96,512]{1,0:T(8,128)S(1)}, f32[96,512]{1,0:T(8,128)S(1)}, u32[]{:S(2)}, u32[]{:S(2)}) collective-permute-start(f32[96,512]{1,0:T(8,128)S(1)} %get-tuple-element.18), channel_id=1, source_target_pairs={{0,8},{8,0},{1,9},{9,1},{2,10},{10,2},{3,11},{11,3},{4,12},{12,4},... | collective-permute-start | bytes 589832 | tf_op jit(solution)/shard_map/ppermute | solution.py:349

commit v7 on v4

--- a/solution.py
+++ b/solution.py
@@ -58,10 +58,23 @@
     out_ref[...] = jnp.broadcast_to(peak[None], out_ref.shape)
 
 
+def combine(counts_ref, fields, crossing, step, n):
+    omega = omega_of(counts_ref)
+    total = None
+    for m, field in enumerate(fields):
+        own, high, low = offsets(step, n, m)
+        factor = SLOPE[own]
+        if m >= 2:
+            factor = jnp.where(crossing, SLOPE[high], SLOPE[low])
+        term = (omega * factor) * field
+        total = term if total is None else total + term
+    return total
+
+
 def add_partials(counts_ref, state_ref, other_ref, out_ref, edge):
     me_x = lax.axis_index("x")
-    upper_half = lax.axis_index("zh")
-    omega = omega_of(counts_ref)
+    is_upper = lax.axis_index("zh") == 1
+    is_even = lax.axis_index("core") == 0
     row = lax.broadcasted_iota(jnp.int32, (8, 512), 0)
     for v in range(5):
         fields = [
@@ -69,18 +82,22 @@
             for ref in (state_ref, other_ref)
             for m in range(2)
         ]
+        if edge:
+            turned = [jnp.where(is_even, f, pltpu.roll(f, 4, axis=0)) for f in fields]
+            turned = turned[2:] + turned[:2]
         for step in range(4):
             target = lax.rem(me_x + step, 4)
             for n in range(2):
-                total = None
-                for m, field in enumerate(fields):
-                    own, high, low = offsets(step, n, m)
-                    factor = SLOPE[own]
-                    if m >= 2:
-                        factor = jnp.where(upper_half == 1, SLOPE[high], SLOPE[low])
-                    term = (omega * factor) * field
-                    total = term if total is None else total + term
+                total = combine(counts_ref, fields, is_upper, step, n)
                 out_ref[target, pl.ds((n * 5 + v) * 8, 8), :] = total
+            if edge:
+                first, second = (
+                    combine(counts_ref, turned, jnp.logical_not(is_upper), step, n)
+                    for n in range(2)
+                )
+                out_ref[target, pl.ds(96 + v * 8, 8), :] = jnp.where(
+                    row < 4, first, pltpu.roll(second, 4, axis=0)
+                )
 
 
 def offsets(step, n, m):
@@ -90,7 +107,7 @@
 
 def partial_kernel(counts_ref, state_ref, other_ref, peaks_ref, out_ref, lag_ref):
     me_x = lax.axis_index("x")
-    upper_half = lax.axis_index("zh")
+    is_lower = lax.axis_index("zh") == 0
     place = lax.axis_index(CELLS)
     is_last = place == lax.axis_size(CELLS) - 1
     add_partials(counts_ref, state_ref, other_ref, out_ref, True)
@@ -118,11 +135,11 @@
             for m in range(4):
                 own, high, low = offsets(step, n, m)
                 factor.append(
-                    lag(own) if m < 2 else jnp.where(upper_half == 1, lag(high), lag(low))
+                    lag(own) if m < 2 else jnp.where(is_lower, lag(high), lag(low))
                 )
             for v in range(5):
                 total = None
-                for m, ref in enumerate((state_ref, state_ref, other_ref, other_ref)):
+                for m, ref in enumerate((other_ref, other_ref, state_ref, state_ref)):
                     edge = jnp.where(is_last, ref[m % 2, v, 15:16, :], ref[m % 2, v, 0:1, :])
                     term = factor[m] * edge
                     total = term if total is None else total + term
@@ -148,17 +165,38 @@
         far_ref[rows, :] = jnp.where(is_even, down, up)
         near_ref[rows, :] = jnp.where(is_even, up, down)
 
-    for n in range(2):
-        for v in range(5):
+    is_low_end = is_even & (lax.axis_index("zl") == 0)
+    is_high_end = jnp.logical_not(is_even) & (
+        lax.axis_index("zl") == lax.axis_size("zl") - 1
+    )
+    is_end = is_low_end | is_high_end
+    near_half = (row < 4) == is_even
+    for v in range(5):
+        extra = added(outer_ref, 96 + v * 8, 8)
+        turned = pltpu.roll(extra, 4, axis=0)
+        for n in range(2):
             at = n * 5 + v
-            lagged = jnp.broadcast_to(added(outer_ref, 80 + at, 1), (8, 512))
+            rows = pl.ds(at * 8, 8)
+            fifth = pl.ds(80 + at, 1)
             source = pltpu.roll(added(outer_ref, at * 8, 8), 4, axis=0)
             up = jnp.where(row >= 4, state_ref[n, v, 8:16, :], source)
-            up = jnp.where(is_last & (row == 7), lagged, up)
             down = jnp.where(row < 4, state_ref[n, v, 0:8, :], source)
-            down = jnp.where(is_first & (row == 0), lagged, down)
-            put(pl.ds(at * 8, 8), up, down)
-            put(pl.ds(80 + at, 1), state_ref[n, v, 11:12, :], state_ref[n, v, 4:5, :])
+            near_ref[rows, :] = jnp.where(is_even, up, down)
+            near_ref[fifth, :] = jnp.where(
+                is_even, state_ref[n, v, 11:12, :], state_ref[n, v, 4:5, :]
+            )
+            far = jnp.where(is_even, down, up)
+            lagged = jnp.broadcast_to(added(outer_ref, 80 + at, 1), (8, 512))
+            theirs = jnp.where(is_even, other_ref[n, v, 0:8, :], other_ref[n, v, 8:16, :])
+            source = jnp.where(is_even, turned, extra) if n == 0 else jnp.where(is_even, extra, turned)
+            theirs = jnp.where(near_half, theirs, source)
+            theirs = jnp.where((is_first & (row == 0)) | (is_last & (row == 7)), lagged, theirs)
+            far_ref[rows, :] = jnp.where(is_end, theirs, far)
+            low, high = (
+                jnp.where(is_end, other_ref[n, v, k : k + 1, :], state_ref[n, v, k : k + 1, :])
+                for k in (4, 11)
+            )
+            far_ref[fifth, :] = jnp.where(is_even, low, high)
     put(pl.ds(90, 4), wall_ref[12:16, :], wall_ref[0:4, :])
     put(pl.ds(94, 2), wall_ref[14:16, :], wall_ref[0:2, :])
     add_partials(counts_ref, state_ref, other_ref, inner_ref, False)
@@ -297,7 +335,7 @@
     )(peaks)
     peaks = lax.all_to_all(peak, ("zl", "zh", "core"), 0, 0)
     outer = pl.pallas_call(
-        partial_kernel, out_shape=field((4, 96, 512)),
+        partial_kernel, out_shape=field((4, 136, 512)),
         in_specs=[SMEM, VMEM, VMEM, VMEM], out_specs=VMEM,
         scratch_shapes=[pltpu.VMEM((NT, 128), f32)],
         compiler_params=PARAMS, name="partial_sources",
@@ -309,8 +347,13 @@
         compiler_params=PARAMS, name="edges",
     )(counts, state, other, wall_distance, outer)
     count = lax.axis_size(CELLS)
-    across = [((i + 1) % count, (i + 2) % count) for i in range(0, count, 2)]
-    far = lax.ppermute(far, CELLS, across + [(j, i) for i, j in across])
+    line = 2 * lax.axis_size("zl")
+    across = []
+    for i in range(1, count, 2):
+        for half in range(2):
+            there = 1 - half if (i + 1) % line == 0 else half
+            across.append((2 * i + half, 2 * ((i + 1) % count) + there))
+    far = lax.ppermute(far, CELLS + ("zh",), across + [(j, i) for i, j in across])
     near = lax.ppermute(near, "core", [(0, 1), (1, 0)])
     inner = lax.all_to_all(inner, "x", 0, 0)
     return pl.pallas_call(

time: 101 us -> 99.4 us (0.984)
  waiting for transfers between devices: 10.3 us -> 4.93 us
  blocking collectives: 50.9 us -> 54.4 us
    ppermute x1, waiting for transfers between devices: 10.3 us -> 4.93 us  [local(): lax.ppermute(far, CELLS + ('zh',), across + [(j, i) for i, j in across])]
    all_to_all x1, blocking collectives: 15.4 us -> 18.9 us  [local(): outer = lax.all_to_all(outer, 'x', 0, 0)]
where the time goes in v7:
time: 99.4 us; the launch traced here: 99 us
  blocking collectives  54.4 us (55%)
  starting transfers between devices  29.6 us (30%)
  Pallas kernels  8.38 us (8%)
  waiting for transfers between devices  4.93 us (5%)
  local copies, waits for them, and re-layouts  1.64 us (2%)
    all_to_all x1, blocking collectives, local(): peaks = lax.all_to_all(peak, ('zl', 'zh', 'core'), 0, 0)  26.1 us
    ppermute x1, starting transfers between devices, local(): other = lax.ppermute(state, 'zh', [(0, 1), (1, 0)])  19.3 us
    all_to_all x1, blocking collectives, local(): outer = lax.all_to_all(outer, 'x', 0, 0)  18.9 us
    all_to_all x1, blocking collectives, local(): peaks = lax.all_to_all(peak, 'y', 0, 0)  9.31 us
    ppermute x1, waiting for transfers between devices, local(): lax.ppermute(far, CELLS + ('zh',), across + [(j, i) for i, j in across])  4.93 us
    all_to_all x1, starting transfers between devices, local(): inner = lax.all_to_all(inner, 'x', 0, 0)  4.91 us
    pallas_call x1, Pallas kernels, local(): pl.pallas_call(march_kernel, out_shape=field(state.shape), in_specs=[SMEM...  4.31 us
    ppermute x1, starting transfers between devices, local(): near = lax.ppermute(near, 'core', [(0, 1), (1, 0)])  3.45 us
  transfers between devices with their start and end apart: 4, of which 1 were waited for; matrix products, arithmetic and copies ran while one was open for 0% of the time, Pallas kernels for 1%

profile of v7, /device:TPU:34, one launch (start us, length us, event | category | flops | bytes accessed | tf_op | source)
XLA Modules:
  0.0 99.0 jit_solution(7840940068661124671)
XLA Ops:
  0.0 19.3 %collective-permute-start = (f32[2,5,16,512]{3,2,1,0:T(8,128)}, f32[2,5,16,512]{3,2,1,0:T(8,128)S(1)}, u32[]{:S(2)}, u32[]{:S(2)}) collective-permute-start(f32[2,5,16,512]{3,2,1,0:T(8,128)} %state_ref.1), channel_id=1, source_target_pairs={{0,1},{1,0},{2,3},{3,2},{4,5},{5,4},{6,7},{7,6},{8,9},{9,8},{10,11... | collective-permute-start | bytes 983048 | tf_op jit(solution)/shard_map/ppermute | solution.py:325
  19.4 0.0 copy-start
  19.4 1.0 copy-done
  20.3 0.0 copy-start.2
  20.3 0.7 copy-done.2
  21.0 1.2 %peak.1 = (f32[8,1,128]{2,1,0:T(1,128)S(1)}, f32[2]{0:T(128)S(1)}, f32[2,5,16,512]{3,2,1,0:T(8,128)S(1)}) custom-call(s32[2]{0:T(128)S(1)} %copy-done.2, f32[2,5,16,512]{3,2,1,0:T(8,128)S(1)} %copy-done), custom_call_target="tpu_custom_call" | custom-call | tf_op jit(solution)/shard_map/peak/pallas_call | solution.py:326
  22.2 9.3 %all_to_all.20.peaks_ref = f32[8,1,128]{2,1,0:T(1,128)S(1)} all-to-all(f32[8,1,128]{2,1,0:T(1,128)S(1)} %get-tuple-element.13), channel_id=1, replica_groups=mesh['y'=8,'zl'=8,'core'=2,'x'=4,'zh'=2] {'y'}, dimensions={0} | all-to-all | bytes 8192 | tf_op jit(solution)/shard_map/all_to_all | solution.py:331
  31.5 26.1 %all_to_all.21.peaks_ref = f32[32,1,128]{2,1,0:T(1,128)S(1)} all-to-all(f32[32,1,128]{2,1,0:T(1,128)S(1)} %fold.1), channel_id=1, replica_groups=mesh['y'=8,'zl'=8,'core'=2,'x'=4,'zh'=2] {'zl','zh','core'}, dimensions={0} | all-to-all | bytes 32768 | tf_op jit(solution)/shard_map/all_to_all | solution.py:336
  57.6 0.0 collective-permute-done.other_ref
  57.6 1.3 %partial_sources.1 = f32[4,136,512]{2,1,0:T(8,128)S(1)} custom-call(f32[2]{0:T(128)S(1)} %get-tuple-element.11.counts_ref, f32[2,5,16,512]{3,2,1,0:T(8,128)S(1)} %get-tuple-element.12.state_ref, f32[2,5,16,512]{3,2,1,0:T(8,128)S(1)} %collective-permute-done.other_ref, f32[32,1,128]{2,1,0:T(1,128)S(1)} %all_to_all.21.peaks_ref), custom_call_target="tpu_custom_call" | custom-call | tf_op jit(solution)/shard_map/partial_sources/pallas_call | solution.py:337
  58.9 0.0 copy-start.1
  58.9 18.9 %all_to_all.22.outer_ref = f32[4,136,512]{2,1,0:T(8,128)S(1)} all-to-all(f32[4,136,512]{2,1,0:T(8,128)S(1)} %partial_sources.1), channel_id=1, replica_groups=mesh['y'=8,'zl'=8,'core'=2,'x'=4,'zh'=2] {'x'}, dimensions={0} | all-to-all | bytes 2228224 | tf_op jit(solution)/shard_map/all_to_all | solution.py:343
  77.8 0.0 copy-done.1
  77.8 1.6 %edges.1 = (f32[96,512]{1,0:T(8,128)S(1)}, f32[96,512]{1,0:T(8,128)S(1)}, f32[4,80,512]{2,1,0:T(8,128)}) custom-call(f32[2]{0:T(128)S(1)} %get-tuple-element.11.counts_ref, f32[2,5,16,512]{3,2,1,0:T(8,128)S(1)} %get-tuple-element.12.state_ref, f32[2,5,16,512]{3,2,1,0:T(8,128)S(1)} %collective-permute-done.other_ref, f32[16,512]{1,0:T(8,128)S(1)} %copy-done.1, ...), custom_call_target="tpu_custom_call" | custom-call | tf_op jit(solution)/shard_map/edges/pallas_call | solution.py:344
  79.5 4.9 %all-to-all-start.3 = ((f32[4,80,512]{2,1,0:T(8,128)}), f32[4,80,512]{2,1,0:T(8,128)S(1)}, u32[]{:S(2)}, u32[]{:S(2)}) async-start(f32[4,80,512]{2,1,0:T(8,128)} %get-tuple-element.14), calls=%async_computation.3 | async-start | bytes 1310720 | tf_op jit(solution)/shard_map/all_to_all | solution.py:358
  84.4 1.9 %collective-permute-start.1 = (f32[96,512]{1,0:T(8,128)S(1)}, f32[96,512]{1,0:T(8,128)S(1)}, u32[]{:S(2)}, u32[]{:S(2)}) collective-permute-start(f32[96,512]{1,0:T(8,128)S(1)} %get-tuple-element.15), channel_id=1, source_target_pairs={{8,16},{9,17},{24,32},{25,33},{40,48},{41,49},{56,64},{57,65},{72,... | collective-permute-start | bytes 589832 | tf_op jit(solution)/shard_map/ppermute | solution.py:356
  86.3 3.4 %collective-permute-start.2 = (f32[96,512]{1,0:T(8,128)S(1)}, f32[96,512]{1,0:T(8,128)S(1)}, u32[]{:S(2)}, u32[]{:S(2)}) collective-permute-start(f32[96,512]{1,0:T(8,128)S(1)} %get-tuple-element.16), channel_id=1, source_target_pairs={{0,8},{8,0},{1,9},{9,1},{2,10},{10,2},{3,11},{11,3},{4,12},{12,4},... | collective-permute-start | bytes 589832 | tf_op jit(solution)/shard_map/ppermute | solution.py:357
  89.7 4.9 %collective-permute-done.1.far_ref = f32[96,512]{1,0:T(8,128)S(1)} collective-permute-done((f32[96,512]{1,0:T(8,128)S(1)}, f32[96,512]{1,0:T(8,128)S(1)}, u32[]{:S(2)}, u32[]{:S(2)}) %collective-permute-start.1) | collective-permute-done | bytes 196640 | tf_op jit(solution)/shard_map/ppermute | solution.py:356
  94.7 0.0 collective-permute-done.2.near_ref
  94.7 0.0 all-to-all-done.3.inner_ref
  94.7 4.3 %march.1 = f32[2,5,16,512]{3,2,1,0:T(8,128)} custom-call(f32[2]{0:T(128)S(1)} %get-tuple-element.11.counts_ref, f32[2,5,16,512]{3,2,1,0:T(8,128)S(1)} %get-tuple-element.12.state_ref, f32[16,512]{1,0:T(8,128)S(1)} %copy-done.1, f32[4,136,512]{2,1,0:T(8,128)S(1)} %all_to_all.22.outer_ref, f32[4,80,512]{2,1,0:T(8,128)S(1)} %all-to-all-done.3.inner_ref, ...), custom_call_target="tpu_custom_call" | custom-call | tf_op jit(solution)/shard_map/march/pallas_call | solution.py:359
  (1 shorter events, 0.0 us)
Async XLA Ops:
  0.0 57.6 %collective-permute-start = (f32[2,5,16,512]{3,2,1,0:T(8,128)}, f32[2,5,16,512]{3,2,1,0:T(8,128)S(1)}, u32[]{:S(2)}, u32[]{:S(2)}) collective-permute-start(f32[2,5,16,512]{3,2,1,0:T(8,128)} %state_ref.1), channel_id=1, source_target_pairs={{0,1},{1,0},{2,3},{3,2},{4,5},{5,4},{6,7},{7,6},{8,9},{9,8},{10,11... | collective-permute-start | bytes 983048 | tf_op jit(solution)/shard_map/ppermute | solution.py:325
  19.4 1.0 copy-start
  20.3 0.7 copy-start.2
  58.9 18.9 %copy-start.1 = (f32[16,512]{1,0:T(8,128)S(1)}, f32[16,512]{1,0:T(8,128)}, u32[]{:S(2)}) copy-start(f32[16,512]{1,0:T(8,128)} %wall_ref.3) | copy-start | bytes 98308
  79.5 15.2 %all-to-all-start.3 = ((f32[4,80,512]{2,1,0:T(8,128)}), f32[4,80,512]{2,1,0:T(8,128)S(1)}, u32[]{:S(2)}, u32[]{:S(2)}) async-start(f32[4,80,512]{2,1,0:T(8,128)} %get-tuple-element.14), calls=%async_computation.3 | async-start | bytes 1310720 | tf_op jit(solution)/shard_map/all_to_all | solution.py:358
  84.4 10.3 %collective-permute-start.1 = (f32[96,512]{1,0:T(8,128)S(1)}, f32[96,512]{1,0:T(8,128)S(1)}, u32[]{:S(2)}, u32[]{:S(2)}) collective-permute-start(f32[96,512]{1,0:T(8,128)S(1)} %get-tuple-element.15), channel_id=1, source_target_pairs={{8,16},{9,17},{24,32},{25,33},{40,48},{41,49},{56,64},{57,65},{72,... | collective-permute-start | bytes 589832 | tf_op jit(solution)/shard_map/ppermute | solution.py:356
  86.3 8.4 %collective-permute-start.2 = (f32[96,512]{1,0:T(8,128)S(1)}, f32[96,512]{1,0:T(8,128)S(1)}, u32[]{:S(2)}, u32[]{:S(2)}) collective-permute-start(f32[96,512]{1,0:T(8,128)S(1)} %get-tuple-element.16), channel_id=1, source_target_pairs={{0,8},{8,0},{1,9},{9,1},{2,10},{10,2},{3,11},{11,3},{4,12},{12,4},... | collective-permute-start | bytes 589832 | tf_op jit(solution)/shard_map/ppermute | solution.py:357

commit v8 on v7

--- a/solution.py
+++ b/solution.py
@@ -89,7 +89,7 @@
             target = lax.rem(me_x + step, 4)
             for n in range(2):
                 total = combine(counts_ref, fields, is_upper, step, n)
-                out_ref[target, pl.ds((n * 5 + v) * 8, 8), :] = total
+                out_ref[target, pl.ds((0 if edge else 136) + (n * 5 + v) * 8, 8), :] = total
             if edge:
                 first, second = (
                     combine(counts_ref, turned, jnp.logical_not(is_upper), step, n)
@@ -111,6 +111,7 @@
     place = lax.axis_index(CELLS)
     is_last = place == lax.axis_size(CELLS) - 1
     add_partials(counts_ref, state_ref, other_ref, out_ref, True)
+    add_partials(counts_ref, state_ref, other_ref, out_ref, False)
     ratio = jnp.full((NT, 128), counts_ref[1]) / jnp.full((NT, 128), counts_ref[0])
     sigma = 2.0 * math.pi * ratio
     shift = jnp.where(is_last, sigma, -sigma)
@@ -154,7 +155,7 @@
     )
 
 
-def edge_kernel(counts_ref, state_ref, other_ref, wall_ref, outer_ref, far_ref, near_ref, inner_ref):
+def edge_kernel(state_ref, other_ref, wall_ref, outer_ref, far_ref, near_ref):
     place = lax.axis_index(CELLS)
     is_first = place == 0
     is_last = place == lax.axis_size(CELLS) - 1
@@ -199,7 +200,6 @@
             far_ref[fifth, :] = jnp.where(is_even, low, high)
     put(pl.ds(90, 4), wall_ref[12:16, :], wall_ref[0:4, :])
     put(pl.ds(94, 2), wall_ref[14:16, :], wall_ref[0:2, :])
-    add_partials(counts_ref, state_ref, other_ref, inner_ref, False)
 
 
 def march_kernel(
@@ -207,7 +207,6 @@
     state_ref,
     wall_ref,
     outer_ref,
-    inner_ref,
     far_ref,
     near_ref,
     out_ref,
@@ -262,7 +261,7 @@
             source_ref[n, v, 24:32, :] = 2.0 * pltpu.roll(packed, 4, axis=0)
             start_ref[n, v, 8:24, :] = state_ref[n, v, :, :]
             outer = 2.0 * added(outer_ref, at * 8, 8)
-            inner = 2.0 * added(inner_ref, at * 8, 8)
+            inner = 2.0 * added(outer_ref, 136 + at * 8, 8)
             source_ref[n, v, 8:16, :] = jnp.where(row < 4, outer, inner)
             source_ref[n, v, 16:24, :] = jnp.where(row < 4, inner, outer)
         for t in range(4):
@@ -335,17 +334,17 @@
     )(peaks)
     peaks = lax.all_to_all(peak, ("zl", "zh", "core"), 0, 0)
     outer = pl.pallas_call(
-        partial_kernel, out_shape=field((4, 136, 512)),
+        partial_kernel, out_shape=field((4, 216, 512)),
         in_specs=[SMEM, VMEM, VMEM, VMEM], out_specs=VMEM,
         scratch_shapes=[pltpu.VMEM((NT, 128), f32)],
         compiler_params=PARAMS, name="partial_sources",
     )(counts, state, other, peaks)
     outer = lax.all_to_all(outer, "x", 0, 0)
-    far, near, inner = pl.pallas_call(
-        edge_kernel, out_shape=(field((96, 512)), field((96, 512)), field((4, 80, 512))),
-        in_specs=[SMEM] + [VMEM] * 4, out_specs=(VMEM, VMEM, VMEM),
+    far, near = pl.pallas_call(
+        edge_kernel, out_shape=(field((96, 512)), field((96, 512))),
+        in_specs=[VMEM] * 4, out_specs=(VMEM, VMEM),
         compiler_params=PARAMS, name="edges",
-    )(counts, state, other, wall_distance, outer)
+    )(state, other, wall_distance, outer)
     count = lax.axis_size(CELLS)
     line = 2 * lax.axis_size("zl")
     across = []
@@ -355,10 +354,9 @@
             across.append((2 * i + half, 2 * ((i + 1) % count) + there))
     far = lax.ppermute(far, CELLS + ("zh",), across + [(j, i) for i, j in across])
     near = lax.ppermute(near, "core", [(0, 1), (1, 0)])
-    inner = lax.all_to_all(inner, "x", 0, 0)
     return pl.pallas_call(
         march_kernel, out_shape=field(state.shape),
-        in_specs=[SMEM] + [VMEM] * 6, out_specs=VMEM,
+        in_specs=[SMEM] + [VMEM] * 5, out_specs=VMEM,
         scratch_shapes=[
             pltpu.VMEM((2, 5, 32, 512), f32),
             pltpu.VMEM((2, 5, 32, 512), f32),
@@ -370,7 +368,7 @@
             pltpu.VMEM((5, 48, 512), f32),
         ],
         compiler_params=PARAMS, name="march",
-    )(counts, state, wall_distance, outer, inner, far, near)
+    )(counts, state, wall_distance, outer, far, near)
 
 
 def solution(mesh):

time: 99.4 us -> 101 us (1.016)
  the two profiles are of different devices: /device:TPU:34 before, /device:TPU:32 now
where the time goes in v8:
time: 101 us
  blocking collectives  62.3 us (62%)
  starting transfers between devices  24.7 us (24%)
  Pallas kernels  7.06 us (7%)
  waiting for transfers between devices  4.93 us (5%)
  local copies, waits for them, and re-layouts  1.64 us (2%)
    all_to_all x1, blocking collectives, local(): outer = lax.all_to_all(outer, 'x', 0, 0)  26.9 us
    all_to_all x1, blocking collectives, local(): peaks = lax.all_to_all(peak, ('zl', 'zh', 'core'), 0, 0)  26.1 us
    ppermute x1, starting transfers between devices, local(): other = lax.ppermute(state, 'zh', [(0, 1), (1, 0)])  19.3 us
    all_to_all x1, blocking collectives, local(): peaks = lax.all_to_all(peak, 'y', 0, 0)  9.31 us
    ppermute x1, waiting for transfers between devices, local(): lax.ppermute(far, CELLS + ('zh',), across + [(j, i) for i, j in across])  4.93 us
    pallas_call x1, Pallas kernels, local(): pl.pallas_call(march_kernel, out_shape=field(state.shape), in_specs=[SMEM...  4.33 us
    ppermute x1, starting transfers between devices, local(): near = lax.ppermute(near, 'core', [(0, 1), (1, 0)])  3.45 us
  transfers between devices with their start and end apart: 3, of which 1 were waited for; matrix products, arithmetic and copies ran while one was open for 0% of the time, Pallas kernels for 1%

profile of v8, /device:TPU:32, one launch (start us, length us, event | category | flops | bytes accessed | tf_op | source)
XLA Modules:
  0.0 100.7 jit_solution(8082707925651415156)
XLA Ops:
  0.0 19.3 %collective-permute-start = (f32[2,5,16,512]{3,2,1,0:T(8,128)}, f32[2,5,16,512]{3,2,1,0:T(8,128)S(1)}, u32[]{:S(2)}, u32[]{:S(2)}) collective-permute-start(f32[2,5,16,512]{3,2,1,0:T(8,128)} %state_ref.1), channel_id=1, source_target_pairs={{0,1},{1,0},{2,3},{3,2},{4,5},{5,4},{6,7},{7,6},{8,9},{9,8},{10,11... | collective-permute-start | bytes 983048 | tf_op jit(solution)/shard_map/ppermute | solution.py:324
  19.4 0.0 copy-start
  19.4 1.0 copy-done
  20.3 0.0 copy-start.2
  20.3 0.7 copy-done.2
  21.0 1.2 %peak.1 = (f32[8,1,128]{2,1,0:T(1,128)S(1)}, f32[2]{0:T(128)S(1)}, f32[2,5,16,512]{3,2,1,0:T(8,128)S(1)}) custom-call(s32[2]{0:T(128)S(1)} %copy-done.2, f32[2,5,16,512]{3,2,1,0:T(8,128)S(1)} %copy-done), custom_call_target="tpu_custom_call" | custom-call | tf_op jit(solution)/shard_map/peak/pallas_call | solution.py:325
  22.2 9.3 %all_to_all.15.peaks_ref = f32[8,1,128]{2,1,0:T(1,128)S(1)} all-to-all(f32[8,1,128]{2,1,0:T(1,128)S(1)} %get-tuple-element.12), channel_id=1, replica_groups=mesh['y'=8,'zl'=8,'core'=2,'x'=4,'zh'=2] {'y'}, dimensions={0} | all-to-all | bytes 8192 | tf_op jit(solution)/shard_map/all_to_all | solution.py:330
  31.5 26.1 %all_to_all.16.peaks_ref = f32[32,1,128]{2,1,0:T(1,128)S(1)} all-to-all(f32[32,1,128]{2,1,0:T(1,128)S(1)} %fold.1), channel_id=1, replica_groups=mesh['y'=8,'zl'=8,'core'=2,'x'=4,'zh'=2] {'zl','zh','core'}, dimensions={0} | all-to-all | bytes 32768 | tf_op jit(solution)/shard_map/all_to_all | solution.py:335
  57.6 0.0 collective-permute-done.other_ref
  57.6 1.4 %partial_sources.1 = f32[4,216,512]{2,1,0:T(8,128)S(1)} custom-call(f32[2]{0:T(128)S(1)} %get-tuple-element.10.counts_ref, f32[2,5,16,512]{3,2,1,0:T(8,128)S(1)} %get-tuple-element.11.state_ref, f32[2,5,16,512]{3,2,1,0:T(8,128)S(1)} %collective-permute-done.other_ref, f32[32,1,128]{2,1,0:T(1,128)S(1)} %all_to_all.16.peaks_ref), custom_call_target="tpu_custom_call" | custom-call | tf_op jit(solution)/shard_map/partial_sources/pallas_call | solution.py:336
  59.1 0.0 copy-start.1
  59.1 26.9 %all_to_all.17.outer_ref = f32[4,216,512]{2,1,0:T(8,128)S(1)} all-to-all(f32[4,216,512]{2,1,0:T(8,128)S(1)} %partial_sources.1), channel_id=1, replica_groups=mesh['y'=8,'zl'=8,'core'=2,'x'=4,'zh'=2] {'x'}, dimensions={0} | all-to-all | bytes 3538944 | tf_op jit(solution)/shard_map/all_to_all | solution.py:342
  86.0 0.0 copy-done.1
  86.0 0.1 edges.1
  86.1 1.9 %collective-permute-start.1 = (f32[96,512]{1,0:T(8,128)S(1)}, f32[96,512]{1,0:T(8,128)S(1)}, u32[]{:S(2)}, u32[]{:S(2)}) collective-permute-start(f32[96,512]{1,0:T(8,128)S(1)} %get-tuple-element.13), channel_id=1, source_target_pairs={{8,16},{9,17},{24,32},{25,33},{40,48},{41,49},{56,64},{57,65},{72,... | collective-permute-start | bytes 589832 | tf_op jit(solution)/shard_map/ppermute | solution.py:355
  88.0 3.4 %collective-permute-start.2 = (f32[96,512]{1,0:T(8,128)S(1)}, f32[96,512]{1,0:T(8,128)S(1)}, u32[]{:S(2)}, u32[]{:S(2)}) collective-permute-start(f32[96,512]{1,0:T(8,128)S(1)} %get-tuple-element.14), channel_id=1, source_target_pairs={{0,8},{8,0},{1,9},{9,1},{2,10},{10,2},{3,11},{11,3},{4,12},{12,4},... | collective-permute-start | bytes 589832 | tf_op jit(solution)/shard_map/ppermute | solution.py:356
  91.5 4.9 %collective-permute-done.1.far_ref = f32[96,512]{1,0:T(8,128)S(1)} collective-permute-done((f32[96,512]{1,0:T(8,128)S(1)}, f32[96,512]{1,0:T(8,128)S(1)}, u32[]{:S(2)}, u32[]{:S(2)}) %collective-permute-start.1) | collective-permute-done | bytes 196640 | tf_op jit(solution)/shard_map/ppermute | solution.py:355
  96.4 0.0 collective-permute-done.2.near_ref
  96.4 4.3 %march.1 = f32[2,5,16,512]{3,2,1,0:T(8,128)} custom-call(f32[2]{0:T(128)S(1)} %get-tuple-element.10.counts_ref, f32[2,5,16,512]{3,2,1,0:T(8,128)S(1)} %get-tuple-element.11.state_ref, f32[16,512]{1,0:T(8,128)S(1)} %copy-done.1, f32[4,216,512]{2,1,0:T(8,128)S(1)} %all_to_all.17.outer_ref, f32[96,512]{1,0:T(8,128)S(1)} %collective-permute-done.1.far_ref, ...), custom_call_target="tpu_custom_call" | custom-call | tf_op jit(solution)/shard_map/march/pallas_call | solution.py:357
  (1 shorter events, 0.0 us)
Async XLA Ops:
  0.0 57.6 %collective-permute-start = (f32[2,5,16,512]{3,2,1,0:T(8,128)}, f32[2,5,16,512]{3,2,1,0:T(8,128)S(1)}, u32[]{:S(2)}, u32[]{:S(2)}) collective-permute-start(f32[2,5,16,512]{3,2,1,0:T(8,128)} %state_ref.1), channel_id=1, source_target_pairs={{0,1},{1,0},{2,3},{3,2},{4,5},{5,4},{6,7},{7,6},{8,9},{9,8},{10,11... | collective-permute-start | bytes 983048 | tf_op jit(solution)/shard_map/ppermute | solution.py:324
  19.4 1.0 copy-start
  20.3 0.7 copy-start.2
  59.1 26.9 %copy-start.1 = (f32[16,512]{1,0:T(8,128)S(1)}, f32[16,512]{1,0:T(8,128)}, u32[]{:S(2)}) copy-start(f32[16,512]{1,0:T(8,128)} %wall_ref.3) | copy-start | bytes 98308
  86.1 10.3 %collective-permute-start.1 = (f32[96,512]{1,0:T(8,128)S(1)}, f32[96,512]{1,0:T(8,128)S(1)}, u32[]{:S(2)}, u32[]{:S(2)}) collective-permute-start(f32[96,512]{1,0:T(8,128)S(1)} %get-tuple-element.13), channel_id=1, source_target_pairs={{8,16},{9,17},{24,32},{25,33},{40,48},{41,49},{56,64},{57,65},{72,... | collective-permute-start | bytes 589832 | tf_op jit(solution)/shard_map/ppermute | solution.py:355
  88.0 8.4 %collective-permute-start.2 = (f32[96,512]{1,0:T(8,128)S(1)}, f32[96,512]{1,0:T(8,128)S(1)}, u32[]{:S(2)}, u32[]{:S(2)}) collective-permute-start(f32[96,512]{1,0:T(8,128)S(1)} %get-tuple-element.14), channel_id=1, source_target_pairs={{0,8},{8,0},{1,9},{9,1},{2,10},{10,2},{3,11},{11,3},{4,12},{12,4},... | collective-permute-start | bytes 589832 | tf_op jit(solution)/shard_map/ppermute | solution.py:356

commit v9 on v7

--- a/solution.py
+++ b/solution.py
@@ -95,7 +95,7 @@
                     combine(counts_ref, turned, jnp.logical_not(is_upper), step, n)
                     for n in range(2)
                 )
-                out_ref[target, pl.ds(96 + v * 8, 8), :] = jnp.where(
+                out_ref[target, pl.ds(80 + v * 8, 8), :] = jnp.where(
                     row < 4, first, pltpu.roll(second, 4, axis=0)
                 )
 
@@ -105,7 +105,7 @@
     return apart % NT, (apart + 2) % NT, (apart - 2) % NT
 
 
-def partial_kernel(counts_ref, state_ref, other_ref, peaks_ref, out_ref, lag_ref):
+def partial_kernel(counts_ref, state_ref, other_ref, _, out_ref, lag_ref):
     me_x = lax.axis_index("x")
     is_lower = lax.axis_index("zh") == 0
     place = lax.axis_index(CELLS)
@@ -126,25 +126,26 @@
     def lag(j):
         return jnp.concatenate([lag_ref[j : j + 1, :]] * 4, axis=1)
 
-    peak = jnp.max(peaks_ref[...], axis=0)
-    peak = jnp.broadcast_to(jnp.concatenate([peak] * 4, axis=1), (6, 512))
-    for step in range(4):
-        target = lax.rem(me_x + step, 4)
-        for n in range(2):
-            factor = []
-            for m in range(4):
-                own, high, low = offsets(step, n, m)
-                factor.append(
-                    lag(own) if m < 2 else jnp.where(is_lower, lag(high), lag(low))
-                )
+    row = lax.broadcasted_iota(jnp.int32, (8, 512), 0)
+
+    @pl.when((place == 0) | is_last)
+    def _():
+        for step in range(4):
+            target = lax.rem(me_x + step, 4)
             for v in range(5):
-                total = None
-                for m, ref in enumerate((other_ref, other_ref, state_ref, state_ref)):
-                    edge = jnp.where(is_last, ref[m % 2, v, 15:16, :], ref[m % 2, v, 0:1, :])
-                    term = factor[m] * edge
-                    total = term if total is None else total + term
-                out_ref[target, pl.ds(80 + n * 5 + v, 1), :] = total
-        out_ref[target, pl.ds(90, 6), :] = peak
+                totals = []
+                for n in range(2):
+                    total = None
+                    for m, ref in enumerate((other_ref, other_ref, state_ref, state_ref)):
+                        own, high, low = offsets(step, n, m)
+                        factor = (
+                            lag(own) if m < 2 else jnp.where(is_lower, lag(high), lag(low))
+                        )
+                        edge = jnp.where(is_last, ref[m % 2, v, 15:16, :], ref[m % 2, v, 0:1, :])
+                        term = factor * edge
+                        total = term if total is None else total + term
+                    totals.append(jnp.broadcast_to(total, (8, 512)))
+                out_ref[target, pl.ds(80 + v * 8, 8), :] = jnp.where(row < 4, *totals)
 
 
 def added(parts_ref, start, count):
@@ -172,7 +173,7 @@
     is_end = is_low_end | is_high_end
     near_half = (row < 4) == is_even
     for v in range(5):
-        extra = added(outer_ref, 96 + v * 8, 8)
+        extra = added(outer_ref, 80 + v * 8, 8)
         turned = pltpu.roll(extra, 4, axis=0)
         for n in range(2):
             at = n * 5 + v
@@ -186,7 +187,7 @@
                 is_even, state_ref[n, v, 11:12, :], state_ref[n, v, 4:5, :]
             )
             far = jnp.where(is_even, down, up)
-            lagged = jnp.broadcast_to(added(outer_ref, 80 + at, 1), (8, 512))
+            lagged = jnp.broadcast_to(extra[4 * n : 4 * n + 1, :], (8, 512))
             theirs = jnp.where(is_even, other_ref[n, v, 0:8, :], other_ref[n, v, 8:16, :])
             source = jnp.where(is_even, turned, extra) if n == 0 else jnp.where(is_even, extra, turned)
             theirs = jnp.where(near_half, theirs, source)
@@ -210,6 +211,7 @@
     inner_ref,
     far_ref,
     near_ref,
+    peaks_ref,
     out_ref,
     start_ref,
     now_ref,
@@ -236,9 +238,8 @@
     def upper(rows):
         return jnp.where(is_even, near_ref[rows, :], far_ref[rows, :])
 
-    peak = outer_ref[0, 90:91, :]
-    for k in range(1, 4):
-        peak = jnp.maximum(peak, outer_ref[k, 90:91, :])
+    peak = jnp.max(peaks_ref[...], axis=0)
+    peak = jnp.concatenate([peak] * 4, axis=1)
     wave = jnp.broadcast_to(peak, (8, 512))
 
     walls = [
@@ -324,18 +325,18 @@
     field = functools.partial(jax.ShapeDtypeStruct, dtype=f32)
     other = lax.ppermute(state, "zh", [(0, 1), (1, 0)])
     peak, counts, state = pl.pallas_call(
-        peak_kernel, out_shape=(field((8, 1, 128)), field((2,)), field(state.shape)),
+        peak_kernel, out_shape=(field((32, 1, 128)), field((2,)), field(state.shape)),
         in_specs=[SMEM, VMEM], out_specs=(VMEM, SMEM, VMEM),
         compiler_params=PARAMS, name="peak",
     )(blade_counts, state)
-    peaks = lax.all_to_all(peak, "y", 0, 0)
+    peaks = lax.all_to_all(peak, ("y", "x"), 0, 0)
     peak = pl.pallas_call(
         fold_kernel, out_shape=field((32, 1, 128)), in_specs=[VMEM], out_specs=VMEM,
         compiler_params=PARAMS, name="fold",
     )(peaks)
     peaks = lax.all_to_all(peak, ("zl", "zh", "core"), 0, 0)
     outer = pl.pallas_call(
-        partial_kernel, out_shape=field((4, 136, 512)),
+        partial_kernel, out_shape=field((4, 120, 512)),
         in_specs=[SMEM, VMEM, VMEM, VMEM], out_specs=VMEM,
         scratch_shapes=[pltpu.VMEM((NT, 128), f32)],
         compiler_params=PARAMS, name="partial_sources",
@@ -358,7 +359,7 @@
     inner = lax.all_to_all(inner, "x", 0, 0)
     return pl.pallas_call(
         march_kernel, out_shape=field(state.shape),
-        in_specs=[SMEM] + [VMEM] * 6, out_specs=VMEM,
+        in_specs=[SMEM] + [VMEM] * 7, out_specs=VMEM,
         scratch_shapes=[
             pltpu.VMEM((2, 5, 32, 512), f32),
             pltpu.VMEM((2, 5, 32, 512), f32),
@@ -370,7 +371,7 @@
             pltpu.VMEM((5, 48, 512), f32),
         ],
         compiler_params=PARAMS, name="march",
-    )(counts, state, wall_distance, outer, inner, far, near)
+    )(counts, state, wall_distance, outer, inner, far, near, peaks)
 
 
 def solution(mesh):

time: 99.4 us -> 101 us (1.016)
  the two profiles are of different devices: /device:TPU:34 before, /device:TPU:2 now
where the time goes in v9:
time: 101 us
  blocking collectives  56 us (55%)
  starting transfers between devices  29 us (29%)
  Pallas kernels  8.31 us (8%)
  waiting for transfers between devices  5.58 us (6%)
  local copies, waits for them, and re-layouts  1.64 us (2%)
    all_to_all x1, blocking collectives, local(): peaks = lax.all_to_all(peak, ('zl', 'zh', 'core'), 0, 0)  20.5 us
    ppermute x1, starting transfers between devices, local(): other = lax.ppermute(state, 'zh', [(0, 1), (1, 0)])  19.3 us
    all_to_all x1, blocking collectives, local(): peaks = lax.all_to_all(peak, ('y', 'x'), 0, 0)  18.6 us
    all_to_all x1, blocking collectives, local(): outer = lax.all_to_all(outer, 'x', 0, 0)  16.9 us
    ppermute x1, waiting for transfers between devices, local(): lax.ppermute(far, CELLS + ('zh',), across + [(j, i) for i, j in across])  5.58 us
    all_to_all x1, starting transfers between devices, local(): inner = lax.all_to_all(inner, 'x', 0, 0)  4.91 us
    pallas_call x1, Pallas kernels, local(): pl.pallas_call(march_kernel, out_shape=field(state.shape), in_specs=[SMEM...  4.29 us
    ppermute x1, starting transfers between devices, local(): near = lax.ppermute(near, 'core', [(0, 1), (1, 0)])  2.8 us
  transfers between devices with their start and end apart: 4, of which 1 were waited for; matrix products, arithmetic and copies ran while one was open for 0% of the time, Pallas kernels for 1%

profile of v9, /device:TPU:2, one launch (start us, length us, event | category | flops | bytes accessed | tf_op | source)
XLA Modules:
  0.0 100.6 jit_solution(13996311564429886787)
XLA Ops:
  0.0 19.3 %collective-permute-start = (f32[2,5,16,512]{3,2,1,0:T(8,128)}, f32[2,5,16,512]{3,2,1,0:T(8,128)S(1)}, u32[]{:S(2)}, u32[]{:S(2)}) collective-permute-start(f32[2,5,16,512]{3,2,1,0:T(8,128)} %state_ref.1), channel_id=1, source_target_pairs={{0,1},{1,0},{2,3},{3,2},{4,5},{5,4},{6,7},{7,6},{8,9},{9,8},{10,11... | collective-permute-start | bytes 983048 | tf_op jit(solution)/shard_map/ppermute | solution.py:326
  19.4 0.0 copy-start
  19.4 1.0 copy-done
  20.3 0.0 copy-start.2
  20.3 0.7 copy-done.2
  21.0 1.2 %peak.1 = (f32[32,1,128]{2,1,0:T(1,128)S(1)}, f32[2]{0:T(128)S(1)}, f32[2,5,16,512]{3,2,1,0:T(8,128)S(1)}) custom-call(s32[2]{0:T(128)S(1)} %copy-done.2, f32[2,5,16,512]{3,2,1,0:T(8,128)S(1)} %copy-done), custom_call_target="tpu_custom_call" | custom-call | tf_op jit(solution)/shard_map/peak/pallas_call | solution.py:327
  22.2 18.6 %all_to_all.20.peaks_ref = f32[32,1,128]{2,1,0:T(1,128)S(1)} all-to-all(f32[32,1,128]{2,1,0:T(1,128)S(1)} %get-tuple-element.13), channel_id=1, replica_groups=mesh['y'=8,'zl'=8,'core'=2,'x'=4,'zh'=2] {'y','x'}, dimensions={0} | all-to-all | bytes 32768 | tf_op jit(solution)/shard_map/all_to_all | solution.py:332
  40.8 20.5 %all_to_all.21._.peaks_ref = f32[32,1,128]{2,1,0:T(1,128)S(1)} all-to-all(f32[32,1,128]{2,1,0:T(1,128)S(1)} %fold.1), channel_id=1, replica_groups=mesh['y'=8,'zl'=8,'core'=2,'x'=4,'zh'=2] {'zl','zh','core'}, dimensions={0} | all-to-all | bytes 32768 | tf_op jit(solution)/shard_map/all_to_all | solution.py:337
  61.3 0.0 collective-permute-done.other_ref
  61.3 1.2 %partial_sources.1 = f32[4,120,512]{2,1,0:T(8,128)S(1)} custom-call(f32[2]{0:T(128)S(1)} %get-tuple-element.11.counts_ref, f32[2,5,16,512]{3,2,1,0:T(8,128)S(1)} %get-tuple-element.12.state_ref, f32[2,5,16,512]{3,2,1,0:T(8,128)S(1)} %collective-permute-done.other_ref, f32[32,1,128]{2,1,0:T(1,128)S(1)} %all_to_all.21._.peaks_ref), custom_call_target="tpu_custom_call" | custom-call | tf_op jit(solution)/shard_map/partial_sources/pallas_call | solution.py:338
  62.5 0.0 copy-start.1
  62.6 16.9 %all_to_all.22.outer_ref = f32[4,120,512]{2,1,0:T(8,128)S(1)} all-to-all(f32[4,120,512]{2,1,0:T(8,128)S(1)} %partial_sources.1), channel_id=1, replica_groups=mesh['y'=8,'zl'=8,'core'=2,'x'=4,'zh'=2] {'x'}, dimensions={0} | all-to-all | bytes 1966080 | tf_op jit(solution)/shard_map/all_to_all | solution.py:344
  79.4 0.0 copy-done.1
  79.4 1.6 %edges.1 = (f32[96,512]{1,0:T(8,128)S(1)}, f32[96,512]{1,0:T(8,128)S(1)}, f32[4,80,512]{2,1,0:T(8,128)}) custom-call(f32[2]{0:T(128)S(1)} %get-tuple-element.11.counts_ref, f32[2,5,16,512]{3,2,1,0:T(8,128)S(1)} %get-tuple-element.12.state_ref, f32[2,5,16,512]{3,2,1,0:T(8,128)S(1)} %collective-permute-done.other_ref, f32[16,512]{1,0:T(8,128)S(1)} %copy-done.1, ...), custom_call_target="tpu_custom_call" | custom-call | tf_op jit(solution)/shard_map/edges/pallas_call | solution.py:345
  81.1 4.9 %all-to-all-start.3 = ((f32[4,80,512]{2,1,0:T(8,128)}), f32[4,80,512]{2,1,0:T(8,128)S(1)}, u32[]{:S(2)}, u32[]{:S(2)}) async-start(f32[4,80,512]{2,1,0:T(8,128)} %get-tuple-element.14), calls=%async_computation.3 | async-start | bytes 1310720 | tf_op jit(solution)/shard_map/all_to_all | solution.py:359
  86.0 1.9 %collective-permute-start.1 = (f32[96,512]{1,0:T(8,128)S(1)}, f32[96,512]{1,0:T(8,128)S(1)}, u32[]{:S(2)}, u32[]{:S(2)}) collective-permute-start(f32[96,512]{1,0:T(8,128)S(1)} %get-tuple-element.15), channel_id=1, source_target_pairs={{8,16},{9,17},{24,32},{25,33},{40,48},{41,49},{56,64},{57,65},{72,... | collective-permute-start | bytes 589832 | tf_op jit(solution)/shard_map/ppermute | solution.py:357
  87.9 2.8 %collective-permute-start.2 = (f32[96,512]{1,0:T(8,128)S(1)}, f32[96,512]{1,0:T(8,128)S(1)}, u32[]{:S(2)}, u32[]{:S(2)}) collective-permute-start(f32[96,512]{1,0:T(8,128)S(1)} %get-tuple-element.16), channel_id=1, source_target_pairs={{0,8},{8,0},{1,9},{9,1},{2,10},{10,2},{3,11},{11,3},{4,12},{12,4},... | collective-permute-start | bytes 589832 | tf_op jit(solution)/shard_map/ppermute | solution.py:358
  90.7 5.6 %collective-permute-done.1.far_ref = f32[96,512]{1,0:T(8,128)S(1)} collective-permute-done((f32[96,512]{1,0:T(8,128)S(1)}, f32[96,512]{1,0:T(8,128)S(1)}, u32[]{:S(2)}, u32[]{:S(2)}) %collective-permute-start.1) | collective-permute-done | bytes 196640 | tf_op jit(solution)/shard_map/ppermute | solution.py:357
  96.3 0.0 collective-permute-done.2.near_ref
  96.3 0.0 all-to-all-done.3.inner_ref
  96.3 4.3 %march.1 = f32[2,5,16,512]{3,2,1,0:T(8,128)} custom-call(f32[2]{0:T(128)S(1)} %get-tuple-element.11.counts_ref, f32[2,5,16,512]{3,2,1,0:T(8,128)S(1)} %get-tuple-element.12.state_ref, f32[16,512]{1,0:T(8,128)S(1)} %copy-done.1, f32[4,120,512]{2,1,0:T(8,128)S(1)} %all_to_all.22.outer_ref, f32[4,80,512]{2,1,0:T(8,128)S(1)} %all-to-all-done.3.inner_ref, ...), custom_call_target="tpu_custom_call" | custom-call | tf_op jit(solution)/shard_map/march/pallas_call | solution.py:360
  (1 shorter events, 0.0 us)
Async XLA Ops:
  0.0 61.3 %collective-permute-start = (f32[2,5,16,512]{3,2,1,0:T(8,128)}, f32[2,5,16,512]{3,2,1,0:T(8,128)S(1)}, u32[]{:S(2)}, u32[]{:S(2)}) collective-permute-start(f32[2,5,16,512]{3,2,1,0:T(8,128)} %state_ref.1), channel_id=1, source_target_pairs={{0,1},{1,0},{2,3},{3,2},{4,5},{5,4},{6,7},{7,6},{8,9},{9,8},{10,11... | collective-permute-start | bytes 983048 | tf_op jit(solution)/shard_map/ppermute | solution.py:326
  19.4 1.0 copy-start
  20.3 0.7 copy-start.2
  62.5 16.9 %copy-start.1 = (f32[16,512]{1,0:T(8,128)S(1)}, f32[16,512]{1,0:T(8,128)}, u32[]{:S(2)}) copy-start(f32[16,512]{1,0:T(8,128)} %wall_ref.3) | copy-start | bytes 98308
  81.1 15.2 %all-to-all-start.3 = ((f32[4,80,512]{2,1,0:T(8,128)}), f32[4,80,512]{2,1,0:T(8,128)S(1)}, u32[]{:S(2)}, u32[]{:S(2)}) async-start(f32[4,80,512]{2,1,0:T(8,128)} %get-tuple-element.14), calls=%async_computation.3 | async-start | bytes 1310720 | tf_op jit(solution)/shard_map/all_to_all | solution.py:359
  86.0 10.3 %collective-permute-start.1 = (f32[96,512]{1,0:T(8,128)S(1)}, f32[96,512]{1,0:T(8,128)S(1)}, u32[]{:S(2)}, u32[]{:S(2)}) collective-permute-start(f32[96,512]{1,0:T(8,128)S(1)} %get-tuple-element.15), channel_id=1, source_target_pairs={{8,16},{9,17},{24,32},{25,33},{40,48},{41,49},{56,64},{57,65},{72,... | collective-permute-start | bytes 589832 | tf_op jit(solution)/shard_map/ppermute | solution.py:357
  87.9 8.4 %collective-permute-start.2 = (f32[96,512]{1,0:T(8,128)S(1)}, f32[96,512]{1,0:T(8,128)S(1)}, u32[]{:S(2)}, u32[]{:S(2)}) collective-permute-start(f32[96,512]{1,0:T(8,128)S(1)} %get-tuple-element.16), channel_id=1, source_target_pairs={{0,8},{8,0},{1,9},{9,1},{2,10},{10,2},{3,11},{11,3},{4,12},{12,4},... | collective-permute-start | bytes 589832 | tf_op jit(solution)/shard_map/ppermute | solution.py:358
